TPU v7x, 32 devices: a whole 2x2x4 slice. The times are simulated.
32 devices in a mesh: dp: 8 (over z, x), seq: 4 (over y, core).
Axes of the slice: x: 2, y: 2, z: 4, core: 2. Of those that a mesh axis runs over, the one named last changes fastest.
Arguments:
- block_in: bfloat16 [16, 768, 768], P('dp', 'seq'), may hold values from -6 to 6
- cotangent: bfloat16 [16, 768, 768], P('dp', 'seq'), may hold values from -6 to 6
- labels: int32 [16], P('dp'), may hold values 0 or 1
- master: float32 [2, 768, 9216], P(None, 'dp', 'seq'), may hold values from -8 to 8
- small_params: float32 [2, 9984], replicated, may hold values from -2 to 3
- row_state: float32 [2, 4, 768], P(None, None, 'dp')
- col_state: float32 [2, 9216], P(None, 'seq')
- small_state: float32 [2, 9984], replicated
Outputs:
- block_out: bfloat16 [16, 768, 768], P('dp', 'seq')
- input_grad: float32 [16, 768, 768], P('dp', 'seq')
- example_norms: float32 [16], P('dp')
- influence: float32 [16], P('dp')
- weight_grads: float32 [2, 768, 9216], P(None, 'dp', 'seq')
- fresh_row_moments: float32 [2, 4, 768], P(None, None, 'dp')
- col_stats: float32 [2, 9216], P(None, 'seq')
- new_master: float32 [2, 768, 9216], P(None, 'dp', 'seq')
- new_low: bfloat16 [2, 768, 9216], P(None, 'dp', 'seq')
- small_grads: float32 [2, 9984], replicated
- small_moments: float32 [2, 9984], replicated
- small_new: float32 [2, 9984], replicated
All inputs are finite; a program needn't handle non-finite values. No bound on the sum of `labels` on one device may be relied on, other than what follows from the above.
Results may differ from a plain program's by a relative error of at most 0.022.
Values may be sent and summed in bfloat16 or wider, within the bound.
No kernel may reach another device: no remote copies, remote signals or barrier semaphores. Data moves between devices by JAX's collectives and lax.ppermute only.
A program may use at most 256 MiB of HBM per device.

v0:
```python
import functools

import jax
import numpy as np
import jax.numpy as jnp
from jax import lax
from jax.experimental import pallas as pl
from jax.experimental.pallas import tpu as pltpu
from jax.sharding import PartitionSpec as P

D = 768
HEADS = 12
FF = 3072
LAYERS = 2
HEAD_DIM = 64
ROT = 16
SMALL = 9984

EPS_NORM = 1e-05
EPS_SQUARE = 1e-30
RATE = 0.5
DECAY = 0.5
NEG_LARGE = -1e30
SCORE_SCALE = HEAD_DIM ** (-0.5)
CONTRACT_LAST = (((1,), (1,)), ((), ()))
CONTRACT_FIRST = (((0,), (0,)), ((), ()))
VMEM_BYTES = 24 * 1024 * 1024
BF16 = jnp.bfloat16
F32 = jnp.float32


def unpack(vector):
    return jnp.split(vector, [D, 2 * D, 3 * D, 4 * D, 7 * D, 8 * D, 8 * D + FF], axis=-1)


def apply_layer_norm(inputs):
    centred = inputs - jnp.mean(inputs, axis=-1, keepdims=True)
    variance = jnp.mean(centred * centred, axis=-1, keepdims=True)
    inverse = lax.rsqrt(variance + EPS_NORM)
    return (centred * inverse, inverse)


def norm_back(grad_scaled, scaled, inverse):
    mean_grad = jnp.mean(grad_scaled, axis=-1, keepdims=True)
    mean_cross = jnp.mean(grad_scaled * scaled, axis=-1, keepdims=True)
    return (grad_scaled - mean_grad - scaled * mean_cross) * inverse


def rotary_tables(length):
    halfway = ROT // 2
    frequency = 10000.0 ** (-2.0 * np.arange(halfway) / ROT)
    angles = np.arange(length)[:, None] * frequency[None, :]
    cosine, sine = np.cos(angles), np.sin(angles)
    rest = np.ones((length, HEAD_DIM - ROT))
    none = np.zeros((length, halfway))
    keep = np.concatenate([cosine, cosine, rest], axis=1)
    ahead = np.concatenate([-sine, none, 0.0 * rest], axis=1)
    behind = np.concatenate([none, sine, 0.0 * rest], axis=1)
    return tuple(
        jnp.asarray(np.concatenate([table, table], axis=1), F32) for table in (keep, ahead, behind)
    )


def swap(values, axis, bits):
    size = lax.axis_size(axis)
    return lax.ppermute(values, axis, [(i, i ^ bits) for i in range(size)])


def sum_pairwise(values, axis, wire=F32):
    bits = 1
    while bits < lax.axis_size(axis):
        sent = values.astype(wire)
        values = sent.astype(F32) + swap(sent, axis, bits).astype(F32)
        bits *= 2
    return values


def both_halves(own):
    return jnp.stack([own, swap(own, "seq", 2)], axis=-3)


def core_sum(keep, send):
    received = swap(send, "seq", 1)
    return keep, received, (keep + received.astype(F32)).astype(BF16)


def gather_rows(rows):
    if lax.axis_size("dp") != 8:
        return [lax.all_gather(rows, "dp", axis=0, tiled=True)]
    pieces = []
    for k in range(4):
        pieces += [rows, swap(rows, "dp", 1)]
        if k < 3:
            rows = lax.ppermute(rows, "dp", [(i, (i + 2) % 8) for i in range(8)])
    return pieces


def piece_places(count, dp_place):
    if count == 1:
        return [0]
    return [(dp_place + 8 - 2 * (k // 2)) % 8 ^ (k % 2) for k in range(count)]


def pair_sum(keep, send, z_place):
    summed = keep + swap(send, "dp", 1).astype(F32)
    own = lax.dynamic_index_in_dim(summed, z_place, 0, keepdims=False)
    return own, [
        lax.dynamic_index_in_dim(summed, z_place ^ k, 0, keepdims=False).astype(BF16)
        for k in range(1, summed.shape[0])
    ]


def pair_total(keep, send):
    return (keep + swap(send, "dp", 1).astype(F32)).astype(BF16).reshape(-1, keep.shape[-1])


def scatter_along_z(total):
    groups = [[2 * z + x for z in range(4)] for x in range(2)]
    return lax.psum_scatter(
        total, "dp", scatter_dimension=0, tiled=True, axis_index_groups=groups
    )


def exchange_parts(parts):
    return [swap(part, "dp", 2 * (k + 1)) for k, part in enumerate(parts)]


def exchange_blocks(blocks, index):
    size = lax.axis_size("seq")
    received = []
    for k in range(size):
        block = lax.dynamic_index_in_dim(blocks, index ^ k, 0, keepdims=False)
        received.append(block if k == 0 else swap(block, "seq", k))
    return received


def heads_together(values):
    heads = values.shape[-1] // (3 * HEAD_DIM)
    lead = values.shape[:-1]
    by_head = values.reshape(*lead, heads, 3 * HEAD_DIM)
    return jnp.concatenate(
        [
            by_head[..., : 2 * HEAD_DIM].reshape(*lead, heads * 2 * HEAD_DIM),
            by_head[..., 2 * HEAD_DIM :].reshape(*lead, heads * HEAD_DIM),
        ],
        axis=-1,
    )


def heads_apart(values):
    heads = values.shape[-1] // (3 * HEAD_DIM)
    lead = values.shape[:-1]
    pairs, last = jnp.split(values, [heads * 2 * HEAD_DIM], axis=-1)
    return jnp.concatenate(
        [
            pairs.reshape(*lead, heads, 2 * HEAD_DIM),
            last.reshape(*lead, heads, HEAD_DIM),
        ],
        axis=-1,
    ).reshape(values.shape)


def halves(core_bit, chunk):
    own = pl.multiple_of(core_bit * chunk, chunk)
    return pl.ds(own, chunk), pl.ds(pl.multiple_of(chunk - own, chunk), chunk)


def place_tokens(dst, own, near, core_bit, y_here, chunk):
    at_own, at_near = halves(core_bit, chunk)
    dst[at_own] = own[y_here]
    dst[at_near] = near[y_here]


def spread_tokens(value, held, keep, send, core_bit, y_here, chunk):
    at_own, at_near = halves(core_bit, chunk)
    held[...] = value
    keep[pl.ds(y_here, 1)] = held[at_own][None]
    send[pl.ds(y_here, 1)] = held[at_near].astype(send.dtype)[None]


def gelu_and_slope(v):
    magnitude = jnp.abs(v) * 0.7071067811865476
    t = 1.0 / (1.0 + 0.3275911 * magnitude)
    falling = jnp.exp(-0.5 * v * v)
    poly = t * (
        0.254829592
        + t * (-0.284496736 + t * (1.421413741 + t * (-1.453152027 + t * 1.061405429)))
    )
    tail = 0.5 * poly * falling
    cdf = jnp.where(v >= 0.0, 1.0 - tail, tail)
    return v * cdf, cdf + v * falling * 0.3989422804014327


def weight_copies(dp_place, sources, targets, sems):
    copies = []
    for (pieces, first), target in zip(sources, targets):
        rows, width = pieces[0].shape[0], target.shape[1]
        for piece, place in zip(pieces, piece_places(len(pieces), dp_place)):
            offset = 0 if len(pieces) == 1 else pl.multiple_of(place * rows, 16)
            copies.append(
                pltpu.make_async_copy(
                    piece.at[:, pl.ds(first, width)],
                    target.at[pl.ds(offset, rows), :],
                    sems.at[len(copies)],
                )
            )
    return copies


def place_columns(whole, blocks, place):
    width = blocks[0].shape[1]
    seq_place = 2 * place[1] + place[0]
    for index in range(len(blocks)):

        @pl.when(seq_place == index)
        def _():
            for k, block in enumerate(blocks):
                at = width * (index ^ k)
                whole[:, at : at + width] = block[...]


def start_all(copies):
    for copy in copies:
        copy.start()


def wait_all(copies):
    for copy in copies:
        copy.wait()


def turn(pair, tables, sign):
    keep_tab, ahead_tab, behind_tab = tables
    ahead = pltpu.roll(pair, 2 * HEAD_DIM - ROT // 2, 1) * ahead_tab[...]
    behind = pltpu.roll(pair, ROT // 2, 1) * behind_tab[...]
    return pair * keep_tab[...] + sign * (ahead + behind)


def forward_kernel(counts, firsts, place, *refs):
    refs = list(refs)

    def take(count):
        taken, refs[:] = refs[:count], refs[count:]
        return taken

    own, near, vec = take(3)
    tables = take(3)
    blocks_out = take(4)
    pieces = [take(count) for count in counts]
    keep, send, xhat, qk, val, att, lse, hid, slope = refs[-16:-7]
    whole_a, whole_b, w_out, k_all, v_all, held, sems = refs[-7:]
    core_bit, y_bit, dp_place = place[0], place[1], place[2]
    step = pl.program_id(0)
    wide = 3 * val.shape[1]
    sources = list(zip(pieces, firsts))
    copies = weight_copies(dp_place, sources, [whole_a, whole_b], sems)

    @pl.when(step == 0)
    def _():
        start_all(copies)
        place_columns(w_out, blocks_out, place)

    chunk = own.shape[1]
    block = 2 * chunk
    y_here = step ^ y_bit
    place_tokens(xhat, own, near, core_bit, y_here, chunk)
    heads = val.shape[-1] // HEAD_DIM
    quarter = hid.shape[-1]
    row = lax.broadcasted_iota(jnp.int32, (block, block), 0)
    column = lax.broadcasted_iota(jnp.int32, (block, block), 1)
    lane = lax.broadcasted_iota(jnp.int32, (block, 128), 1)

    def attend(here, h, joined, log_sums):
        at_q, at_k = 2 * HEAD_DIM * h, 2 * HEAD_DIM * h + HEAD_DIM
        turned = turn(joined[:, at_q : at_k + HEAD_DIM], tables, 1.0)
        qk[:, at_q : at_k + HEAD_DIM] = turned.astype(BF16)
        k_all[h, block * here : block * (here + 1)] = turned[:, HEAD_DIM:].astype(BF16)
        first = 2 * HEAD_DIM * heads + HEAD_DIM * h
        v_all[h, block * here : block * (here + 1)] = joined[:, first : first + HEAD_DIM].astype(
            BF16
        )
        query = qk[:, at_q : at_q + HEAD_DIM] * jnp.asarray(SCORE_SCALE, BF16)
        scores = []
        for j in range(here + 1):
            part = lax.dot_general(
                query,
                k_all[h, block * j : block * (j + 1)],
                CONTRACT_LAST,
                preferred_element_type=F32,
            )
            if j == here:
                part = jnp.where(column <= row, part, NEG_LARGE)
            scores.append(part)
        largest = functools.reduce(
            jnp.maximum, [jnp.max(part, axis=-1, keepdims=True) for part in scores]
        )
        total = 0.0
        mixed = 0.0
        for j, part in enumerate(scores):
            exponent = jnp.exp(part - largest)
            total = total + jnp.sum(exponent, axis=-1, keepdims=True)
            mixed = mixed + jnp.dot(
                exponent.astype(BF16),
                v_all[h, block * j : block * (j + 1)],
                preferred_element_type=F32,
            )
        att[:, HEAD_DIM * h : HEAD_DIM * (h + 1)] = (mixed / total).astype(BF16)
        return jnp.where(lane == h, largest + jnp.log(total), log_sums)

    for here in range(2):

        @pl.when(step == here)
        def _():
            scaled = xhat[...].astype(F32)
            normed_one = (scaled * vec[0:1] + vec[1:2]).astype(BF16)
            normed_two = (scaled * vec[2:3] + vec[3:4]).astype(BF16)
            if here == 0:
                wait_all(copies)
            joined = (
                jnp.dot(normed_one, whole_a[:, :wide], preferred_element_type=F32) + vec[5:6, :wide]
            )
            val[...] = joined[:, 2 * HEAD_DIM * heads :].astype(BF16)
            hidden_pre = (
                jnp.dot(normed_two, whole_b[:, :quarter], preferred_element_type=F32)
                + vec[4:5, :quarter]
            )
            log_sums = jnp.zeros((block, 128), F32)
            for h in range(heads):
                log_sums = attend(here, h, joined, log_sums)
            lse[...] = log_sums.T[:8]
            hidden, gradient = gelu_and_slope(hidden_pre)
            hid[...] = hidden.astype(BF16)
            slope[...] = gradient.astype(BF16)
            partial = jnp.dot(att[...], w_out[...], preferred_element_type=F32) + lax.dot_general(
                hid[...], whole_b[:, quarter:], CONTRACT_LAST, preferred_element_type=F32
            )
            spread_tokens(partial, held, keep, send, core_bit, y_here, chunk)


def normalised(stream):
    centred = stream - jnp.mean(stream, axis=-1, keepdims=True)
    variance = jnp.mean(centred * centred, axis=-1, keepdims=True)
    inverse = lax.rsqrt(variance + EPS_NORM)
    return centred * inverse, inverse


def seq_sum(keep, near, across):
    return keep[...] + near[...].astype(F32) + across[...].astype(F32)


def finish_stream_kernel(keep, near, across, stream, bias, out, *low):
    value = stream[...].astype(F32) + seq_sum(keep, near, across) + bias[...]
    out[...] = value.astype(out.dtype)
    if low:
        low[0][...] = normalised(value)[0].astype(BF16)


def finish_grad_kernel(keep, near, across, grad, stream, out, *low):
    scaled, inverse = normalised(stream[...].astype(F32))
    back = norm_back(seq_sum(keep, near, across), scaled, inverse)
    value = grad[...].astype(F32) + back
    out[...] = value
    if low:
        low[0][...] = value.astype(BF16)


def add_up(sums, place_row, values):
    sums[place_row : place_row + 1, : values.shape[-1]] += jnp.sum(
        values.astype(F32), axis=0, keepdims=True
    )


def mlp_backward_kernel(count, first, sequence, n_before, n_outward, place, *refs):
    own, near, vec, xhat, slope, att = refs[:6]
    pieces = refs[6 : 6 + count]
    before = refs[6 + count : 6 + count + n_before]
    grad, grad_pre, grad_two, sums = refs[-7 - n_outward : -3 - n_outward]
    outward, (whole_b, product, sems) = refs[-3 - n_outward : -3], refs[-3:]
    core_bit, y_bit, dp_place = place[0], place[1], place[2]
    step = pl.program_id(0)
    copies = weight_copies(dp_place, [(pieces, first)], [whole_b], sems)

    @pl.when(step == 0)
    def _():
        start_all(copies)
        sums[...] = jnp.zeros_like(sums)

    chunk = own.shape[1]
    place_tokens(grad, own, near, core_bit, step ^ y_bit, chunk)

    @pl.when(step == 0)
    def _():
        wait_all(copies)

    quarter = slope.shape[-1]
    grad_hidden = jnp.dot(grad[...], whole_b[:, quarter:], preferred_element_type=F32)
    low_pre = (grad_hidden * slope[...].astype(F32)).astype(BF16)
    grad_pre[...] = low_pre
    normed = lax.dot_general(
        low_pre, whole_b[:, :quarter], CONTRACT_LAST, preferred_element_type=F32
    )
    grad_two[...] = (normed * vec[2:3]).astype(BF16)
    add_up(sums, 0, normed * xhat[...].astype(F32))
    add_up(sums, 1, normed)
    add_up(sums, 2, low_pre)
    add_up(sums, 3, grad[...])
    kept = jnp.where(place[3 + sequence] > 0, grad[...], jnp.zeros_like(grad))
    part = lax.dot_general(att[...], kept, CONTRACT_FIRST, preferred_element_type=F32)

    @pl.when(step == 0)
    def _():
        product[...] = part + before[0][...] if before else part

    @pl.when(step != 0)
    def _():
        product[...] += part
        if len(outward) == 1:
            outward[0][...] = product[...]
            return
        width = outward[0].shape[1]
        for index in range(len(outward)):

            @pl.when(2 * y_bit + core_bit == index)
            def _():
                for k, block in enumerate(outward):
                    at = width * (index ^ k)
                    block[...] = product[:, at : at + width].astype(BF16)


def attention_backward_kernel(count, first, place, *refs):
    refs = list(refs)

    def take(number):
        taken, refs[:] = refs[:number], refs[number:]
        return taken

    grad, vec = take(2)
    tables = take(3)
    blocks_out = take(4)
    xhat, qk, val, lse, grad_two = take(5)
    pieces = take(count)
    keep, send, grad_joined, sums = refs[-10:-6]
    whole_a, w_out, dk_all, dv_all, held, sems = refs[-6:]
    core_bit, y_bit, dp_place = place[0], place[1], place[2]
    step = 1 - pl.program_id(0)
    copies = weight_copies(dp_place, [(pieces, first)], [whole_a], sems)

    @pl.when(step == 1)
    def _():
        start_all(copies)
        sums[...] = jnp.zeros_like(sums)
        place_columns(w_out, blocks_out, place)

    block = grad.shape[0]
    chunk = block // 2
    heads = val.shape[-1] // HEAD_DIM
    row = lax.broadcasted_iota(jnp.int32, (block, block), 0)
    column = lax.broadcasted_iota(jnp.int32, (block, block), 1)

    def attend_back(here, h, near_grad):
        at_q, at_k = 2 * HEAD_DIM * h, 2 * HEAD_DIM * h + HEAD_DIM
        at_v = 2 * HEAD_DIM * heads + HEAD_DIM * h
        query = qk[block * here : block * (here + 1), at_q:at_k]
        query = query * jnp.asarray(SCORE_SCALE, BF16)
        log_row = lse[h : h + 1]
        probs, grad_probs, keys = [], [], []
        delta = 0.0
        for j in range(here + 1):
            key = qk[block * j : block * (j + 1), at_k : at_k + HEAD_DIM]
            value = val[block * j : block * (j + 1), HEAD_DIM * h : HEAD_DIM * (h + 1)]
            scores = lax.dot_general(key, query, CONTRACT_LAST, preferred_element_type=F32)
            prob = jnp.exp(scores - log_row)
            if j == here:
                prob = jnp.where(row <= column, prob, 0.0)
            grad_prob = lax.dot_general(
                value, near_grad, CONTRACT_LAST, preferred_element_type=F32
            )
            delta = delta + jnp.sum(prob * grad_prob, axis=0, keepdims=True)
            probs.append(prob)
            grad_probs.append(grad_prob)
            keys.append(key)
        dq = 0.0
        for j in range(here + 1):
            grad_score = (probs[j] * (grad_probs[j] - delta)).astype(BF16)
            dk = jnp.dot(grad_score, query, preferred_element_type=F32)
            dv = jnp.dot(probs[j].astype(BF16), near_grad, preferred_element_type=F32)
            dq = dq + lax.dot_general(
                grad_score, keys[j], CONTRACT_FIRST, preferred_element_type=F32
            )
            if j < here:
                dk_all[h], dv_all[h] = dk, dv
            elif here == 0:
                dk, dv = dk + dk_all[h], dv + dv_all[h]
        pair = jnp.concatenate([dq * SCORE_SCALE, dk], axis=1)
        grad_joined[:, at_q : at_q + 2 * HEAD_DIM] = turn(pair, tables, -1.0).astype(BF16)
        grad_joined[:, at_v : at_v + HEAD_DIM] = dv.astype(BF16)

    for here in (1, 0):

        @pl.when(step == here)
        def _():
            grad_att = lax.dot_general(
                grad[...], w_out[...], CONTRACT_LAST, preferred_element_type=F32
            ).astype(BF16)
            for h in range(heads):
                attend_back(here, h, grad_att[:, HEAD_DIM * h : HEAD_DIM * (h + 1)])
            if here == 1:
                wait_all(copies)
            normed = lax.dot_general(
                grad_joined[...],
                whole_a[:, : grad_joined.shape[1]],
                CONTRACT_LAST,
                preferred_element_type=F32,
            )
            spread_tokens(
                normed * vec[0:1] + grad_two[...].astype(F32),
                held,
                keep,
                send,
                core_bit,
                step ^ y_bit,
                chunk,
            )
            add_up(sums, 0, normed * xhat[...].astype(F32))
            add_up(sums, 1, normed)
            add_up(sums, 2, grad_joined[...])


def fetch(sources, targets, sems):
    copies = [
        pltpu.make_async_copy(source, target, sems.at[k])
        for k, (source, target) in enumerate(zip(sources, targets))
    ]
    start_all(copies)
    return copies


def outer_sum(flags, pairs):
    total = 0.0
    for flag, pair in zip(flags, pairs):
        left, right = pair()
        kept = jnp.where(flag > 0, right, jnp.zeros_like(right))
        total = total + lax.dot_general(left, kept, CONTRACT_FIRST, preferred_element_type=F32)
    return total


def store_rows(value, outs, first, x_bit):
    columns = pl.ds(first, value.shape[1])
    if len(outs) == 1:
        outs[0][:, columns] = value.astype(BF16)
        return
    keep, send = outs
    rows = keep.shape[1]
    for bit in (0, 1):

        @pl.when(x_bit == bit)
        def _():
            for z in range(keep.shape[0]):
                at = rows * (2 * z + bit)
                to = rows * (2 * z + 1 - bit)
                keep[z, :, columns] = value[at : at + rows]
                send[z, :, columns] = value[to : to + rows].astype(BF16)


def mlp_outer_kernel(count, n_outs, scalars, vec, *refs):
    sources, outs = refs[: 4 * count], refs[-n_outs - 4 * count - 1 : -4 * count - 1]
    held, sems = refs[-4 * count - 1 : -1], refs[-1]
    copies = fetch(sources, held, sems)
    x_bit, flags = scalars[0], [scalars[2 + s] for s in range(count)]

    def ready(k):
        copies[k].wait()
        return held[k][...]

    def up(s):
        def pair():
            xhat, grad_pre = ready(4 * s), ready(4 * s + 1)
            return (xhat.astype(F32) * vec[2:3] + vec[3:4]).astype(BF16), grad_pre

        return pair

    def down(s):
        return lambda: (ready(4 * s + 2), ready(4 * s + 3))

    store_rows(outer_sum(flags, [up(s) for s in range(count)]), outs, 0, x_bit)
    store_rows(
        outer_sum(flags, [down(s) for s in range(count)]), outs, held[3].shape[1], x_bit
    )


def qkv_outer_kernel(count, n_blocks, n_outs, scalars, vec, *refs):
    sources, blocks = refs[: 2 * count], refs[2 * count : 2 * count + n_blocks]
    held, outward, sems = refs[-2 * count - 2 : -2], refs[-2], refs[-1]
    outs = refs[-2 * count - 2 - n_outs : -2 * count - 2]
    copies = fetch(sources, held, sems)
    x_bit, flags = scalars[0], [scalars[2 + s] for s in range(count)]

    def pair_of(s):
        def pair():
            copies[2 * s].wait()
            copies[2 * s + 1].wait()
            normed = held[2 * s][...].astype(F32) * vec[0:1] + vec[1:2]
            return normed.astype(BF16), held[2 * s + 1][...]

        return pair

    rows = blocks[0].shape[0]
    for k, block in enumerate(blocks):
        outward[pl.ds(pl.multiple_of((scalars[1] ^ k) * rows, 16), rows)] = block[...]
    wide = held[1].shape[1]
    store_rows(outward[...].astype(F32), outs, wide, x_bit)
    store_rows(outer_sum(flags, [pair_of(s) for s in range(count)]), outs, 0, x_bit)


def natural_heads(values):
    heads = values.shape[1] // (3 * HEAD_DIM)
    parts = []
    for h in range(heads):
        parts.append(values[:, 2 * HEAD_DIM * h : 2 * HEAD_DIM * (h + 1)])
        at = 2 * HEAD_DIM * heads + HEAD_DIM * h
        parts.append(values[:, at : at + HEAD_DIM])
    return parts


def matrix_cuts(width):
    unit = width // 12
    return [0, 3 * unit, 4 * unit, 8 * unit, width]


def gradient_kernel(counts, cuts, *refs):
    refs = list(refs)
    row_state, (grads, row_sums, col_sums) = refs[sum(counts)], refs[-3:]
    parts = []
    for count in counts:
        taken, refs[:] = refs[:count], refs[count:]
        parts.append(sum(ref[...].astype(F32) for ref in taken))
    both, rest = parts
    at = 0
    for part in natural_heads(rest[:, : cuts[1]]):
        grads[0, :, at : at + part.shape[1]] = part
        at += part.shape[1]
    grads[0, :, cuts[1] : cuts[2]] = rest[:, cuts[1] :]
    grads[0, :, cuts[2] :] = both
    whole = grads[0]
    squares = whole * whole + EPS_SQUARE
    by_column = jnp.sum(squares, axis=0, keepdims=True)
    lanes = whole.shape[1] // 128
    row = lax.broadcasted_iota(jnp.int32, (whole.shape[0], 128), 1)
    lane = lax.broadcasted_iota(jnp.int32, (1, 128), 1)
    by_row = jnp.zeros((whole.shape[0], 128), F32)
    for m in range(4):
        total = jnp.sum(squares[:, cuts[m] : cuts[m + 1]], axis=1, keepdims=True)
        by_row = jnp.where(row == m, total, by_row)
    row_sums[0] = by_row.T[:8]
    totals = jnp.sum(by_row, axis=0, keepdims=True)
    states = jnp.sum(row_state[0], axis=1, keepdims=True)
    for m in range(4):
        totals = jnp.where(lane == 4 + m, states[m : m + 1], totals)
    col_sums[0] = jnp.zeros_like(col_sums[0])
    for k in range(lanes):
        col_sums[0, k : k + 1] = by_column[:, 128 * k : 128 * (k + 1)]
    col_sums[0, lanes : lanes + 1] = totals


def in_a_row(rows):
    return jnp.concatenate([rows[k : k + 1] for k in range(rows.shape[0])], axis=1)


def upright(rows):
    padded = jnp.concatenate([rows, jnp.zeros((4, rows.shape[1]), F32)], axis=0)
    spare = -rows.shape[1] % 128
    if spare:
        padded = jnp.concatenate([padded, jnp.zeros((8, spare), F32)], axis=1)
    return padded.T[: rows.shape[1]]


def scaled_update(grads, row_inverse, col_inverse, cuts, i, m):
    columns = slice(cuts[m], cuts[m + 1])
    return grads[i, :, columns] * row_inverse[:, m : m + 1] * col_inverse[:, columns]


def square_kernel(cuts, grads, master, rows, cols, row_state, col_state, fresh, stats, sums):
    layers = grads.shape[0]
    lanes = cuts[4] // 128
    lane = lax.broadcasted_iota(jnp.int32, (1, 128), 1)
    matrix = lax.broadcasted_iota(jnp.int32, (4, 1), 0)
    widths = jnp.where(matrix == 0, 3.0 * D, jnp.where(matrix == 1, 1.0 * D, 1.0 * FF))
    sums[...] = jnp.zeros_like(sums)
    for i in range(layers):
        fresh[i] = DECAY * row_state[i] + (1.0 - DECAY) * (rows[i, :4] / widths)
        stats[i : i + 1] = DECAY * col_state[i : i + 1] + (1.0 - DECAY) * (
            in_a_row(cols[i, :lanes]) / D
        )
        row_inverse = upright(lax.rsqrt(fresh[i]))
        col_inverse = lax.rsqrt(stats[i : i + 1])
        result = jnp.zeros((1, 128), F32)
        for m in range(4):
            update = scaled_update(grads, row_inverse, col_inverse, cuts, i, m)
            old = master[i, :, cuts[m] : cuts[m + 1]]
            for at, values in ((0, update), (4, old)):
                total = jnp.sum(
                    jnp.sum(values * values, axis=0, keepdims=True), axis=1, keepdims=True
                )
                result = jnp.where(lane == at + m, total, result)
        sums[i : i + 1] = result
        sums[layers + i : layers + i + 1] = cols[i, lanes : lanes + 1]


def update_kernel(cuts, grads, master, fresh, stats, sums, row_sums, new, new_low):
    layers = grads.shape[0]
    for i in range(layers):
        row_inverse = upright(lax.rsqrt(fresh[i]))
        col_inverse = lax.rsqrt(stats[i : i + 1])
        for m, width in enumerate((3.0 * D, 1.0 * D, 1.0 * FF, 1.0 * FF)):
            square_total = row_sums[layers + i : layers + i + 1, m : m + 1]
            state_total = row_sums[2 * layers + i : 2 * layers + i + 1, 4 + m : 5 + m]
            row_mean = (DECAY * state_total + (1.0 - DECAY) * (square_total / width)) / D
            update_rms = jnp.sqrt(row_mean * sums[i : i + 1, m : m + 1] / (D * width))
            weight_rms = jnp.sqrt(sums[i : i + 1, 4 + m : 5 + m] / (D * width))
            factor = RATE * weight_rms * jnp.sqrt(row_mean) / jnp.maximum(1.0, update_rms)
            columns = slice(cuts[m], cuts[m + 1])
            update = scaled_update(grads, row_inverse, col_inverse, cuts, i, m)
            value = master[i, :, columns] - factor * update
            new[i, :, columns] = value
            new_low[i, :, columns] = value.astype(BF16)


def whole_spec(shape):
    return pl.BlockSpec(shape, lambda *_: (0,) * len(shape))


def in_any(count):
    return [pl.BlockSpec(memory_space=pl.ANY)] * count


def far(arrays):
    return [pltpu.with_memory_space_constraint(array, pltpu.HBM) for array in arrays]


def cost(micros):
    return pl.CostEstimate(
        flops=int(micros * 10**9), bytes_accessed=int(micros * 10**6), transcendentals=0
    )


def chunk_specs(chunks):
    specs = []
    for array, place in chunks:
        if place is None:
            specs.append(whole_spec(array.shape))
        else:
            specs.append(
                pl.BlockSpec((None, *array.shape[1:]), lambda *_, place=place: (place, 0, 0, 0))
            )
    return specs


def rows_spec(rows, width, block_of):
    return pl.BlockSpec((rows, width), lambda t, *_: (block_of(t), 0))


def run_forward(place, chunks, vec, tables, weight, riders=()):
    blocks_out, sources = weight
    chunk = chunks[0][0].shape[-2]
    block, length = 2 * chunk, 4 * chunk
    counts = [len(pieces) for pieces, _ in sources]
    firsts = [first for _, first in sources]
    pieces = [piece for pieces, _ in sources for piece in pieces]
    count = len(pieces)
    out_wide = blocks_out[0].shape[0]
    heads = out_wide // HEAD_DIM
    wide = 3 * out_wide
    quarter = FF * out_wide // D

    def same(t):
        return t

    widths = [
        (D, BF16),
        (2 * out_wide, BF16),
        (out_wide, BF16),
        (out_wide, BF16),
        (quarter, BF16),
        (quarter, BF16),
    ]
    shapes = [pltpu.HBM((length, width), kind) for width, kind in widths]
    specs = [rows_spec(block, width, same) for width, _ in widths]
    shapes.insert(4, pltpu.HBM((8, length), F32))
    specs.insert(4, pl.BlockSpec((8, block), lambda t, *_: (0, t)))
    return pl.pallas_call(
        functools.partial(forward_kernel, counts, firsts),
        grid_spec=pltpu.PrefetchScalarGridSpec(
            num_scalar_prefetch=1,
            grid=(2,),
            in_specs=[
                *chunk_specs(chunks),
                whole_spec((8, D)),
                *[rows_spec(block, 2 * HEAD_DIM, same)] * 3,
                *[whole_spec((out_wide, out_wide))] * 4,
                *in_any(count + len(riders)),
            ],
            out_specs=[whole_spec((2, chunk, D))] * 2 + specs,
            scratch_shapes=[
                pltpu.VMEM((D, wide + out_wide), BF16),
                pltpu.VMEM((D, 2 * quarter), BF16),
                pltpu.VMEM((out_wide, D), BF16),
                pltpu.VMEM((heads, length, HEAD_DIM), BF16),
                pltpu.VMEM((heads, length, HEAD_DIM), BF16),
                pltpu.VMEM((block, D), F32),
                pltpu.SemaphoreType.DMA((count,)),
            ],
        ),
        out_shape=[
            pltpu.HBM((2, chunk, D), F32),
            jax.ShapeDtypeStruct((2, chunk, D), BF16),
            *shapes,
        ],
        compiler_params=pltpu.CompilerParams(vmem_limit_bytes=VMEM_BYTES),
        cost_estimate=cost(13),
        name="layer_forward",
    )(place, *[array for array, _ in chunks], vec, *far(tables), *blocks_out, *far(pieces), *far(riders))


def run_mlp_backward(place, sequence, last, chunks, vec, weight, xhat, slope, att, before, riders=()):
    pieces, first = weight[1][1]
    chunk = chunks[0][0].shape[-2]
    block, length = 2 * chunk, 4 * chunk
    quarter, out_wide = slope.shape[1], att.shape[1]

    def same(t):
        return t

    if last:
        outward = [jax.ShapeDtypeStruct((out_wide, out_wide), BF16)] * (D // out_wide)
    else:
        outward = [pltpu.HBM((out_wide, D), F32)]
    return pl.pallas_call(
        functools.partial(
            mlp_backward_kernel, len(pieces), first, sequence, len(before), len(outward)
        ),
        grid_spec=pltpu.PrefetchScalarGridSpec(
            num_scalar_prefetch=1,
            grid=(2,),
            in_specs=[
                *chunk_specs(chunks),
                whole_spec((8, D)),
                rows_spec(block, D, same),
                rows_spec(block, quarter, same),
                rows_spec(block, out_wide, same),
                *in_any(len(pieces)),
                *[whole_spec((out_wide, D))] * len(before),
                *in_any(len(riders)),
            ],
            out_specs=[
                rows_spec(block, D, same),
                rows_spec(block, quarter, same),
                rows_spec(block, D, same),
                whole_spec((8, D)),
                *[whole_spec(array.shape) for array in outward],
            ],
            scratch_shapes=[
                pltpu.VMEM((D, 2 * quarter), BF16),
                pltpu.VMEM((out_wide, D), F32),
                pltpu.SemaphoreType.DMA((len(pieces),)),
            ],
        ),
        out_shape=[
            pltpu.HBM((length, D), BF16),
            pltpu.HBM((length, quarter), BF16),
            pltpu.HBM((length, D), BF16),
            pltpu.HBM((8, D), F32),
            *outward,
        ],
        compiler_params=pltpu.CompilerParams(vmem_limit_bytes=VMEM_BYTES),
        cost_estimate=cost(8),
        name="mlp_backward",
    )(
        place,
        *[array for array, _ in chunks],
        vec,
        *far([xhat, slope, att, *pieces]),
        *before,
        *far(riders),
    )


def run_attention_backward(
    place, grad, vec, tables, weight, xhat, qk, val, lse, grad_two, riders=()
):
    blocks_out, ((pieces, first), _) = weight
    length = grad.shape[0]
    block, chunk = length // 2, length // 4
    out_wide = blocks_out[0].shape[0]
    heads = out_wide // HEAD_DIM
    wide = 3 * out_wide

    def turned(t):
        return 1 - t

    return pl.pallas_call(
        functools.partial(attention_backward_kernel, len(pieces), first),
        grid_spec=pltpu.PrefetchScalarGridSpec(
            num_scalar_prefetch=1,
            grid=(2,),
            in_specs=[
                rows_spec(block, D, turned),
                whole_spec((8, D)),
                *[rows_spec(block, 2 * HEAD_DIM, turned)] * 3,
                *[whole_spec((out_wide, out_wide))] * 4,
                rows_spec(block, D, turned),
                whole_spec(qk.shape),
                whole_spec(val.shape),
                pl.BlockSpec((8, block), lambda t, *_: (0, 1 - t)),
                rows_spec(block, D, turned),
                *in_any(len(pieces) + len(riders)),
            ],
            out_specs=[
                *[whole_spec((2, chunk, D))] * 2,
                rows_spec(block, wide, turned),
                whole_spec((8, D)),
            ],
            scratch_shapes=[
                pltpu.VMEM((D, wide + out_wide), BF16),
                pltpu.VMEM((out_wide, D), BF16),
                pltpu.VMEM((heads, block, HEAD_DIM), F32),
                pltpu.VMEM((heads, block, HEAD_DIM), F32),
                pltpu.VMEM((block, D), F32),
                pltpu.SemaphoreType.DMA((len(pieces),)),
            ],
        ),
        out_shape=[
            pltpu.HBM((2, chunk, D), F32),
            jax.ShapeDtypeStruct((2, chunk, D), BF16),
            pltpu.HBM((length, wide), BF16),
            pltpu.HBM((8, D), F32),
        ],
        compiler_params=pltpu.CompilerParams(vmem_limit_bytes=VMEM_BYTES),
        cost_estimate=cost(11),
        name="attention_backward",
    )(
        place,
        *far([grad]),
        vec,
        *far(tables),
        *blocks_out,
        *far([xhat, qk, val, lse, grad_two, *pieces, *riders]),
    )


def outer_outputs(split, columns):
    if split:
        shape = (4, D // 8, columns)
        kinds = [F32, BF16]
    else:
        shape, kinds = (D, columns), [BF16]
    return [jax.ShapeDtypeStruct(shape, kind) for kind in kinds], [whole_spec(shape)] * len(kinds)


def run_mlp_outer(scalars, vec, groups, split, riders=()):
    xhats, grads, pres, hids = groups
    arrays = [array for both in zip(xhats, pres, grads, hids) for array in both]
    shapes, specs = outer_outputs(split, 2 * hids[0].shape[1])
    return pl.pallas_call(
        functools.partial(mlp_outer_kernel, len(xhats), len(shapes)),
        grid_spec=pltpu.PrefetchScalarGridSpec(
            num_scalar_prefetch=1,
            grid=(1,),
            in_specs=[whole_spec((8, D)), *in_any(len(arrays) + len(riders))],
            out_specs=specs,
            scratch_shapes=[
                *[pltpu.VMEM(array.shape, BF16) for array in arrays],
                pltpu.SemaphoreType.DMA((len(arrays),)),
            ],
        ),
        out_shape=shapes,
        compiler_params=pltpu.CompilerParams(vmem_limit_bytes=VMEM_BYTES),
        cost_estimate=cost(10),
        name="mlp_outer",
    )(scalars, vec, *far(arrays), *far(riders))


def run_qkv_outer(scalars, vec, groups, outward, split, riders=()):
    arrays = [array for both in zip(*groups) for array in both]
    out_wide = outward[0].shape[1]
    shapes, specs = outer_outputs(split, groups[1][0].shape[1] + out_wide)
    return pl.pallas_call(
        functools.partial(qkv_outer_kernel, len(groups[0]), len(outward), len(shapes)),
        grid_spec=pltpu.PrefetchScalarGridSpec(
            num_scalar_prefetch=1,
            grid=(1,),
            in_specs=[
                whole_spec((8, D)),
                *in_any(len(arrays)),
                *[whole_spec(block.shape) for block in outward],
                *in_any(len(riders)),
            ],
            out_specs=specs,
            scratch_shapes=[
                *[pltpu.VMEM(array.shape, BF16) for array in arrays],
                pltpu.VMEM((D, out_wide), BF16),
                pltpu.SemaphoreType.DMA((len(arrays),)),
            ],
        ),
        out_shape=shapes,
        compiler_params=pltpu.CompilerParams(vmem_limit_bytes=VMEM_BYTES),
        cost_estimate=cost(6),
        name="qkv_outer",
    )(scalars, vec, *far(arrays), *outward, *far(riders))


def run_gradient(sources, row_state, layer, shape, earlier=(), riders=()):
    layers, rows, width = shape
    arrays = [array for source in sources for array in source]
    shapes = [shape, (layers, 8, rows), (layers, 8 * -(-(width // 128 + 1) // 8), 128)]

    def of_layer(shape):
        return pl.BlockSpec((1, *shape[1:]), lambda *_: (layer, 0, 0))

    return pl.pallas_call(
        functools.partial(
            gradient_kernel, [len(source) for source in sources], matrix_cuts(width)
        ),
        grid=(1,),
        in_specs=[
            *[whole_spec(array.shape) for array in arrays],
            of_layer(row_state.shape),
            *in_any(len(earlier) + len(riders)),
        ],
        out_specs=[of_layer(shape) for shape in shapes],
        out_shape=[jax.ShapeDtypeStruct(shape, F32) for shape in shapes],
        input_output_aliases={len(arrays) + 1 + k: k for k in range(len(earlier))},
        compiler_params=pltpu.CompilerParams(vmem_limit_bytes=VMEM_BYTES),
        cost_estimate=cost(2),
        name="gradient",
    )(*arrays, row_state, *earlier, *riders)


def run_whole(kernel, arrays, shapes, name):
    return pl.pallas_call(
        functools.partial(kernel, matrix_cuts(arrays[0].shape[2])),
        grid=(1,),
        in_specs=[whole_spec(array.shape) for array in arrays],
        out_specs=[whole_spec(shape) for shape, _ in shapes],
        out_shape=[jax.ShapeDtypeStruct(shape, kind) for shape, kind in shapes],
        compiler_params=pltpu.CompilerParams(vmem_limit_bytes=VMEM_BYTES),
        cost_estimate=cost(2),
        name=name,
    )(*arrays)


def example_kernel(layers, sequences, scalars, *refs):
    out = refs[-1]
    out[...] = jnp.zeros_like(out)
    seq_place = scalars[0]
    mine = jnp.where(seq_place == 0, 1.0, 0.0)
    for s in range(sequences):
        for i in range(layers):
            of_mlp, of_attention = refs[2 * (i * sequences + s) : 2 * (i * sequences + s) + 2]
            at = s * layers + i
            out[at, 0:2] = of_attention[0:2]
            out[at, 2:4] = of_mlp[0:2]
            out[at, 4:5] = of_mlp[3:4] * mine
            out[at, pl.ds(5 + seq_place, 1)] = of_mlp[2:3]
            wide = 3 * D * D // FF
            out[at, pl.ds(5 + FF // D + seq_place, 1), :wide] = of_attention[2:3, :wide]


def run_example(scalars, sums, sequences):
    arrays = [array for layer in sums for pair in layer for array in pair]
    shape = (sequences * len(sums), 16, D)
    return pl.pallas_call(
        functools.partial(example_kernel, len(sums), sequences),
        grid_spec=pltpu.PrefetchScalarGridSpec(
            num_scalar_prefetch=1,
            grid=(1,),
            in_specs=[whole_spec(array.shape) for array in arrays],
            out_specs=whole_spec(shape),
        ),
        out_shape=jax.ShapeDtypeStruct(shape, F32),
        cost_estimate=cost(1),
        name="examples",
    )(scalars, *arrays)


def example_vector(rows):
    groups = FF // D
    wide = 3 * D // groups
    qkv = [
        part for k in range(groups) for part in natural_heads(rows[5 + groups + k : 6 + groups + k, :wide])
    ]
    up = [rows[5 + k : 6 + k] for k in range(groups)]
    return jnp.concatenate(
        [*[rows[k : k + 1] for k in range(4)], *qkv, rows[4:5], *up, rows[4:5]], axis=1
    )


def small_kernel(length, totals, examples, state, params, grads, moments, new, scores):
    layers = state.shape[0]
    sequences = scores.shape[0]
    lane = lax.broadcasted_iota(jnp.int32, (1, scores.shape[1]), 1)
    row = lax.broadcasted_iota(jnp.int32, totals.shape[1:], 0)
    weight = jnp.where(row == 4, 2.0, 1.0)

    def product(left, right):
        value = jnp.sum(left * right * weight, axis=1, keepdims=True)
        return jnp.sum(value, axis=0, keepdims=True)

    query = [totals[layers + i] for i in range(layers)]
    mean = sum(product(rows, rows) for rows in query) / (layers * SMALL)
    spread = length * layers * SMALL * (mean + 1e-06)
    for s in range(sequences):
        each = [examples[s * layers + i] for i in range(layers)]
        norm = sum(product(rows, rows) for rows in each) / (layers * SMALL * length)
        influence = sum(product(*pair) for pair in zip(each, query)) / jnp.sqrt(spread)
        scores[s : s + 1] = jnp.where(lane == 0, norm, influence)
    edges = [0, D, 2 * D, 3 * D, 4 * D, 7 * D, 8 * D, 8 * D + FF, SMALL]
    for i in range(layers):
        place = slice(i, i + 1)
        gradient = example_vector(totals[i])
        grads[place] = gradient
        moment = DECAY * state[place] + (1.0 - DECAY) * (gradient * gradient + EPS_SQUARE)
        moments[place] = moment
        for first, end in zip(edges, edges[1:]):
            columns = slice(first, end)
            update = gradient[:, columns] * lax.rsqrt(moment[:, columns])
            old = params[place, columns]
            rms = jnp.sqrt(jnp.mean(update * update, axis=1, keepdims=True))
            old_rms = jnp.sqrt(jnp.mean(old * old, axis=1, keepdims=True))
            new[place, columns] = old - RATE * old_rms * (update / jnp.maximum(1.0, rms))


def run_small(length, totals, examples, state, params, sequences):
    arrays = [totals, examples, state, params]
    shapes = [state.shape] * 3 + [(sequences, 128)]
    return pl.pallas_call(
        functools.partial(small_kernel, length),
        grid=(1,),
        in_specs=[whole_spec(array.shape) for array in arrays],
        out_specs=[whole_spec(shape) for shape in shapes],
        out_shape=[jax.ShapeDtypeStruct(shape, F32) for shape in shapes],
        cost_estimate=cost(2),
        name="small_vectors",
    )(*arrays)


def half_spec(array, place, flipped=False):
    def index(h):
        half = 1 - h if flipped else h
        return (half, 0, 0) if place is None else (place, half, 0, 0)

    block = (None, *array.shape[-2:])
    return pl.BlockSpec(block if place is None else (None, *block), index)


def run_finish(kernel, sums, received, others, bias, name):
    keep, near, _ = sums
    shape = keep.shape
    arrays = [(keep, None), (near, None), (received, None), *others]
    specs = [half_spec(array, place, k == 2) for k, (array, place) in enumerate(arrays)]
    return pl.pallas_call(
        kernel,
        grid=(2,),
        in_specs=specs + ([] if bias is None else [whole_spec(bias.shape)]),
        out_specs=[half_spec(keep, None)] * 2,
        out_shape=[pltpu.HBM(shape, F32), jax.ShapeDtypeStruct(shape, BF16)],
        compiler_params=pltpu.CompilerParams(vmem_limit_bytes=VMEM_BYTES),
        cost_estimate=cost(2),
        name=name,
    )(*far([array for array, _ in arrays]), *([] if bias is None else [bias]))


def last_kernel(kernel, count, n_inputs, *refs):
    out = refs[-1]
    bias = refs[count * n_inputs : -1]
    for s in range(count):
        kernel(*refs[n_inputs * s : n_inputs * (s + 1)], *bias, out.at[s])


def run_last(kernel, sums, received, others, bias, kind, name):
    arrays, specs = [], []
    for (keep, near, _), across, more in zip(sums, received, others):
        chunk = keep.shape[-2]
        arrays += [keep, near, across]
        half = pl.BlockSpec((None, chunk, D), lambda i: (0, 0, 0))
        specs += [half, half, whole_spec(across.shape)]
        for array, place in more:
            arrays.append(array)
            if place is None:
                specs.append(half)
            else:
                specs.append(
                    pl.BlockSpec((None, None, chunk, D), lambda i, place=place: (place, 0, 0, 0))
                )
    count = len(sums)
    return pl.pallas_call(
        functools.partial(last_kernel, kernel, count, len(arrays) // count),
        grid=(1,),
        in_specs=specs + ([] if bias is None else [whole_spec(bias.shape)]),
        out_specs=whole_spec((count, chunk, D)),
        out_shape=jax.ShapeDtypeStruct((count, chunk, D), kind),
        compiler_params=pltpu.CompilerParams(vmem_limit_bytes=VMEM_BYTES),
        cost_estimate=cost(2),
        name=name,
    )(*far(arrays), *([] if bias is None else [bias]))


def pass_through_kernel(*refs):
    del refs


def after(values, *others):
    return pl.pallas_call(
        pass_through_kernel,
        in_specs=in_any(1 + len(others)),
        out_specs=pl.BlockSpec(memory_space=pl.ANY),
        out_shape=jax.ShapeDtypeStruct(values.shape, values.dtype),
        input_output_aliases={0: 0},
        name="after",
    )(values, *others)


def out_blocks(columns, dp_place, seq_place):
    stacked = jnp.zeros((D, columns[0].shape[1]), BF16)
    for column, place in zip(columns, piece_places(len(columns), dp_place)):
        stacked = lax.dynamic_update_slice(stacked, column, (place * column.shape[0], 0))
    size = lax.axis_size("seq")
    return exchange_blocks(stacked.reshape(size, D // size, -1), seq_place)


def on_device(block_in, cotangent, labels, master, small_params, row_state, col_state, small_state):
    sequences, chunk = block_in.shape[:2]
    group_count = lax.axis_size("seq")
    seq_place, dp_place = lax.axis_index("seq"), lax.axis_index("dp")
    length = chunk * group_count
    flags = (labels == 0).astype(jnp.int32)
    place = jnp.concatenate(
        [jnp.stack([seq_place % 2, seq_place // 2, dp_place]).astype(jnp.int32), flags]
    )
    train_flag = flags.astype(F32)
    scalars = jnp.concatenate(
        [jnp.stack([dp_place % 2, seq_place]).astype(jnp.int32), flags]
    )
    query_flag = 1.0 - train_flag
    wide, out_wide, quarter = 3 * D // group_count, D // group_count, FF // group_count
    cuts = matrix_cuts(master.shape[2])
    split = lax.axis_size("dp") == 8
    x_bit, z_place = dp_place % 2, dp_place // 2
    tables = rotary_tables(length)

    def normalise(stream):
        scaled, inverse = apply_layer_norm(stream)
        low_scaled = scaled.astype(BF16)
        return (scaled, inverse), low_scaled

    stream = both_halves(block_in)
    _, low_scaled = normalise(stream.astype(F32))
    near = swap(low_scaled, "seq", 1)
    chunks = [((low_scaled, s), (near, s)) for s in range(sequences)]

    low = master.astype(BF16)
    rows_of = [
        jnp.concatenate([heads_together(low[i, :, : cuts[1]]), low[i, :, cuts[1] :]], axis=1)
        for i in range(LAYERS)
    ]
    pieces = gather_rows(rows_of[0])
    whole_one = lax.all_gather(after(rows_of[1], *pieces[4:5]), "dp", axis=0, tiled=True)

    def weight_of(pieces):
        columns = [piece[:, wide : wide + out_wide] for piece in pieces]
        return out_blocks(columns, dp_place, seq_place), [(pieces, 0), (pieces, cuts[2])]

    weights = [weight_of(pieces)]
    vectors, params = [], []
    for i in range(LAYERS):
        param = unpack(small_params[i])
        params.append(param)
        bias_qkv = heads_together(lax.dynamic_slice_in_dim(param[4], seq_place * wide, wide))
        bias_up = lax.dynamic_slice_in_dim(param[6], seq_place * quarter, quarter)
        vectors.append(
            jnp.stack(
                [
                    *param[:4],
                    jnp.pad(bias_up, (0, D - quarter)),
                    jnp.pad(bias_qkv, (0, D - wide)),
                    jnp.zeros((D,), F32),
                    jnp.zeros((D,), F32),
                ]
            )
        )

    streams = [[(stream, s) for s in range(sequences)]]
    saved_all = []
    open_sum = None

    def close_sum(behind):
        nonlocal open_sum
        sums, received, finish = open_sum
        open_sum = None
        finish(sums, after(received, behind))

    def open_exchange(keep, send, behind, finish):
        nonlocal open_sum
        if open_sum is not None:
            send = after(send, open_sum[1])
            close_sum(behind)
        sums = core_sum(keep, send)
        open_sum = (sums, swap(sums[2], "seq", 2), finish)
        return [sums[2]]

    def own_exchange(keep, send):
        near = swap(send, "seq", 1)
        low = (keep[1] + near[1].astype(F32)).astype(BF16)
        return (keep, near, None), swap(low, "seq", 2)

    both_grads = both_halves(cotangent)
    near_grads = swap(both_grads, "seq", 1)
    riders = []
    for i in range(LAYERS):
        last = i == LAYERS - 1
        saved_all.append([])
        next_chunks, next_streams, ends = [], [], []
        bias = (params[i][5] + params[i][7])[None]

        def finish_stream(s, old, bias, next_chunks, next_streams, sums, received):
            fresh, low = run_finish(
                finish_stream_kernel, sums, received, [old], bias, "finish_stream"
            )
            next_streams.append((fresh, None))
            next_chunks.append(((low, None), (swap(low, "seq", 1), None)))

        for s in range(sequences):
            keep, send, *saved = run_forward(
                place, chunks[s], vectors[i], tables, weights[i], riders
            )
            saved_all[i].append(saved)
            if last:
                if open_sum is not None:
                    send = after(send, open_sum[1])
                    close_sum(saved[0])
                ends.append(own_exchange(keep, send))
                continue
            riders = open_exchange(
                keep,
                send,
                saved[0],
                functools.partial(
                    finish_stream, s, streams[i][s], bias, next_chunks, next_streams
                ),
            )
            if i == 0:
                riders = riders + [near_grads]
        if i == 0:
            whole_one = after(whole_one, saved_all[0][0][0])
            weights.append(weight_of([whole_one]))
        if last:
            break
        chunks = next_chunks
        streams.append(next_streams)
    block_out = run_last(
        finish_stream_kernel,
        [sums for sums, _ in ends],
        [received for _, received in ends],
        [[old] for old in streams[-1]],
        bias,
        BF16,
        "block_out",
    )

    grads = [(both_grads, s) for s in range(sequences)]
    chunks = [((both_grads, s), (near_grads, s)) for s in range(sequences)]
    sources, sums = [None] * LAYERS, [None] * LAYERS
    riders, later, latest = [], [], []
    for i in reversed(range(LAYERS)):
        last = i == 0
        xhats, qks, vals, atts, lses, hids, slopes = zip(*saved_all[i])
        mlp, attention, next_chunks, next_grads, ends = [], [], [], [], []

        def finish_grad(s, others, next_chunks, next_grads, sums, received):
            fresh, low = run_finish(
                finish_grad_kernel, sums, received, others, None, "finish_grad"
            )
            next_grads.append((fresh, None))
            next_chunks.append(((low, None), (swap(low, "seq", 1), None)))

        for s in range(sequences):
            mlp.append(
                run_mlp_backward(
                    place,
                    s,
                    s == sequences - 1,
                    chunks[s],
                    vectors[i],
                    weights[i],
                    xhats[s],
                    slopes[s],
                    atts[s],
                    mlp[s - 1][4:] if s else [],
                    riders,
                )
            )
            riders = [mlp[s][3]]
            if open_sum is not None:
                close_sum(mlp[s][3])
            if s == 0:
                riders += later
        outward = [
            block if k == 0 else swap(block, "seq", k) for k, block in enumerate(mlp[-1][4:])
        ]
        groups_b = [xhats, [out[0] for out in mlp], [out[1] for out in mlp], hids]
        both = run_mlp_outer(
            scalars, vectors[i], groups_b, split, [block_out, *latest] if last else []
        )
        riders = [both[-1], *outward]
        for s in range(sequences):
            keep, send, grad_joined, sums_t = run_attention_backward(
                place,
                mlp[s][0],
                vectors[i],
                tables,
                weights[i],
                xhats[s],
                qks[s],
                vals[s],
                lses[s],
                mlp[s][2],
                riders,
            )
            attention.append((grad_joined, sums_t))
            if last:
                riders = []
                ends.append(own_exchange(keep, send))
            else:
                riders = open_exchange(
                    keep,
                    send,
                    grad_joined,
                    functools.partial(
                        finish_grad, s, [grads[s], streams[i][s]], next_chunks, next_grads
                    ),
                )
        if split and not last:
            total_b = pair_total(*both)
            part_b = scatter_along_z(total_b)
        if split and last:
            total_b = pair_total(after(both[0], *[out[0] for out in attention]), both[1])
            part_b = scatter_along_z(total_b)
            riders = [total_b]
        elif not split:
            part_b = lax.psum_scatter(both[0], "dp", scatter_dimension=0, tiled=True)
        groups = [xhats, [out[0] for out in attention]]
        rest = run_qkv_outer(scalars, vectors[i], groups, outward, split, riders)
        if not split:
            part_a = [lax.psum_scatter(rest[0], "dp", scatter_dimension=0, tiled=True)]
        elif last:
            own_a, parts_a = pair_sum(after(rest[0], part_b), rest[1], z_place)
            part_a = [own_a, *exchange_parts(parts_a)]
        else:
            total_a = pair_total(*rest)
            part_a = [scatter_along_z(total_a)]
            later, latest = [total_b], [total_a]
        sources[i] = [[part_b], part_a]
        riders = rest[:1]
        chunks = next_chunks
        grads = next_grads or grads
        sums[i] = [(out[3], other[1]) for out, other in zip(mlp, attention)]
    behind_a = parts_a[:1] if split else rest
    grad_stream = run_last(
        finish_grad_kernel,
        [sums_of for sums_of, _ in ends],
        [after(received, *behind_a) for _, received in ends],
        [[grad, old] for grad, old in zip(grads, streams[0])],
        None,
        F32,
        "input_grad",
    )

    examples = after(run_example(scalars[1:2], sums, sequences), *behind_a)
    examples = sum_pairwise(examples, "seq", BF16)
    stacked = ()
    for i in reversed(range(LAYERS)):
        behind = [] if i else [examples, grad_stream]
        stacked = run_gradient(sources[i], row_state, i, master.shape, stacked, behind)
    reduced_all, row_part, col_part = stacked
    dp_bits, seq_bits = [], []
    for axis, bits in (("dp", dp_bits), ("seq", seq_bits)):
        bits += [(axis, 1 << k) for k in range(lax.axis_size(axis).bit_length() - 1)]
    first_steps = max(len(seq_bits), len(dp_bits))
    flat = examples.reshape(sequences, -1)
    small = jnp.stack(
        [
            jnp.sum(train_flag[:, None] * flat, axis=0),
            jnp.sum((1.0 - train_flag)[:, None] * flat, axis=0),
        ]
    ).reshape(2 * LAYERS, *examples.shape[1:])
    small_steps = list(dp_bits)

    def small_step():
        nonlocal small_steps
        step, *small_steps = small_steps
        sent = small.astype(BF16)
        return sent, swap(sent, *step)

    def together(values):
        nonlocal small
        received = [swap(value, *step) for value, step in values]
        sent = None
        if small_steps:
            sent, small_in = small_step()
            received.append(small_in)
        if len(received) > 1:
            received = [
                after(value, *[other for other in received if other is not value])
                for value in received
            ]
        if sent is not None:
            small = sent.astype(F32) + received.pop().astype(F32)
        return [value + other for (value, _), other in zip(values, received)]

    for k in range(first_steps):
        now = []
        if k < len(seq_bits):
            now.append((row_part, seq_bits[k]))
        if k < len(dp_bits):
            now.append((col_part, dp_bits[k]))
        *rest_sums, last_sum = together(now)
        if k < len(seq_bits) and k < len(dp_bits):
            (row_part,), col_part = rest_sums, last_sum
        elif k < len(dp_bits):
            col_part = last_sum
        else:
            row_part = last_sum
    layers = master.shape[0]
    fresh_row_moments, col_stats, local_sums = run_whole(
        square_kernel,
        [reduced_all, master, row_part, col_part, row_state, col_state],
        [(row_state.shape, F32), (col_state.shape, F32), ((8, 128), F32)],
        "squares",
    )
    state_sums = local_sums
    for step in seq_bits:
        (local_sums,) = together([(local_sums, step)])
    seq_sums = jnp.concatenate(
        [local_sums[: 2 * layers], state_sums[layers : 2 * layers], local_sums[3 * layers :]], axis=0
    )
    for step in dp_bits:
        (local_sums,) = together([(local_sums, step)])
    while small_steps:
        together([])
    small_grads, small_moments, small_new, scores = run_small(
        length, small, examples, small_state, small_params, sequences
    )
    example_norms, influence = scores[:, 0], scores[:, 1]
    new_master, new_low = run_whole(
        update_kernel,
        [reduced_all, master, fresh_row_moments, col_stats, local_sums, seq_sums],
        [(master.shape, F32), (master.shape, BF16)],
        "update",
    )
    return (
        block_out,
        grad_stream,
        example_norms,
        influence,
        reduced_all,
        fresh_row_moments,
        col_stats,
        new_master,
        new_low,
        small_grads,
        small_moments,
        small_new,
    )


def solution(mesh):
    placed = (
        P("dp", "seq", None),
        P("dp", "seq", None),
        P("dp"),
        P(None, "dp", "seq"),
        P(),
        P(None, None, "dp"),
        P(None, "seq"),
        P(),
    )
    return jax.shard_map(
        on_device,
        mesh=mesh,
        in_specs=placed,
        out_specs=(
            P("dp", "seq", None),
            P("dp", "seq", None),
            P("dp"),
            P("dp"),
            P(None, "dp", "seq"),
            P(None, None, "dp"),
            P(None, "seq"),
            P(None, "dp", "seq"),
            P(None, "dp", "seq"),
            P(),
            P(),
            P(),
        ),
        check_vma=False,
    )
```

profile of v0, /device:TPU:0, one launch (start us, length us, event | category | flops | bytes accessed | tf_op | source)
XLA Modules:
  0.0 421.3 jit_solution(9604253139500424077)
XLA Ops:
  7.2 1.6 convert_element_type.169
  9.8 3.0 collective-permute-start.2
  12.8 1.6 collective-permute-start.3
  14.4 1.5 collective-permute-start
  19.1 7.4 %collective-permute-done.3.refs_12_.refs_20_.refs_8_.refs_16_ = bf16[96,2304]{1,0:T(8,128)(2,1)} collective-permute-done((bf16[96,2304]{1,0:T(8,128)(2,1)S(1)}, bf16[96,2304]{1,0:T(8,128)(2,1)}, u32[]{:S(2)}, u32[]{:S(2)}) %collective-permute-start.3) | collective-permute-done | bytes 442400 | tf_op jit(solution)/shard_map/ppermute | solution.py:94
  28.9 10.8 %collective-permute-done.5.refs_14_.refs_22_.refs_1_.refs_10_.refs_18_ = bf16[96,2304]{1,0:T(8,128)(2,1)S(1)} collective-permute-done((bf16[96,2304]{1,0:T(8,128)(2,1)}, bf16[96,2304]{1,0:T(8,128)(2,1)S(1)}, u32[]{:S(2)}, u32[]{:S(2)}) %collective-permute-start.5) | collective-permute-done | bytes 442400 | tf_op jit(solution)/shard_map/ppermute | solution.py:94
  45.0 19.7 %collective-permute-done.7.refs_16_.refs_24_.refs_12_.refs_20_ = bf16[96,2304]{1,0:T(8,128)(2,1)S(1)} collective-permute-done((bf16[96,2304]{1,0:T(8,128)(2,1)S(1)}, bf16[96,2304]{1,0:T(8,128)(2,1)S(1)}, u32[]{:S(2)}, u32[]{:S(2)}) %collective-permute-start.7) | collective-permute-done | bytes 442400 | tf_op jit(solution)/shard_map/ppermute | solution.py:94
  64.9 8.0 %collective-permute-done.8.refs_17_.refs_25_.refs_13_.refs_21_ = bf16[96,2304]{1,0:T(8,128)(2,1)S(1)} collective-permute-done((bf16[96,2304]{1,0:T(8,128)(2,1)S(1)}, bf16[96,2304]{1,0:T(8,128)(2,1)S(1)}, u32[]{:S(2)}, u32[]{:S(2)}) %collective-permute-start.8) | collective-permute-done | bytes 442400 | tf_op jit(solution)/shard_map/ppermute | solution.py:66
  73.2 1.6 collective-permute-start.10
  76.9 1.9 collective-permute-done.10.refs_8_.refs_7_
  80.0 13.9 %layer_forward.4 = (f32[2,192,768]{2,1,0:T(8,128)}, bf16[2,192,768]{2,1,0:T(8,128)(2,1)S(1)}, bf16[768,768]{1,0:T(8,128)(2,1)}, bf16[768,384]{1,0:T(8,128)(2,1)}...) custom-call(s32[5]{0:T(128)S(1)} %pad_add_fusion.place, ...), custom_call_target="tpu_custom_call" | custom-call | flops 12999999488 | bytes 13000000 | tf_op jit(solution)/shard_map/layer_forward/pallas_call | solution.py:790
  94.8 1.6 collective-permute-done.12.near
  96.4 1.7 add_convert_fusion.6.refs_26_
  98.1 1.6 collective-permute-start.13
  99.7 14.1 %layer_forward.5 = (f32[2,192,768]{2,1,0:T(8,128)}, bf16[2,192,768]{2,1,0:T(8,128)(2,1)S(1)}, bf16[768,768]{1,0:T(8,128)(2,1)}, bf16[768,384]{1,0:T(8,128)(2,1)}...) custom-call(s32[5]{0:T(128)S(1)} %pad_add_fusion.place, ...), custom_call_target="tpu_custom_call" | custom-call | flops 12999999488 | bytes 13000000 | tf_op jit(solution)/shard_map/layer_forward/pallas_call | solution.py:790
  117.1 2.8 finish_stream.2
  125.6 2.0 collective-permute-done.18.refs_8_.refs_7_
  128.0 14.2 %layer_forward.6 = (f32[2,192,768]{2,1,0:T(8,128)}, bf16[2,192,768]{2,1,0:T(8,128)(2,1)S(1)}, bf16[768,768]{1,0:T(8,128)(2,1)}, bf16[768,384]{1,0:T(8,128)(2,1)}...) custom-call(s32[5]{0:T(128)S(1)} %pad_add_fusion.place, ...), custom_call_target="tpu_custom_call" | custom-call | flops 12999999488 | bytes 13000000 | tf_op jit(solution)/shard_map/layer_forward/pallas_call | solution.py:790
  143.1 1.6 collective-permute-start.22
  144.6 2.8 finish_stream.3
  147.5 8.2 %mlp_backward.4 = (bf16[768,768]{1,0:T(8,128)(2,1)}, bf16[768,768]{1,0:T(8,128)(2,1)}, bf16[768,768]{1,0:T(8,128)(2,1)}, f32[8,768]{1,0:T(8,128)}, f32[192,768]{1,0:T(8,128)}) custom-call(s32[5]{0:T(128)S(1)} %pad_add_fusion.place, bf16[2,2,192,768]{3,2,1,0:T(8,128)(2,1)S(1)} %pad_maximum_fusion.1.refs_0_.grad, ...), custom_call_target="tpu_custom_call" | custom-call | flops 8000000000 | bytes 8000000 | tf_op jit(solution)/shard_map/mlp_backward/pallas_call | solution.py:837
  155.7 13.9 %layer_forward.7 = (f32[2,192,768]{2,1,0:T(8,128)}, bf16[2,192,768]{2,1,0:T(8,128)(2,1)S(1)}, bf16[768,768]{1,0:T(8,128)(2,1)}, bf16[768,384]{1,0:T(8,128)(2,1)}...) custom-call(s32[5]{0:T(128)S(1)} %pad_add_fusion.place, ...), custom_call_target="tpu_custom_call" | custom-call | flops 12999999488 | bytes 13000000 | tf_op jit(solution)/shard_map/layer_forward/pallas_call | solution.py:790
  170.1 8.3 %mlp_backward.5 = (bf16[768,768]{1,0:T(8,128)(2,1)}, bf16[768,768]{1,0:T(8,128)(2,1)}, bf16[768,768]{1,0:T(8,128)(2,1)}, f32[8,768]{1,0:T(8,128)}, bf16[192,192]...) custom-call(s32[5]{0:T(128)S(1)} %pad_add_fusion.place, ...), custom_call_target="tpu_custom_call" | custom-call | flops 8000000000 | bytes 8000000 | tf_op jit(solution)/shard_map/mlp_backward/pallas_call | solution.py:837
  181.0 10.4 %mlp_outer.2 = (f32[4,96,1536]{2,1,0:T(8,128)S(1)}, bf16[4,96,1536]{2,1,0:T(8,128)(2,1)}) custom-call(s32[4]{0:T(128)S(1)} %pad_add_fusion.1.scalars, f32[8,768]{1,0:T(8,128)S(1)} %stack.79.refs_2_.vec.refs_1_, bf16[768,768]{1,0:T(8,128)(2,1)} %get-tuple-element.131.refs_1_.refs_3_.refs_0_.refs_9_, bf16[768,768]{1,0:T(8,128)(2,1)} %get-tuple-element.143.refs_1_, ...), custom_call_target="tpu_custom_call" | custom-call | flops 10000000000 | bytes 10000000 | tf_op jit(solution)/shard_map/mlp_outer/pallas_call | solution.py:963
  192.1 11.7 %attention_backward.4 = (f32[2,192,768]{2,1,0:T(8,128)}, bf16[2,192,768]{2,1,0:T(8,128)(2,1)S(1)}, bf16[768,576]{1,0:T(8,128)(2,1)}, f32[8,768]{1,0:T(8,128)}) custom-call(s32[5]{0:T(128)S(1)} %pad_add_fusion.place, bf16[768,768]{1,0:T(8,128)(2,1)} %get-tuple-element.138.refs_2_.refs_0_, f32[8,768]{1,0:T(8,128)S(1)} %stack.79.refs_2_.vec.refs_1_, ...), custom_call_target="tpu_custom_call" | custom-call | flops 11000000512 | bytes 11000000 | tf_op jit(solution)/shard_map/attention_backward/pallas_call | solution.py:900
  204.3 1.8 fusion.4
  210.7 12.1 %attention_backward.5 = (f32[2,192,768]{2,1,0:T(8,128)}, bf16[2,192,768]{2,1,0:T(8,128)(2,1)S(1)}, bf16[768,576]{1,0:T(8,128)(2,1)}, f32[8,768]{1,0:T(8,128)}) custom-call(s32[5]{0:T(128)S(1)} %pad_add_fusion.place, bf16[768,768]{1,0:T(8,128)(2,1)} %get-tuple-element.151.refs_6_.refs_0_, f32[8,768]{1,0:T(8,128)S(1)} %stack.79.refs_2_.vec.refs_1_, ...), custom_call_target="tpu_custom_call" | custom-call | flops 11000000512 | bytes 11000000 | tf_op jit(solution)/shard_map/attention_backward/pallas_call | solution.py:900
  223.6 10.8 %collective-permute-done.31.refs_0_.refs_1_ = bf16[2,192,768]{2,1,0:T(8,128)(2,1)} collective-permute-done((bf16[2,192,768]{2,1,0:T(8,128)(2,1)S(1)}, bf16[2,192,768]{2,1,0:T(8,128)(2,1)}, u32[]{:S(2)}, u32[]{:S(2)}) %collective-permute-start.31) | collective-permute-done | bytes 589856 | tf_op jit(solution)/shard_map/ppermute | solution.py:66
  234.4 2.6 add_convert_fusion.1
  237.1 3.5 finish_grad.2
  243.1 4.9 %qkv_outer.2 = (f32[4,96,768]{2,1,0:T(8,128)S(1)}, bf16[4,96,768]{2,1,0:T(8,128)(2,1)S(1)}) custom-call(s32[4]{0:T(128)S(1)} %pad_add_fusion.1.scalars, f32[8,768]{1,0:T(8,128)S(1)} %stack.79.refs_2_.vec.refs_1_, bf16[768,768]{1,0:T(8,128)(2,1)} %get-tuple-element.131.refs_1_.refs_3_.refs_0_.refs_9_, bf16[768,576]{1,0:T(8,128)(2,1)} %get-tuple-element.168.refs_1_, ...), custom_call_target="tpu_custom_call" | custom-call | flops 6000000000 | bytes 6000000 | tf_op jit(solution)/shard_map/qkv_outer/pallas_call | solution.py:986
  249.0 1.7 collective-permute-start.37
  250.8 8.1 %mlp_backward.6 = (bf16[768,768]{1,0:T(8,128)(2,1)}, bf16[768,768]{1,0:T(8,128)(2,1)}, bf16[768,768]{1,0:T(8,128)(2,1)}, f32[8,768]{1,0:T(8,128)}, f32[192,768]{1,0:T(8,128)}) custom-call(s32[5]{0:T(128)S(1)} %pad_add_fusion.place, bf16[2,192,768]{2,1,0:T(8,128)(2,1)S(1)} %get-tuple-element.165.refs_0_, ...), custom_call_target="tpu_custom_call" | custom-call | flops 8000000000 | bytes 8000000 | tf_op jit(solution)/shard_map/mlp_backward/pallas_call | solution.py:837
  259.7 3.5 finish_grad.3
  263.2 3.1 block_out.1.refs_8_
  267.5 7.8 %mlp_backward.7 = (bf16[768,768]{1,0:T(8,128)(2,1)}, bf16[768,768]{1,0:T(8,128)(2,1)}, bf16[768,768]{1,0:T(8,128)(2,1)}, f32[8,768]{1,0:T(8,128)}, bf16[192,192]...) custom-call(s32[5]{0:T(128)S(1)} %pad_add_fusion.place, ...), custom_call_target="tpu_custom_call" | custom-call | flops 8000000000 | bytes 8000000 | tf_op jit(solution)/shard_map/mlp_backward/pallas_call | solution.py:837
  277.2 9.4 %mlp_outer.3 = (f32[4,96,1536]{2,1,0:T(8,128)S(1)}, bf16[4,96,1536]{2,1,0:T(8,128)(2,1)S(1)}) custom-call(s32[4]{0:T(128)S(1)} %pad_add_fusion.1.scalars, f32[8,768]{1,0:T(8,128)S(1)} %stack.74.refs_2_.vec.refs_1_, bf16[768,768]{1,0:T(8,128)(2,1)} %get-tuple-element.125.refs_1_.refs_3_.refs_0_.refs_9_, bf16[768,768]{1,0:T(8,128)(2,1)} %get-tuple-element.177.refs_1_, ...), custom_call_target="tpu_custom_call" | custom-call | flops 10000000000 | bytes 10000000 | tf_op jit(solution)/shard_map/mlp_outer/pallas_call | solution.py:963
  288.4 12.0 %attention_backward.7 = (f32[2,192,768]{2,1,0:T(8,128)}, bf16[2,192,768]{2,1,0:T(8,128)(2,1)S(1)}, bf16[768,576]{1,0:T(8,128)(2,1)}, f32[8,768]{1,0:T(8,128)}) custom-call(s32[5]{0:T(128)S(1)} %pad_add_fusion.place, bf16[768,768]{1,0:T(8,128)(2,1)} %get-tuple-element.186.refs_6_.refs_0_, f32[8,768]{1,0:T(8,128)S(1)} %stack.74.refs_2_.vec.refs_1_, ...), custom_call_target="tpu_custom_call" | custom-call | flops 11000000512 | bytes 11000000 | tf_op jit(solution)/shard_map/attention_backward/pallas_call | solution.py:900
  301.2 12.0 %attention_backward.6 = (f32[2,192,768]{2,1,0:T(8,128)}, bf16[2,192,768]{2,1,0:T(8,128)(2,1)S(1)}, bf16[768,576]{1,0:T(8,128)(2,1)}, f32[8,768]{1,0:T(8,128)}) custom-call(s32[5]{0:T(128)S(1)} %pad_add_fusion.place, bf16[768,768]{1,0:T(8,128)(2,1)} %get-tuple-element.172.refs_2_.refs_0_, f32[8,768]{1,0:T(8,128)S(1)} %stack.74.refs_2_.vec.refs_1_, ...), custom_call_target="tpu_custom_call" | custom-call | flops 11000000512 | bytes 11000000 | tf_op jit(solution)/shard_map/attention_backward/pallas_call | solution.py:900
  313.2 3.5 collective-permute-done.43
  316.8 3.3 add_convert_fusion
  321.3 1.6 examples.1.refs_0_
  322.9 5.2 %qkv_outer.3 = (f32[4,96,768]{2,1,0:T(8,128)S(1)}, bf16[4,96,768]{2,1,0:T(8,128)(2,1)S(1)}) custom-call(s32[4]{0:T(128)S(1)} %pad_add_fusion.1.scalars, f32[8,768]{1,0:T(8,128)S(1)} %stack.74.refs_2_.vec.refs_1_, bf16[768,768]{1,0:T(8,128)(2,1)} %get-tuple-element.125.refs_1_.refs_3_.refs_0_.refs_9_, bf16[768,576]{1,0:T(8,128)(2,1)} %get-tuple-element.196.refs_1_, ...), custom_call_target="tpu_custom_call" | custom-call | flops 6000000000 | bytes 6000000 | tf_op jit(solution)/shard_map/qkv_outer/pallas_call | solution.py:986
  337.4 9.0 %reduce-scatter.4.cloned.1.call-done.refs_1_.refs_0_ = bf16[96,1536]{1,0:T(8,128)(2,1)} async-done(((bf16[384,1536]{1,0:T(8,128)(2,1)}), bf16[96,1536]{1,0:T(8,128)(2,1)}) %reduce-scatter.4.cloned.1.call-update) | async-done | bytes 294928 | tf_op jit(solution)/shard_map/reduce_scatter | solution.py:119
  346.4 1.5 convert_add_fusion
  348.1 1.7 collective-permute-start.51
  349.8 2.7 collective-permute-start.52
  354.9 4.0 input_grad.1.refs_10_
  358.9 1.5 collective-permute-start.48
  361.4 2.2 collective-permute-done.48
  364.8 1.5 collective-permute-start.49
  369.8 1.5 collective-permute-done.54.refs_2_.refs_1_
  374.4 2.0 collective-permute-start.57
  377.1 1.5 collective-permute-start.56
  378.5 2.2 collective-permute-done.56.refs_1_
  384.5 2.7 collective-permute-start.59
  387.9 1.9 collective-permute-done.59.refs_1_
  395.9 1.5 collective-permute-start.61
  397.4 1.6 convert_add_fusion.1.totals
  400.1 2.3 small_vectors.1
  404.1 1.5 slice_reduce_fusion
  406.8 2.1 collective-permute-start.64
  408.9 2.4 collective-permute-done.64
  412.1 2.2 update.1
  (399 shorter events, 83.4 us)
Async XLA Ops:
  7.2 112.9 %all-gather.2.cloned.1.call-start = ((), (), s32[]{:S(2)}) async-start(), calls=%async_computation.3 | async-start | bytes 3981312 | tf_op jit(solution)/shard_map/all_gather | solution.py:1266
  9.8 17.1 %collective-permute-start.2 = (bf16[96,2304]{1,0:T(8,128)(2,1)S(1)}, bf16[96,2304]{1,0:T(8,128)(2,1)}, u32[]{:S(2)}, u32[]{:S(2)}) collective-permute-start(bf16[96,2304]{1,0:T(8,128)(2,1)S(1)} %concatenate.23.refs_10_.refs_18_.refs_6_.refs_14_), channel_id=1, source_target_pairs={{0,4},{4,0},{8,12},{12,8},{16,20},{20,16},{24,28},{28,24},{1,5},{5... | collective-permute-start | bytes 1327112 | tf_op jit(solution)/shard_map/ppermute | solution.py:66
  12.8 13.6 %collective-permute-start.3 = (bf16[96,2304]{1,0:T(8,128)(2,1)S(1)}, bf16[96,2304]{1,0:T(8,128)(2,1)}, u32[]{:S(2)}, u32[]{:S(2)}) collective-permute-start(bf16[96,2304]{1,0:T(8,128)(2,1)S(1)} %concatenate.23.refs_10_.refs_18_.refs_6_.refs_14_), channel_id=1, source_target_pairs={{0,8},{4,12},{8,16},{12,20},{16,24},{20,28},{24,0},{28,4},{1,9},{5... | collective-permute-start | bytes 1327112 | tf_op jit(solution)/shard_map/ppermute | solution.py:94
  14.4 26.2 %collective-permute-start = (bf16[2,192,768]{2,1,0:T(8,128)(2,1)S(1)}, bf16[2,192,768]{2,1,0:T(8,128)(2,1)S(1)}, u32[]{:S(2)}, u32[]{:S(2)}) collective-permute-start(bf16[2,192,768]{2,1,0:T(8,128)(2,1)S(1)} %copy-done.41), channel_id=1, source_target_pairs={{0,2},{1,3},{2,0},{3,1},{4,6},{5,7},{6,4},{7,5},{8,10},{9,11},{10,... | collective-permute-start | bytes 1769480 | tf_op jit(solution)/shard_map/ppermute | solution.py:66
  15.9 59.1 %collective-permute-start.14 = (bf16[2,192,768]{2,1,0:T(8,128)(2,1)}, bf16[2,192,768]{2,1,0:T(8,128)(2,1)}, u32[]{:S(2)}, u32[]{:S(2)}) collective-permute-start(bf16[2,192,768]{2,1,0:T(8,128)(2,1)} %param.12), channel_id=1, source_target_pairs={{0,2},{1,3},{2,0},{3,1},{4,6},{5,7},{6,4},{7,5},{8,10},{9,11},{10,... | collective-permute-start | bytes 1769480 | tf_op jit(solution)/shard_map/ppermute | solution.py:66
  26.4 17.5 %collective-permute-start.4 = (bf16[96,2304]{1,0:T(8,128)(2,1)}, bf16[96,2304]{1,0:T(8,128)(2,1)}, u32[]{:S(2)}, u32[]{:S(2)}) collective-permute-start(bf16[96,2304]{1,0:T(8,128)(2,1)} %collective-permute-done.3.refs_12_.refs_20_.refs_8_.refs_16_), channel_id=1, source_target_pairs={{0,4},{4,0},{8,12},{12,8},{16,20},{20,16},{24,28},{28,24},{1,5},{5... | collective-permute-start | bytes 1327112 | tf_op jit(solution)/shard_map/ppermute | solution.py:66
  27.0 12.8 %collective-permute-start.5 = (bf16[96,2304]{1,0:T(8,128)(2,1)}, bf16[96,2304]{1,0:T(8,128)(2,1)S(1)}, u32[]{:S(2)}, u32[]{:S(2)}) collective-permute-start(bf16[96,2304]{1,0:T(8,128)(2,1)} %collective-permute-done.3.refs_12_.refs_20_.refs_8_.refs_16_), channel_id=1, source_target_pairs={{0,8},{4,12},{8,16},{12,20},{16,24},{20,28},{24,0},{28,4},{1,9},{5... | collective-permute-start | bytes 1327112 | tf_op jit(solution)/shard_map/ppermute | solution.py:94
  40.5 289.2 %reduce-scatter.6.cloned.1.call-start = ((), (), s32[]{:S(2)}) async-start(), calls=%async_computation.5 | async-start | bytes 1474560 | tf_op jit(solution)/shard_map/reduce_scatter | solution.py:119
  41.8 35.1 %collective-permute-start.1 = (bf16[2,2,192,768]{3,2,1,0:T(8,128)(2,1)S(1)}, bf16[2,2,192,768]{3,2,1,0:T(8,128)(2,1)S(1)}, u32[]{:S(2)}, u32[]{:S(2)}) collective-permute-start(bf16[2,2,192,768]{3,2,1,0:T(8,128)(2,1)S(1)} %fusion.3.refs_0_), channel_id=1, source_target_pairs={{0,1},{1,0},{2,3},{3,2},{4,5},{5,4},{6,7},{7,6},{8,9},{9,8},{10,11... | collective-permute-start | bytes 3538952 | tf_op jit(solution)/shard_map/ppermute | solution.py:66
  42.5 22.3 %collective-permute-start.6 = (bf16[96,2304]{1,0:T(8,128)(2,1)S(1)}, bf16[96,2304]{1,0:T(8,128)(2,1)S(1)}, u32[]{:S(2)}, u32[]{:S(2)}) collective-permute-start(bf16[96,2304]{1,0:T(8,128)(2,1)S(1)} %copy-done.66), channel_id=1, source_target_pairs={{0,4},{4,0},{8,12},{12,8},{16,20},{20,16},{24,28},{28,24},{1,5},{5... | collective-permute-start | bytes 1327112 | tf_op jit(solution)/shard_map/ppermute | solution.py:66
  43.7 20.9 %collective-permute-start.7 = (bf16[96,2304]{1,0:T(8,128)(2,1)S(1)}, bf16[96,2304]{1,0:T(8,128)(2,1)S(1)}, u32[]{:S(2)}, u32[]{:S(2)}) collective-permute-start(bf16[96,2304]{1,0:T(8,128)(2,1)S(1)} %copy-done.66), channel_id=1, source_target_pairs={{0,8},{4,12},{8,16},{12,20},{16,24},{20,28},{24,0},{28,4},{1,9},{5... | collective-permute-start | bytes 1327112 | tf_op jit(solution)/shard_map/ppermute | solution.py:94
  64.6 8.3 %collective-permute-start.8 = (bf16[96,2304]{1,0:T(8,128)(2,1)S(1)}, bf16[96,2304]{1,0:T(8,128)(2,1)S(1)}, u32[]{:S(2)}, u32[]{:S(2)}) collective-permute-start(bf16[96,2304]{1,0:T(8,128)(2,1)S(1)} %collective-permute-done.7.refs_16_.refs_24_.refs_12_.refs_20_), channel_id=1, source_target_pairs={{0,4},{4,0},{8,12},{12,8},{16,20},{20,16},{24,28},{28,24},{1,5},{5... | collective-permute-start | bytes 1327112 | tf_op jit(solution)/shard_map/ppermute | solution.py:66
  73.1 3.8 collective-permute-start.9
  73.2 5.7 %collective-permute-start.10 = (bf16[192,192]{1,0:T(8,128)(2,1)S(1)}, bf16[192,192]{1,0:T(8,128)(2,1)S(1)}, u32[]{:S(2)}, u32[]{:S(2)}) collective-permute-start(bf16[192,192]{1,0:T(8,128)(2,1)S(1)} %get-tuple-element.246), channel_id=1, source_target_pairs={{0,2},{1,3},{2,0},{3,1},{4,6},{5,7},{6,4},{7,5},{8,10},{9,11},{10,... | collective-permute-start | bytes 221192 | tf_op jit(solution)/shard_map/ppermute | solution.py:66
  74.8 5.3 %collective-permute-start.11 = (bf16[192,192]{1,0:T(8,128)(2,1)S(1)}, bf16[192,192]{1,0:T(8,128)(2,1)S(1)}, u32[]{:S(2)}, u32[]{:S(2)}) collective-permute-start(bf16[192,192]{1,0:T(8,128)(2,1)S(1)} %get-tuple-element.245), channel_id=1, source_target_pairs={{0,3},{1,2},{2,1},{3,0},{4,7},{5,6},{6,5},{7,4},{8,11},{9,10},{10,... | collective-permute-start | bytes 221192 | tf_op jit(solution)/shard_map/ppermute | solution.py:66
  76.5 23.3 %collective-permute-start.15 = (bf16[2,2,192,768]{3,2,1,0:T(8,128)(2,1)S(1)}, bf16[2,2,192,768]{3,2,1,0:T(8,128)(2,1)}, u32[]{:S(2)}, u32[]{:S(2)}) collective-permute-start(bf16[2,2,192,768]{3,2,1,0:T(8,128)(2,1)S(1)} %pad_maximum_fusion.1.refs_0_.grad), channel_id=1, source_target_pairs={{0,1},{1,0},{2,3},{3,2},{4,5},{5,4},{6,7},{7,6},{8,9},{9,8},{10,11... | collective-permute-start | bytes 3538952 | tf_op jit(solution)/shard_map/ppermute | solution.py:66
  98.1 16.6 %collective-permute-start.13 = (bf16[2,192,768]{2,1,0:T(8,128)(2,1)S(1)}, bf16[2,192,768]{2,1,0:T(8,128)(2,1)}, u32[]{:S(2)}, u32[]{:S(2)}) collective-permute-start(bf16[2,192,768]{2,1,0:T(8,128)(2,1)S(1)} %add_convert_fusion.6.refs_26_), channel_id=1, source_target_pairs={{0,2},{1,3},{2,0},{3,1},{4,6},{5,7},{6,4},{7,5},{8,10},{9,11},{10,... | collective-permute-start | bytes 1769480 | tf_op jit(solution)/shard_map/ppermute | solution.py:66
  114.7 8.7 %collective-permute-start.20 = (bf16[2,192,768]{2,1,0:T(8,128)(2,1)}, bf16[2,192,768]{2,1,0:T(8,128)(2,1)}, u32[]{:S(2)}, u32[]{:S(2)}) collective-permute-start(bf16[2,192,768]{2,1,0:T(8,128)(2,1)} %after.25), channel_id=1, source_target_pairs={{0,1},{1,0},{2,3},{3,2},{4,5},{5,4},{6,7},{7,6},{8,9},{9,8},{10,11... | collective-permute-start | bytes 1769480 | tf_op jit(solution)/shard_map/ppermute | solution.py:66
  119.9 5.7 %collective-permute-start.16 = (bf16[2,192,768]{2,1,0:T(8,128)(2,1)S(1)}, bf16[2,192,768]{2,1,0:T(8,128)(2,1)S(1)}, u32[]{:S(2)}, u32[]{:S(2)}) collective-permute-start(bf16[2,192,768]{2,1,0:T(8,128)(2,1)S(1)} %get-tuple-element.124.refs_0_), channel_id=1, source_target_pairs={{0,1},{1,0},{2,3},{3,2},{4,5},{5,4},{6,7},{7,6},{8,9},{9,8},{10,11... | collective-permute-start | bytes 1769480 | tf_op jit(solution)/shard_map/ppermute | solution.py:66
  121.4 4.2 collective-permute-start.17
  122.0 5.7 %collective-permute-start.18 = (bf16[192,192]{1,0:T(8,128)(2,1)S(1)}, bf16[192,192]{1,0:T(8,128)(2,1)S(1)}, u32[]{:S(2)}, u32[]{:S(2)}) collective-permute-start(bf16[192,192]{1,0:T(8,128)(2,1)S(1)} %get-tuple-element.242), channel_id=1, source_target_pairs={{0,2},{1,3},{2,0},{3,1},{4,6},{5,7},{6,4},{7,5},{8,10},{9,11},{10,... | collective-permute-start | bytes 221192 | tf_op jit(solution)/shard_map/ppermute | solution.py:66
  122.7 5.3 %collective-permute-start.19 = (bf16[192,192]{1,0:T(8,128)(2,1)S(1)}, bf16[192,192]{1,0:T(8,128)(2,1)S(1)}, u32[]{:S(2)}, u32[]{:S(2)}) collective-permute-start(bf16[192,192]{1,0:T(8,128)(2,1)S(1)} %get-tuple-element.241), channel_id=1, source_target_pairs={{0,3},{1,2},{2,1},{3,0},{4,7},{5,6},{6,5},{7,4},{8,11},{9,10},{10,... | collective-permute-start | bytes 221192 | tf_op jit(solution)/shard_map/ppermute | solution.py:66
  124.6 18.4 %collective-permute-start.21 = (bf16[2,192,768]{2,1,0:T(8,128)(2,1)S(1)}, bf16[2,192,768]{2,1,0:T(8,128)(2,1)}, u32[]{:S(2)}, u32[]{:S(2)}) collective-permute-start(bf16[2,192,768]{2,1,0:T(8,128)(2,1)S(1)} %add_convert_fusion.5.refs_12_), channel_id=1, source_target_pairs={{0,2},{1,3},{2,0},{3,1},{4,6},{5,7},{6,4},{7,5},{8,10},{9,11},{10,... | collective-permute-start | bytes 1769480 | tf_op jit(solution)/shard_map/ppermute | solution.py:66
  143.1 61.2 %collective-permute-start.22 = (bf16[2,192,768]{2,1,0:T(8,128)(2,1)}, bf16[2,192,768]{2,1,0:T(8,128)(2,1)}, u32[]{:S(2)}, u32[]{:S(2)}) collective-permute-start(bf16[2,192,768]{2,1,0:T(8,128)(2,1)} %after.26), channel_id=1, source_target_pairs={{0,1},{1,0},{2,3},{3,2},{4,5},{5,4},{6,7},{7,6},{8,9},{9,8},{10,11... | collective-permute-start | bytes 1769480 | tf_op jit(solution)/shard_map/ppermute | solution.py:66
  147.4 8.3 %collective-permute-start.24 = (bf16[2,192,768]{2,1,0:T(8,128)(2,1)S(1)}, bf16[2,192,768]{2,1,0:T(8,128)(2,1)S(1)}, u32[]{:S(2)}, u32[]{:S(2)}) collective-permute-start(bf16[2,192,768]{2,1,0:T(8,128)(2,1)S(1)} %get-tuple-element.132.refs_0_), channel_id=1, source_target_pairs={{0,1},{1,0},{2,3},{3,2},{4,5},{5,4},{6,7},{7,6},{8,9},{9,8},{10,11... | collective-permute-start | bytes 1769480 | tf_op jit(solution)/shard_map/ppermute | solution.py:66
  169.6 37.2 %collective-permute-start.25 = (bf16[2,192,768]{2,1,0:T(8,128)(2,1)S(1)}, bf16[2,192,768]{2,1,0:T(8,128)(2,1)S(1)}, u32[]{:S(2)}, u32[]{:S(2)}) collective-permute-start(bf16[2,192,768]{2,1,0:T(8,128)(2,1)S(1)} %get-tuple-element.134), channel_id=1, source_target_pairs={{0,1},{1,0},{2,3},{3,2},{4,5},{5,4},{6,7},{7,6},{8,9},{9,8},{10,11... | collective-permute-start | bytes 1769480 | tf_op jit(solution)/shard_map/ppermute | solution.py:66
  179.1 12.2 %collective-permute-start.27 = (bf16[192,192]{1,0:T(8,128)(2,1)S(1)}, bf16[192,192]{1,0:T(8,128)(2,1)S(1)}, u32[]{:S(2)}, u32[]{:S(2)}) collective-permute-start(bf16[192,192]{1,0:T(8,128)(2,1)S(1)} %get-tuple-element.155), channel_id=1, source_target_pairs={{0,1},{1,0},{2,3},{3,2},{4,5},{5,4},{6,7},{7,6},{8,9},{9,8},{10,11... | collective-permute-start | bytes 221192 | tf_op jit(solution)/shard_map/ppermute | solution.py:66
  179.1 12.2 %collective-permute-start.28 = (bf16[192,192]{1,0:T(8,128)(2,1)S(1)}, bf16[192,192]{1,0:T(8,128)(2,1)S(1)}, u32[]{:S(2)}, u32[]{:S(2)}) collective-permute-start(bf16[192,192]{1,0:T(8,128)(2,1)S(1)} %get-tuple-element.156), channel_id=1, source_target_pairs={{0,2},{1,3},{2,0},{3,1},{4,6},{5,7},{6,4},{7,5},{8,10},{9,11},{10,... | collective-permute-start | bytes 221192 | tf_op jit(solution)/shard_map/ppermute | solution.py:66
  179.8 11.6 %collective-permute-start.29 = (bf16[192,192]{1,0:T(8,128)(2,1)S(1)}, bf16[192,192]{1,0:T(8,128)(2,1)S(1)}, u32[]{:S(2)}, u32[]{:S(2)}) collective-permute-start(bf16[192,192]{1,0:T(8,128)(2,1)S(1)} %get-tuple-element.157), channel_id=1, source_target_pairs={{0,3},{1,2},{2,1},{3,0},{4,7},{5,6},{6,5},{7,4},{8,11},{9,10},{10,... | collective-permute-start | bytes 221192 | tf_op jit(solution)/shard_map/ppermute | solution.py:66
  203.8 5.2 %collective-permute-start.30 = (bf16[2,192,768]{2,1,0:T(8,128)(2,1)S(1)}, bf16[2,192,768]{2,1,0:T(8,128)(2,1)S(1)}, u32[]{:S(2)}, u32[]{:S(2)}) collective-permute-start(bf16[2,192,768]{2,1,0:T(8,128)(2,1)S(1)} %get-tuple-element.159), channel_id=1, source_target_pairs={{0,1},{1,0},{2,3},{3,2},{4,5},{5,4},{6,7},{7,6},{8,9},{9,8},{10,11... | collective-permute-start | bytes 1769480 | tf_op jit(solution)/shard_map/ppermute | solution.py:66
  204.2 30.3 %collective-permute-start.36 = (bf16[4,96,1536]{2,1,0:T(8,128)(2,1)}, bf16[4,96,1536]{2,1,0:T(8,128)(2,1)}, u32[]{:S(2)}, u32[]{:S(2)}) collective-permute-start(bf16[4,96,1536]{2,1,0:T(8,128)(2,1)} %get-tuple-element.153.refs_15_), channel_id=1, source_target_pairs={{0,4},{4,0},{8,12},{12,8},{16,20},{20,16},{24,28},{28,24},{1,5},{5... | collective-permute-start | bytes 3538952 | tf_op jit(solution)/shard_map/ppermute | solution.py:66
  206.1 57.1 %collective-permute-start.23 = (bf16[192,768]{1,0:T(8,128)(2,1)}, bf16[192,768]{1,0:T(8,128)(2,1)}, u32[]{:S(2)}, u32[]{:S(2)}) collective-permute-start(bf16[192,768]{1,0:T(8,128)(2,1)} %fusion.4), channel_id=1, source_target_pairs={{0,2},{1,3},{2,0},{3,1},{4,6},{5,7},{6,4},{7,5},{8,10},{9,11},{10,... | collective-permute-start | bytes 884744 | tf_op jit(solution)/shard_map/ppermute | solution.py:66
  207.6 55.6 %collective-permute-start.26 = (bf16[192,768]{1,0:T(8,128)(2,1)}, bf16[192,768]{1,0:T(8,128)(2,1)}, u32[]{:S(2)}, u32[]{:S(2)}) collective-permute-start(bf16[192,768]{1,0:T(8,128)(2,1)} %fusion.5), channel_id=1, source_target_pairs={{0,2},{1,3},{2,0},{3,1},{4,6},{5,7},{6,4},{7,5},{8,10},{9,11},{10,... | collective-permute-start | bytes 884744 | tf_op jit(solution)/shard_map/ppermute | solution.py:66
  209.8 24.6 %collective-permute-start.31 = (bf16[2,192,768]{2,1,0:T(8,128)(2,1)S(1)}, bf16[2,192,768]{2,1,0:T(8,128)(2,1)}, u32[]{:S(2)}, u32[]{:S(2)}) collective-permute-start(bf16[2,192,768]{2,1,0:T(8,128)(2,1)S(1)} %add_convert_fusion.4.refs_15_), channel_id=1, source_target_pairs={{0,2},{1,3},{2,0},{3,1},{4,6},{5,7},{6,4},{7,5},{8,10},{9,11},{10,... | collective-permute-start | bytes 1769480 | tf_op jit(solution)/shard_map/ppermute | solution.py:66
  234.4 6.8 %collective-permute-start.33 = (bf16[2,192,768]{2,1,0:T(8,128)(2,1)}, bf16[2,192,768]{2,1,0:T(8,128)(2,1)S(1)}, u32[]{:S(2)}, u32[]{:S(2)}) collective-permute-start(bf16[2,192,768]{2,1,0:T(8,128)(2,1)} %after.29), channel_id=1, source_target_pairs={{0,1},{1,0},{2,3},{3,2},{4,5},{5,4},{6,7},{7,6},{8,9},{9,8},{10,11... | collective-permute-start | bytes 1769480 | tf_op jit(solution)/shard_map/ppermute | solution.py:66
  237.1 92.7 %reduce-scatter.8.cloned.1.call-start = ((), (), s32[]{:S(2)}) async-start(), calls=%async_computation.6 | async-start | bytes 737280 | tf_op jit(solution)/shard_map/reduce_scatter | solution.py:119
  240.7 10.1 %collective-permute-start.32 = (bf16[2,192,768]{2,1,0:T(8,128)(2,1)S(1)}, bf16[2,192,768]{2,1,0:T(8,128)(2,1)S(1)}, u32[]{:S(2)}, u32[]{:S(2)}) collective-permute-start(bf16[2,192,768]{2,1,0:T(8,128)(2,1)S(1)} %get-tuple-element.165.refs_0_), channel_id=1, source_target_pairs={{0,1},{1,0},{2,3},{3,2},{4,5},{5,4},{6,7},{7,6},{8,9},{9,8},{10,11... | collective-permute-start | bytes 1769480 | tf_op jit(solution)/shard_map/ppermute | solution.py:66
  242.1 16.7 %collective-permute-start.34 = (bf16[2,192,768]{2,1,0:T(8,128)(2,1)S(1)}, bf16[2,192,768]{2,1,0:T(8,128)(2,1)S(1)}, u32[]{:S(2)}, u32[]{:S(2)}) collective-permute-start(bf16[2,192,768]{2,1,0:T(8,128)(2,1)S(1)} %add_convert_fusion.3.refs_8_), channel_id=1, source_target_pairs={{0,2},{1,3},{2,0},{3,1},{4,6},{5,7},{6,4},{7,5},{8,10},{9,11},{10,... | collective-permute-start | bytes 1769480 | tf_op jit(solution)/shard_map/ppermute | solution.py:66
  249.0 17.3 %collective-permute-start.37 = (bf16[4,96,768]{2,1,0:T(8,128)(2,1)S(1)}, bf16[4,96,768]{2,1,0:T(8,128)(2,1)S(1)}, u32[]{:S(2)}, u32[]{:S(2)}) collective-permute-start(bf16[4,96,768]{2,1,0:T(8,128)(2,1)S(1)} %get-tuple-element.188), channel_id=1, source_target_pairs={{0,4},{4,0},{8,12},{12,8},{16,20},{20,16},{24,28},{28,24},{1,5},{5... | collective-permute-start | bytes 1769480 | tf_op jit(solution)/shard_map/ppermute | solution.py:66
  263.2 4.2 %collective-permute-start.35 = (bf16[2,192,768]{2,1,0:T(8,128)(2,1)S(1)}, bf16[2,192,768]{2,1,0:T(8,128)(2,1)S(1)}, u32[]{:S(2)}, u32[]{:S(2)}) collective-permute-start(bf16[2,192,768]{2,1,0:T(8,128)(2,1)S(1)} %get-tuple-element.180.refs_0_), channel_id=1, source_target_pairs={{0,1},{1,0},{2,3},{3,2},{4,5},{5,4},{6,7},{7,6},{8,9},{9,8},{10,11... | collective-permute-start | bytes 1769480 | tf_op jit(solution)/shard_map/ppermute | solution.py:66
  267.3 79.1 %reduce-scatter.4.cloned.1.call-start = ((), (), s32[]{:S(2)}) async-start(), calls=%async_computation.4 | async-start | bytes 1474560 | tf_op jit(solution)/shard_map/reduce_scatter | solution.py:119
  275.3 25.2 %collective-permute-start.38 = (bf16[192,192]{1,0:T(8,128)(2,1)S(1)}, bf16[192,192]{1,0:T(8,128)(2,1)S(1)}, u32[]{:S(2)}, u32[]{:S(2)}) collective-permute-start(bf16[192,192]{1,0:T(8,128)(2,1)S(1)} %get-tuple-element.191), channel_id=1, source_target_pairs={{0,1},{1,0},{2,3},{3,2},{4,5},{5,4},{6,7},{7,6},{8,9},{9,8},{10,11... | collective-permute-start | bytes 221192 | tf_op jit(solution)/shard_map/ppermute | solution.py:66
  275.8 24.7 %collective-permute-start.39 = (bf16[192,192]{1,0:T(8,128)(2,1)S(1)}, bf16[192,192]{1,0:T(8,128)(2,1)S(1)}, u32[]{:S(2)}, u32[]{:S(2)}) collective-permute-start(bf16[192,192]{1,0:T(8,128)(2,1)S(1)} %get-tuple-element.192), channel_id=1, source_target_pairs={{0,2},{1,3},{2,0},{3,1},{4,6},{5,7},{6,4},{7,5},{8,10},{9,11},{10,... | collective-permute-start | bytes 221192 | tf_op jit(solution)/shard_map/ppermute | solution.py:66
  277.0 23.5 %collective-permute-start.40 = (bf16[192,192]{1,0:T(8,128)(2,1)S(1)}, bf16[192,192]{1,0:T(8,128)(2,1)S(1)}, u32[]{:S(2)}, u32[]{:S(2)}) collective-permute-start(bf16[192,192]{1,0:T(8,128)(2,1)S(1)} %get-tuple-element.193), channel_id=1, source_target_pairs={{0,3},{1,2},{2,1},{3,0},{4,7},{5,6},{6,5},{7,4},{8,11},{9,10},{10,... | collective-permute-start | bytes 221192 | tf_op jit(solution)/shard_map/ppermute | solution.py:66
  288.1 28.7 %collective-permute-start.43 = (bf16[4,96,1536]{2,1,0:T(8,128)(2,1)S(1)}, bf16[4,96,1536]{2,1,0:T(8,128)(2,1)}, u32[]{:S(2)}, u32[]{:S(2)}) collective-permute-start(bf16[4,96,1536]{2,1,0:T(8,128)(2,1)S(1)} %get-tuple-element.189.refs_22_), channel_id=1, source_target_pairs={{0,4},{4,0},{8,12},{12,8},{16,20},{20,16},{24,28},{28,24},{1,5},{5... | collective-permute-start | bytes 3538952 | tf_op jit(solution)/shard_map/ppermute | solution.py:66
  320.8 12.0 %collective-permute-start.45 = (bf16[2,192,768]{2,1,0:T(8,128)(2,1)S(1)}, bf16[2,192,768]{2,1,0:T(8,128)(2,1)}, u32[]{:S(2)}, u32[]{:S(2)}) collective-permute-start(bf16[2,192,768]{2,1,0:T(8,128)(2,1)S(1)} %get-tuple-element.207), channel_id=1, source_target_pairs={{0,1},{1,0},{2,3},{3,2},{4,5},{5,4},{6,7},{7,6},{8,9},{9,8},{10,11... | collective-permute-start | bytes 1769480 | tf_op jit(solution)/shard_map/ppermute | solution.py:66
  320.8 14.7 %collective-permute-start.41 = (bf16[2,192,768]{2,1,0:T(8,128)(2,1)S(1)}, bf16[2,192,768]{2,1,0:T(8,128)(2,1)}, u32[]{:S(2)}, u32[]{:S(2)}) collective-permute-start(bf16[2,192,768]{2,1,0:T(8,128)(2,1)S(1)} %get-tuple-element.195), channel_id=1, source_target_pairs={{0,1},{1,0},{2,3},{3,2},{4,5},{5,4},{6,7},{7,6},{8,9},{9,8},{10,11... | collective-permute-start | bytes 1769480 | tf_op jit(solution)/shard_map/ppermute | solution.py:66
  329.2 17.2 %collective-permute-start.44 = (bf16[4,96,768]{2,1,0:T(8,128)(2,1)S(1)}, bf16[4,96,768]{2,1,0:T(8,128)(2,1)}, u32[]{:S(2)}, u32[]{:S(2)}) collective-permute-start(bf16[4,96,768]{2,1,0:T(8,128)(2,1)S(1)} %get-tuple-element.204), channel_id=1, source_target_pairs={{0,4},{4,0},{8,12},{12,8},{16,20},{20,16},{24,28},{28,24},{1,5},{5... | collective-permute-start | bytes 1769480 | tf_op jit(solution)/shard_map/ppermute | solution.py:66
  334.2 19.9 %collective-permute-start.46 = (bf16[192,768]{1,0:T(8,128)(2,1)S(1)}, bf16[192,768]{1,0:T(8,128)(2,1)S(1)}, u32[]{:S(2)}, u32[]{:S(2)}) collective-permute-start(bf16[192,768]{1,0:T(8,128)(2,1)S(1)} %fusion.7), channel_id=1, source_target_pairs={{0,2},{1,3},{2,0},{3,1},{4,6},{5,7},{6,4},{7,5},{8,10},{9,11},{10,... | collective-permute-start | bytes 884744 | tf_op jit(solution)/shard_map/ppermute | solution.py:66
  336.5 17.0 %collective-permute-start.42 = (bf16[192,768]{1,0:T(8,128)(2,1)S(1)}, bf16[192,768]{1,0:T(8,128)(2,1)S(1)}, u32[]{:S(2)}, u32[]{:S(2)}) collective-permute-start(bf16[192,768]{1,0:T(8,128)(2,1)S(1)} %fusion.6), channel_id=1, source_target_pairs={{0,2},{1,3},{2,0},{3,1},{4,6},{5,7},{6,4},{7,5},{8,10},{9,11},{10,... | collective-permute-start | bytes 884744 | tf_op jit(solution)/shard_map/ppermute | solution.py:66
  348.0 18.3 %collective-permute-start.50 = (bf16[96,768]{1,0:T(8,128)(2,1)S(1)}, bf16[96,768]{1,0:T(8,128)(2,1)S(1)}, u32[]{:S(2)}, u32[]{:S(2)}) collective-permute-start(bf16[96,768]{1,0:T(8,128)(2,1)S(1)} %get-tuple-element.236.refs_1_), channel_id=1, source_target_pairs={{0,8},{4,12},{8,0},{12,4},{16,24},{20,28},{24,16},{28,20},{1,9},{5... | collective-permute-start | bytes 442376 | tf_op jit(solution)/shard_map/ppermute | solution.py:66
  348.1 18.2 %collective-permute-start.51 = (bf16[96,768]{1,0:T(8,128)(2,1)S(1)}, bf16[96,768]{1,0:T(8,128)(2,1)S(1)}, u32[]{:S(2)}, u32[]{:S(2)}) collective-permute-start(bf16[96,768]{1,0:T(8,128)(2,1)S(1)} %get-tuple-element.235), channel_id=1, source_target_pairs={{0,16},{4,20},{8,24},{12,28},{16,0},{20,4},{24,8},{28,12},{1,17},{... | collective-permute-start | bytes 442376 | tf_op jit(solution)/shard_map/ppermute | solution.py:66
  349.8 16.6 %collective-permute-start.52 = (bf16[96,768]{1,0:T(8,128)(2,1)S(1)}, bf16[96,768]{1,0:T(8,128)(2,1)S(1)}, u32[]{:S(2)}, u32[]{:S(2)}) collective-permute-start(bf16[96,768]{1,0:T(8,128)(2,1)S(1)} %get-tuple-element.234), channel_id=1, source_target_pairs={{0,24},{4,28},{8,16},{12,20},{16,8},{20,12},{24,0},{28,4},{1,25},{... | collective-permute-start | bytes 442376 | tf_op jit(solution)/shard_map/ppermute | solution.py:66
  353.4 5.4 %collective-permute-start.47 = (bf16[4,16,768]{2,1,0:T(8,128)(2,1)S(1)}, bf16[4,16,768]{2,1,0:T(8,128)(2,1)S(1)}, u32[]{:S(2)}, u32[]{:S(2)}) collective-permute-start(bf16[4,16,768]{2,1,0:T(8,128)(2,1)S(1)} %convert_element_type.200), channel_id=1, source_target_pairs={{0,1},{1,0},{2,3},{3,2},{4,5},{5,4},{6,7},{7,6},{8,9},{9,8},{10,11... | collective-permute-start | bytes 294920 | tf_op jit(solution)/shard_map/ppermute | solution.py:66
  358.9 4.7 %collective-permute-start.48 = (bf16[4,16,768]{2,1,0:T(8,128)(2,1)S(1)}, bf16[4,16,768]{2,1,0:T(8,128)(2,1)S(1)}, u32[]{:S(2)}, u32[]{:S(2)}) collective-permute-start(bf16[4,16,768]{2,1,0:T(8,128)(2,1)S(1)} %add_convert_fusion.13), channel_id=1, source_target_pairs={{0,2},{1,3},{2,0},{3,1},{4,6},{5,7},{6,4},{7,5},{8,10},{9,11},{10,... | collective-permute-start | bytes 294920 | tf_op jit(solution)/shard_map/ppermute | solution.py:66
  364.8 7.2 %collective-permute-start.49 = (bf16[4,16,768]{2,1,0:T(8,128)(2,1)S(1)}, bf16[4,16,768]{2,1,0:T(8,128)(2,1)S(1)}, u32[]{:S(2)}, u32[]{:S(2)}) collective-permute-start(bf16[4,16,768]{2,1,0:T(8,128)(2,1)S(1)} %convert_element_type.206), channel_id=1, source_target_pairs={{0,4},{4,0},{8,12},{12,8},{16,20},{20,16},{24,28},{28,24},{1,5},{5... | collective-permute-start | bytes 294920 | tf_op jit(solution)/shard_map/ppermute | solution.py:66
  367.5 3.8 collective-permute-start.54
  373.5 8.4 %collective-permute-start.55 = (bf16[4,16,768]{2,1,0:T(8,128)(2,1)S(1)}, bf16[4,16,768]{2,1,0:T(8,128)(2,1)S(1)}, u32[]{:S(2)}, u32[]{:S(2)}) collective-permute-start(bf16[4,16,768]{2,1,0:T(8,128)(2,1)S(1)} %add_convert_fusion.12), channel_id=1, source_target_pairs={{0,8},{4,12},{8,0},{12,4},{16,24},{20,28},{24,16},{28,20},{1,9},{5... | collective-permute-start | bytes 294920 | tf_op jit(solution)/shard_map/ppermute | solution.py:66
  374.4 7.0 %collective-permute-start.57 = (f32[2,24,128]{2,1,0:T(8,128)S(1)}, f32[2,24,128]{2,1,0:T(8,128)S(1)}, u32[]{:S(2)}, u32[]{:S(2)}) collective-permute-start(f32[2,24,128]{2,1,0:T(8,128)S(1)} %add.265), channel_id=1, source_target_pairs={{0,8},{4,12},{8,0},{12,4},{16,24},{20,28},{24,16},{28,20},{1,9},{5... | collective-permute-start | bytes 73736 | tf_op jit(solution)/shard_map/ppermute | solution.py:66
  377.1 3.7 collective-permute-start.56
  383.5 7.0 %collective-permute-start.58 = (bf16[4,16,768]{2,1,0:T(8,128)(2,1)S(1)}, bf16[4,16,768]{2,1,0:T(8,128)(2,1)S(1)}, u32[]{:S(2)}, u32[]{:S(2)}) collective-permute-start(bf16[4,16,768]{2,1,0:T(8,128)(2,1)S(1)} %add_convert_fusion.11), channel_id=1, source_target_pairs={{0,16},{4,20},{8,24},{12,28},{16,0},{20,4},{24,8},{28,12},{1,17},{... | collective-permute-start | bytes 294920 | tf_op jit(solution)/shard_map/ppermute | solution.py:66
  384.5 5.3 %collective-permute-start.59 = (f32[2,24,128]{2,1,0:T(8,128)S(1)}, f32[2,24,128]{2,1,0:T(8,128)S(1)}, u32[]{:S(2)}, u32[]{:S(2)}) collective-permute-start(f32[2,24,128]{2,1,0:T(8,128)S(1)} %add.267), channel_id=1, source_target_pairs={{0,16},{4,20},{8,24},{12,28},{16,0},{20,4},{24,8},{28,12},{1,17},{... | collective-permute-start | bytes 73736 | tf_op jit(solution)/shard_map/ppermute | solution.py:66
  399.5 3.7 collective-permute-start.62
  406.8 4.5 %collective-permute-start.64 = (f32[8,128]{1,0:T(8,128)S(1)}, f32[8,128]{1,0:T(8,128)S(1)}, u32[]{:S(2)}, u32[]{:S(2)}) collective-permute-start(f32[8,128]{1,0:T(8,128)S(1)} %add.274), channel_id=1, source_target_pairs={{0,16},{4,20},{8,24},{12,28},{16,0},{20,4},{24,8},{28,12},{1,17},{... | collective-permute-start | bytes 12296 | tf_op jit(solution)/shard_map/ppermute | solution.py:66
  (88 other events, 427.6 us)
Sparse Core Ops, SparseCore 0:
  40.7 68.2 all-gather.1
  237.2 26.8 reduce-scatter.5
  267.4 19.6 reduce-scatter.7
  320.2 26.0 reduce-scatter.3
where the time goes:
time: 426 us; the launch traced here: 421 us
  Pallas kernels  196 us (46%)
  waiting for transfers between devices  91.5 us (21%)
  starting transfers between devices  52 us (12%)
  local copies, waits for them, and re-layouts  35.5 us (8%)
  other arithmetic  31 us (7%)
  between operations  15.6 us (4%)
    pallas_call x4, Pallas kernels, run_forward(): pl.pallas_call(functools.partial(forward_kernel, counts, firsts), grid_sp...  56.1 us
    ppermute x62, starting transfers between devices, swap(): return lax.ppermute(values, axis, [(i, i ^ bits) for i in range(size)])  50.1 us
    pallas_call x4, Pallas kernels, run_attention_backward(): pl.pallas_call(functools.partial(attention_backward_kernel, len(pieces),...  47.9 us
    ppermute x62, waiting for transfers between devices, swap(): return lax.ppermute(values, axis, [(i, i ^ bits) for i in range(size)])  44.6 us
    ppermute x3, waiting for transfers between devices, gather_rows(): rows = lax.ppermute(rows, 'dp', [(i, (i + 2) % 8) for i in range(8)])  37.8 us
    pallas_call x4, Pallas kernels, run_mlp_backward(): pl.pallas_call(functools.partial(mlp_backward_kernel, len(pieces), first,...  32.4 us
    unnamed x171, local copies, waits for them, and re-layouts  25 us
    pallas_call x2, Pallas kernels, run_mlp_outer(): pl.pallas_call(functools.partial(mlp_outer_kernel, len(xhats), len(shapes...  19.8 us
  transfers between devices with their start and end apart: 69, of which 22 were waited for; matrix products, arithmetic and copies ran while one was open for 9% of the time, Pallas kernels for 46%

commit v1 on v0

--- a/solution.py
+++ b/solution.py
@@ -81,7 +81,7 @@
 
 def core_sum(keep, send):
     received = swap(send, "seq", 1)
-    return keep, received, (keep + received.astype(F32)).astype(BF16)
+    return keep, received, (keep.astype(F32) + received.astype(F32)).astype(BF16)
 
 
 def gather_rows(rows):
@@ -102,7 +102,7 @@
 
 
 def pair_sum(keep, send, z_place):
-    summed = keep + swap(send, "dp", 1).astype(F32)
+    summed = keep.astype(F32) + swap(send, "dp", 1).astype(F32)
     own = lax.dynamic_index_in_dim(summed, z_place, 0, keepdims=False)
     return own, [
         lax.dynamic_index_in_dim(summed, z_place ^ k, 0, keepdims=False).astype(BF16)
@@ -111,7 +111,8 @@
 
 
 def pair_total(keep, send):
-    return (keep + swap(send, "dp", 1).astype(F32)).astype(BF16).reshape(-1, keep.shape[-1])
+    total = keep.astype(F32) + swap(send, "dp", 1).astype(F32)
+    return total.astype(BF16).reshape(-1, keep.shape[-1])
 
 
 def scatter_along_z(total):
@@ -174,13 +175,16 @@
 def spread_tokens(value, held, keep, send, core_bit, y_here, chunk):
     at_own, at_near = halves(core_bit, chunk)
     held[...] = value
-    keep[pl.ds(y_here, 1)] = held[at_own][None]
+    keep[pl.ds(y_here, 1)] = held[at_own].astype(keep.dtype)[None]
     send[pl.ds(y_here, 1)] = held[at_near].astype(send.dtype)[None]
 
 
 def gelu_and_slope(v):
     magnitude = jnp.abs(v) * 0.7071067811865476
-    t = 1.0 / (1.0 + 0.3275911 * magnitude)
+    bottom = 1.0 + 0.3275911 * magnitude
+    t = pl.reciprocal(bottom, approx=True)
+    t = t * (2.0 - bottom * t)
+    t = t * (2.0 - bottom * t)
     falling = jnp.exp(-0.5 * v * v)
     poly = t * (
         0.254829592
@@ -345,7 +349,7 @@
 
 
 def seq_sum(keep, near, across):
-    return keep[...] + near[...].astype(F32) + across[...].astype(F32)
+    return keep[...].astype(F32) + near[...].astype(F32) + across[...].astype(F32)
 
 
 def finish_stream_kernel(keep, near, across, stream, bias, out, *low):
@@ -370,55 +374,83 @@
     )
 
 
-def mlp_backward_kernel(count, first, sequence, n_before, n_outward, place, *refs):
-    own, near, vec, xhat, slope, att = refs[:6]
-    pieces = refs[6 : 6 + count]
-    before = refs[6 + count : 6 + count + n_before]
-    grad, grad_pre, grad_two, sums = refs[-7 - n_outward : -3 - n_outward]
-    outward, (whole_b, product, sems) = refs[-3 - n_outward : -3], refs[-3:]
+def mlp_backward_kernel(count, first, sequences, n_outs, place, vec, *refs):
+    refs = list(refs)
+
+    def take(number):
+        taken, refs[:] = refs[:number], refs[number:]
+        return taken
+
+    inputs = [take(6) for _ in range(sequences)]
+    pieces = take(count)
+    n_blocks = D // inputs[0][4].shape[1]
+    whole_b, product, sum_up, sum_down, sems = refs[-5:]
+    del refs[: -5 - 4 * sequences - n_blocks - n_outs]
+    outputs = [take(4) for _ in range(sequences)]
+    outward, outs = take(n_blocks), take(n_outs)
     core_bit, y_bit, dp_place = place[0], place[1], place[2]
     step = pl.program_id(0)
     copies = weight_copies(dp_place, [(pieces, first)], [whole_b], sems)
+    quarter = sum_up.shape[1]
 
     @pl.when(step == 0)
     def _():
         start_all(copies)
-        sums[...] = jnp.zeros_like(sums)
-
-    chunk = own.shape[1]
-    place_tokens(grad, own, near, core_bit, step ^ y_bit, chunk)
-
-    @pl.when(step == 0)
+        product[...] = jnp.zeros_like(product)
+        sum_up[...] = jnp.zeros_like(sum_up)
+        sum_down[...] = jnp.zeros_like(sum_down)
+
+    def one_block(s):
+        own, near, xhat, slope, att, hid = inputs[s]
+        grad, grad_pre, grad_two, sums = outputs[s]
+        chunk = own.shape[1]
+        half = step - 2 * s
+        place_tokens(grad, own, near, core_bit, half ^ y_bit, chunk)
+
+        @pl.when(half == 0)
+        def _():
+            sums[...] = jnp.zeros_like(sums)
+            if s == 0:
+                wait_all(copies)
+
+        flag = place[3 + s] > 0
+        scaled = xhat[...].astype(F32)
+        grad_hidden = jnp.dot(grad[...], whole_b[:, quarter:], preferred_element_type=F32)
+        low_pre = (grad_hidden * slope[...].astype(F32)).astype(BF16)
+        grad_pre[...] = low_pre
+        normed = lax.dot_general(
+            low_pre, whole_b[:, :quarter], CONTRACT_LAST, preferred_element_type=F32
+        )
+        grad_two[...] = (normed * vec[2:3]).astype(BF16)
+        kept = jnp.where(flag, grad[...], jnp.zeros_like(grad))
+        kept_pre = jnp.where(flag, low_pre, jnp.zeros_like(low_pre))
+        forward_normed = (scaled * vec[2:3] + vec[3:4]).astype(BF16)
+        product[...] += lax.dot_general(
+            att[...], kept, CONTRACT_FIRST, preferred_element_type=F32
+        )
+        sum_up[...] += lax.dot_general(
+            forward_normed, kept_pre, CONTRACT_FIRST, preferred_element_type=F32
+        )
+        sum_down[...] += lax.dot_general(
+            kept, hid[...], CONTRACT_FIRST, preferred_element_type=F32
+        )
+        add_up(sums, 0, normed * scaled)
+        add_up(sums, 1, normed)
+        add_up(sums, 2, low_pre)
+        add_up(sums, 3, grad[...])
+
+    for s in range(sequences):
+
+        @pl.when(step // 2 == s)
+        def _():
+            one_block(s)
+
+    @pl.when(step == 2 * sequences - 1)
     def _():
-        wait_all(copies)
-
-    quarter = slope.shape[-1]
-    grad_hidden = jnp.dot(grad[...], whole_b[:, quarter:], preferred_element_type=F32)
-    low_pre = (grad_hidden * slope[...].astype(F32)).astype(BF16)
-    grad_pre[...] = low_pre
-    normed = lax.dot_general(
-        low_pre, whole_b[:, :quarter], CONTRACT_LAST, preferred_element_type=F32
-    )
-    grad_two[...] = (normed * vec[2:3]).astype(BF16)
-    add_up(sums, 0, normed * xhat[...].astype(F32))
-    add_up(sums, 1, normed)
-    add_up(sums, 2, low_pre)
-    add_up(sums, 3, grad[...])
-    kept = jnp.where(place[3 + sequence] > 0, grad[...], jnp.zeros_like(grad))
-    part = lax.dot_general(att[...], kept, CONTRACT_FIRST, preferred_element_type=F32)
-
-    @pl.when(step == 0)
-    def _():
-        product[...] = part + before[0][...] if before else part
-
-    @pl.when(step != 0)
-    def _():
-        product[...] += part
-        if len(outward) == 1:
-            outward[0][...] = product[...]
-            return
+        store_rows(sum_up, outs, 0, dp_place % 2)
+        store_rows(sum_down, outs, quarter, dp_place % 2)
         width = outward[0].shape[1]
-        for index in range(len(outward)):
+        for index in range(n_blocks):
 
             @pl.when(2 * y_bit + core_bit == index)
             def _():
@@ -547,7 +579,7 @@
 def store_rows(value, outs, first, x_bit):
     columns = pl.ds(first, value.shape[1])
     if len(outs) == 1:
-        outs[0][:, columns] = value.astype(BF16)
+        outs[0][:, columns] = value[...].astype(BF16)
         return
     keep, send = outs
     rows = keep.shape[1]
@@ -558,34 +590,8 @@
             for z in range(keep.shape[0]):
                 at = rows * (2 * z + bit)
                 to = rows * (2 * z + 1 - bit)
-                keep[z, :, columns] = value[at : at + rows]
+                keep[z, :, columns] = value[at : at + rows].astype(BF16)
                 send[z, :, columns] = value[to : to + rows].astype(BF16)
-
-
-def mlp_outer_kernel(count, n_outs, scalars, vec, *refs):
-    sources, outs = refs[: 4 * count], refs[-n_outs - 4 * count - 1 : -4 * count - 1]
-    held, sems = refs[-4 * count - 1 : -1], refs[-1]
-    copies = fetch(sources, held, sems)
-    x_bit, flags = scalars[0], [scalars[2 + s] for s in range(count)]
-
-    def ready(k):
-        copies[k].wait()
-        return held[k][...]
-
-    def up(s):
-        def pair():
-            xhat, grad_pre = ready(4 * s), ready(4 * s + 1)
-            return (xhat.astype(F32) * vec[2:3] + vec[3:4]).astype(BF16), grad_pre
-
-        return pair
-
-    def down(s):
-        return lambda: (ready(4 * s + 2), ready(4 * s + 3))
-
-    store_rows(outer_sum(flags, [up(s) for s in range(count)]), outs, 0, x_bit)
-    store_rows(
-        outer_sum(flags, [down(s) for s in range(count)]), outs, held[3].shape[1], x_bit
-    )
 
 
 def qkv_outer_kernel(count, n_blocks, n_outs, scalars, vec, *refs):
@@ -811,7 +817,7 @@
             ],
         ),
         out_shape=[
-            pltpu.HBM((2, chunk, D), F32),
+            pltpu.HBM((2, chunk, D), BF16),
             jax.ShapeDtypeStruct((2, chunk, D), BF16),
             *shapes,
         ],
@@ -821,67 +827,70 @@
     )(place, *[array for array, _ in chunks], vec, *far(tables), *blocks_out, *far(pieces), *far(riders))
 
 
-def run_mlp_backward(place, sequence, last, chunks, vec, weight, xhat, slope, att, before, riders=()):
+def run_mlp_backward(place, chunks, vec, weight, saved, split, riders=()):
     pieces, first = weight[1][1]
-    chunk = chunks[0][0].shape[-2]
+    sequences = len(chunks)
+    chunk = chunks[0][0][0].shape[-2]
     block, length = 2 * chunk, 4 * chunk
+    xhat, slope, att, hid = saved[0]
     quarter, out_wide = slope.shape[1], att.shape[1]
-
-    def same(t):
-        return t
-
-    if last:
-        outward = [jax.ShapeDtypeStruct((out_wide, out_wide), BF16)] * (D // out_wide)
-    else:
-        outward = [pltpu.HBM((out_wide, D), F32)]
-    return pl.pallas_call(
-        functools.partial(
-            mlp_backward_kernel, len(pieces), first, sequence, len(before), len(outward)
-        ),
-        grid_spec=pltpu.PrefetchScalarGridSpec(
-            num_scalar_prefetch=1,
-            grid=(2,),
-            in_specs=[
-                *chunk_specs(chunks),
-                whole_spec((8, D)),
-                rows_spec(block, D, same),
-                rows_spec(block, quarter, same),
-                rows_spec(block, out_wide, same),
-                *in_any(len(pieces)),
-                *[whole_spec((out_wide, D))] * len(before),
-                *in_any(len(riders)),
-            ],
-            out_specs=[
-                rows_spec(block, D, same),
-                rows_spec(block, quarter, same),
-                rows_spec(block, D, same),
-                whole_spec((8, D)),
-                *[whole_spec(array.shape) for array in outward],
-            ],
-            scratch_shapes=[
-                pltpu.VMEM((D, 2 * quarter), BF16),
-                pltpu.VMEM((out_wide, D), F32),
-                pltpu.SemaphoreType.DMA((len(pieces),)),
-            ],
-        ),
-        out_shape=[
+    n_blocks = D // out_wide
+
+    def block_of(s):
+        return lambda t: jnp.clip(t - 2 * s, 0, 1)
+
+    def once(spec):
+        return pl.BlockSpec(spec.block_shape, spec.index_map, pipeline_mode=pl.Buffered(1))
+
+    arrays, in_specs = [], []
+    for s in range(sequences):
+        arrays += [array for array, _ in chunks[s]] + far(saved[s])
+        in_specs += [once(spec) for spec in chunk_specs(chunks[s])]
+        in_specs += [rows_spec(block, array.shape[1], block_of(s)) for array in saved[s]]
+    shapes, specs = outer_outputs(split, 2 * quarter)
+    out_shape, out_specs = [], []
+    for s in range(sequences):
+        out_shape += [
             pltpu.HBM((length, D), BF16),
             pltpu.HBM((length, quarter), BF16),
             pltpu.HBM((length, D), BF16),
             pltpu.HBM((8, D), F32),
-            *outward,
-        ],
-        compiler_params=pltpu.CompilerParams(vmem_limit_bytes=VMEM_BYTES),
-        cost_estimate=cost(8),
+        ]
+        out_specs += [
+            rows_spec(block, D, block_of(s)),
+            rows_spec(block, quarter, block_of(s)),
+            rows_spec(block, D, block_of(s)),
+            whole_spec((8, D)),
+        ]
+    out_shape += [jax.ShapeDtypeStruct((out_wide, out_wide), BF16)] * n_blocks + shapes
+    out_specs += [whole_spec((out_wide, out_wide))] * n_blocks + [once(spec) for spec in specs]
+    results = pl.pallas_call(
+        functools.partial(mlp_backward_kernel, len(pieces), first, sequences, len(shapes)),
+        grid_spec=pltpu.PrefetchScalarGridSpec(
+            num_scalar_prefetch=1,
+            grid=(2 * sequences,),
+            in_specs=[
+                whole_spec((8, D)),
+                *in_specs,
+                *in_any(len(pieces) + len(riders)),
+            ],
+            out_specs=out_specs,
+            scratch_shapes=[
+                pltpu.VMEM((D, 2 * quarter), BF16),
+                pltpu.VMEM((out_wide, D), F32),
+                pltpu.VMEM((D, quarter), F32),
+                pltpu.VMEM((D, quarter), F32),
+                pltpu.SemaphoreType.DMA((len(pieces),)),
+            ],
+        ),
+        out_shape=out_shape,
+        compiler_params=pltpu.CompilerParams(vmem_limit_bytes=2 * VMEM_BYTES),
+        cost_estimate=cost(20),
         name="mlp_backward",
-    )(
-        place,
-        *[array for array, _ in chunks],
-        vec,
-        *far([xhat, slope, att, *pieces]),
-        *before,
-        *far(riders),
-    )
+    )(place, vec, *arrays, *far(pieces), *far(riders))
+    each = [results[4 * s : 4 * s + 4] for s in range(sequences)]
+    rest = results[4 * sequences :]
+    return each, rest[:n_blocks], rest[n_blocks:]
 
 
 def run_attention_backward(
@@ -929,7 +938,7 @@
             ],
         ),
         out_shape=[
-            pltpu.HBM((2, chunk, D), F32),
+            pltpu.HBM((2, chunk, D), BF16),
             jax.ShapeDtypeStruct((2, chunk, D), BF16),
             pltpu.HBM((length, wide), BF16),
             pltpu.HBM((8, D), F32),
@@ -950,33 +959,10 @@
 def outer_outputs(split, columns):
     if split:
         shape = (4, D // 8, columns)
-        kinds = [F32, BF16]
+        kinds = [BF16, BF16]
     else:
         shape, kinds = (D, columns), [BF16]
     return [jax.ShapeDtypeStruct(shape, kind) for kind in kinds], [whole_spec(shape)] * len(kinds)
-
-
-def run_mlp_outer(scalars, vec, groups, split, riders=()):
-    xhats, grads, pres, hids = groups
-    arrays = [array for both in zip(xhats, pres, grads, hids) for array in both]
-    shapes, specs = outer_outputs(split, 2 * hids[0].shape[1])
-    return pl.pallas_call(
-        functools.partial(mlp_outer_kernel, len(xhats), len(shapes)),
-        grid_spec=pltpu.PrefetchScalarGridSpec(
-            num_scalar_prefetch=1,
-            grid=(1,),
-            in_specs=[whole_spec((8, D)), *in_any(len(arrays) + len(riders))],
-            out_specs=specs,
-            scratch_shapes=[
-                *[pltpu.VMEM(array.shape, BF16) for array in arrays],
-                pltpu.SemaphoreType.DMA((len(arrays),)),
-            ],
-        ),
-        out_shape=shapes,
-        compiler_params=pltpu.CompilerParams(vmem_limit_bytes=VMEM_BYTES),
-        cost_estimate=cost(10),
-        name="mlp_outer",
-    )(scalars, vec, *far(arrays), *far(riders))
 
 
 def run_qkv_outer(scalars, vec, groups, outward, split, riders=()):
@@ -1309,7 +1295,7 @@
 
     def own_exchange(keep, send):
         near = swap(send, "seq", 1)
-        low = (keep[1] + near[1].astype(F32)).astype(BF16)
+        low = (keep[1].astype(F32) + near[1].astype(F32)).astype(BF16)
         return (keep, near, None), swap(low, "seq", 2)
 
     both_grads = both_halves(cotangent)
@@ -1382,35 +1368,21 @@
             next_grads.append((fresh, None))
             next_chunks.append(((low, None), (swap(low, "seq", 1), None)))
 
-        for s in range(sequences):
-            mlp.append(
-                run_mlp_backward(
-                    place,
-                    s,
-                    s == sequences - 1,
-                    chunks[s],
-                    vectors[i],
-                    weights[i],
-                    xhats[s],
-                    slopes[s],
-                    atts[s],
-                    mlp[s - 1][4:] if s else [],
-                    riders,
-                )
-            )
-            riders = [mlp[s][3]]
-            if open_sum is not None:
-                close_sum(mlp[s][3])
-            if s == 0:
-                riders += later
+        if open_sum is not None:
+            close_sum(riders[0])
+        mlp, outward, both = run_mlp_backward(
+            place,
+            chunks,
+            vectors[i],
+            weights[i],
+            list(zip(xhats, slopes, atts, hids)),
+            split,
+            [*riders, *later],
+        )
         outward = [
-            block if k == 0 else swap(block, "seq", k) for k, block in enumerate(mlp[-1][4:])
+            block if k == 0 else swap(block, "seq", k) for k, block in enumerate(outward)
         ]
-        groups_b = [xhats, [out[0] for out in mlp], [out[1] for out in mlp], hids]
-        both = run_mlp_outer(
-            scalars, vectors[i], groups_b, split, [block_out, *latest] if last else []
-        )
-        riders = [both[-1], *outward]
+        riders = [both[-1], *latest] if last else [both[-1], block_out]
         for s in range(sequences):
             keep, send, grad_joined, sums_t = run_attention_backward(
                 place,
@@ -1438,6 +1410,8 @@
                         finish_grad, s, [grads[s], streams[i][s]], next_chunks, next_grads
                     ),
                 )
+                if s == 0:
+                    riders = riders + outward
         if split and not last:
             total_b = pair_total(*both)
             part_b = scatter_along_z(total_b)

time: 426 us -> 416 us (0.977)
  Pallas kernels: 196 us -> 179 us
  waiting for transfers between devices: 91.5 us -> 99.7 us
    pallas_call x2 -> x0, Pallas kernels: 19.8 us -> none  [run_mlp_outer(): pl.pallas_call(functools.partial(mlp_outer_kernel, len(xhats), len(shapes...]
    ppermute x62, waiting for transfers between devices: 44.6 us -> 56.7 us  [swap(): return lax.ppermute(values, axis, [(i, i ^ bits) for i in range(size)])]
    pallas_call x4 -> x2, Pallas kernels: 32.4 us -> 36 us  [run_mlp_backward(): pl.pallas_call(functools.partial(mlp_backward_kernel, len(pieces), first,...]
    unnamed x171 -> x175, local copies, waits for them, and re-layouts: 25 us -> 24.6 us
  transfers between devices with their start and end apart: 69 -> 69, of which waited for: 22 -> 30; matrix products, arithmetic and copies ran while one was open for 9% -> 10% of each run, Pallas kernels for 46% -> 38%
where the time goes in v1:
time: 416 us; the launch traced here: 411 us
  Pallas kernels  179 us (43%)
  waiting for transfers between devices  99.7 us (24%)
  starting transfers between devices  50.5 us (12%)
  local copies, waits for them, and re-layouts  35.1 us (8%)
  other arithmetic  31.3 us (8%)
  between operations  15.6 us (4%)
    pallas_call x4, Pallas kernels, run_forward(): pl.pallas_call(functools.partial(forward_kernel, counts, firsts), grid_sp...  57.1 us
    ppermute x62, waiting for transfers between devices, swap(): return lax.ppermute(values, axis, [(i, i ^ bits) for i in range(size)])  56.7 us
    ppermute x62, starting transfers between devices, swap(): return lax.ppermute(values, axis, [(i, i ^ bits) for i in range(size)])  48.6 us
    pallas_call x4, Pallas kernels, run_attention_backward(): pl.pallas_call(functools.partial(attention_backward_kernel, len(pieces),...  47.4 us
    ppermute x3, waiting for transfers between devices, gather_rows(): rows = lax.ppermute(rows, 'dp', [(i, (i + 2) % 8) for i in range(8)])  37.8 us
    pallas_call x2, Pallas kernels, run_mlp_backward(): pl.pallas_call(functools.partial(mlp_backward_kernel, len(pieces), first,...  36 us
    unnamed x175, local copies, waits for them, and re-layouts  24.6 us
    pallas_call x4, Pallas kernels, run_finish(): pl.pallas_call(kernel, grid=(2,), in_specs=specs + ([] if bias is None el...  12.2 us
  transfers between devices with their start and end apart: 69, of which 30 were waited for; matrix products, arithmetic and copies ran while one was open for 10% of the time, Pallas kernels for 38%

profile of v1, /device:TPU:0, one launch (start us, length us, event | category | flops | bytes accessed | tf_op | source)
XLA Modules:
  0.0 411.4 jit_solution(3963817102248025580)
XLA Ops:
  7.2 1.6 convert_element_type.209
  9.8 3.0 collective-permute-start.2
  12.8 1.6 collective-permute-start.3
  14.4 1.5 collective-permute-start
  19.1 7.4 %collective-permute-done.3.refs_12_.refs_20_.refs_14_.refs_16_ = bf16[96,2304]{1,0:T(8,128)(2,1)} collective-permute-done((bf16[96,2304]{1,0:T(8,128)(2,1)S(1)}, bf16[96,2304]{1,0:T(8,128)(2,1)}, u32[]{:S(2)}, u32[]{:S(2)}) %collective-permute-start.3) | collective-permute-done | bytes 442400 | tf_op jit(solution)/shard_map/ppermute | solution.py:94
  28.9 10.8 %collective-permute-done.5.refs_14_.refs_22_.refs_1_.refs_16_.refs_18_ = bf16[96,2304]{1,0:T(8,128)(2,1)S(1)} collective-permute-done((bf16[96,2304]{1,0:T(8,128)(2,1)}, bf16[96,2304]{1,0:T(8,128)(2,1)S(1)}, u32[]{:S(2)}, u32[]{:S(2)}) %collective-permute-start.5) | collective-permute-done | bytes 442400 | tf_op jit(solution)/shard_map/ppermute | solution.py:94
  45.0 19.7 %collective-permute-done.7.refs_16_.refs_24_.refs_18_.refs_20_ = bf16[96,2304]{1,0:T(8,128)(2,1)S(1)} collective-permute-done((bf16[96,2304]{1,0:T(8,128)(2,1)S(1)}, bf16[96,2304]{1,0:T(8,128)(2,1)S(1)}, u32[]{:S(2)}, u32[]{:S(2)}) %collective-permute-start.7) | collective-permute-done | bytes 442400 | tf_op jit(solution)/shard_map/ppermute | solution.py:94
  64.9 8.0 %collective-permute-done.8.refs_17_.refs_25_.refs_19_.refs_21_ = bf16[96,2304]{1,0:T(8,128)(2,1)S(1)} collective-permute-done((bf16[96,2304]{1,0:T(8,128)(2,1)S(1)}, bf16[96,2304]{1,0:T(8,128)(2,1)S(1)}, u32[]{:S(2)}, u32[]{:S(2)}) %collective-permute-start.8) | collective-permute-done | bytes 442400 | tf_op jit(solution)/shard_map/ppermute | solution.py:66
  73.2 1.6 collective-permute-start.10
  75.0 1.4 pad_maximum_fusion.1.refs_0_.refs_6_.grad
  76.9 1.9 collective-permute-done.10.refs_8_.refs_7_
  80.0 14.1 %layer_forward.4 = (bf16[2,192,768]{2,1,0:T(8,128)(2,1)}, bf16[2,192,768]{2,1,0:T(8,128)(2,1)S(1)}, bf16[768,768]{1,0:T(8,128)(2,1)}, bf16[768,384]{1,0:T(8,128)...) custom-call(s32[5]{0:T(128)S(1)} %pad_add_fusion.place, ...), custom_call_target="tpu_custom_call" | custom-call | flops 12999999488 | bytes 13000000 | tf_op jit(solution)/shard_map/layer_forward/pallas_call | solution.py:796
  95.0 1.6 collective-permute-done.12.near
  96.6 1.4 add_convert_fusion.6.refs_26_
  98.1 1.6 collective-permute-start.13
  99.7 14.4 %layer_forward.5 = (bf16[2,192,768]{2,1,0:T(8,128)(2,1)}, bf16[2,192,768]{2,1,0:T(8,128)(2,1)S(1)}, bf16[768,768]{1,0:T(8,128)(2,1)}, bf16[768,384]{1,0:T(8,128)...) custom-call(s32[5]{0:T(128)S(1)} %pad_add_fusion.place, ...), custom_call_target="tpu_custom_call" | custom-call | flops 12999999488 | bytes 13000000 | tf_op jit(solution)/shard_map/layer_forward/pallas_call | solution.py:796
  117.3 2.7 finish_stream.2
  125.7 2.0 collective-permute-done.18.refs_8_.refs_7_
  128.1 14.4 %layer_forward.6 = (bf16[2,192,768]{2,1,0:T(8,128)(2,1)}, bf16[2,192,768]{2,1,0:T(8,128)(2,1)S(1)}, bf16[768,768]{1,0:T(8,128)(2,1)}, bf16[768,384]{1,0:T(8,128)...) custom-call(s32[5]{0:T(128)S(1)} %pad_add_fusion.place, ...), custom_call_target="tpu_custom_call" | custom-call | flops 12999999488 | bytes 13000000 | tf_op jit(solution)/shard_map/layer_forward/pallas_call | solution.py:796
  143.4 2.8 finish_stream.3
  146.2 1.5 collective-permute-start.24
  147.8 1.5 collective-permute-done.24.refs_1_
  149.3 14.2 %layer_forward.7 = (bf16[2,192,768]{2,1,0:T(8,128)(2,1)}, bf16[2,192,768]{2,1,0:T(8,128)(2,1)S(1)}, bf16[768,768]{1,0:T(8,128)(2,1)}, bf16[768,384]{1,0:T(8,128)...) custom-call(s32[5]{0:T(128)S(1)} %pad_add_fusion.place, ...), custom_call_target="tpu_custom_call" | custom-call | flops 12999999488 | bytes 13000000 | tf_op jit(solution)/shard_map/layer_forward/pallas_call | solution.py:796
  167.6 18.4 %mlp_backward.2 = (bf16[768,768]{1,0:T(8,128)(2,1)}, bf16[768,768]{1,0:T(8,128)(2,1)}, bf16[768,768]{1,0:T(8,128)(2,1)}, f32[8,768]{1,0:T(8,128)}, bf16[768,768]...) custom-call(s32[5]{0:T(128)S(1)} %pad_add_fusion.place, ...), custom_call_target="tpu_custom_call" | custom-call | flops 20000000000 | bytes 20000000 | tf_op jit(solution)/shard_map/mlp_backward/pallas_call | solution.py:867
  186.9 2.9 block_out.1.refs_16_
  189.8 11.7 %attention_backward.4 = (bf16[2,192,768]{2,1,0:T(8,128)(2,1)}, bf16[2,192,768]{2,1,0:T(8,128)(2,1)S(1)}, bf16[768,576]{1,0:T(8,128)(2,1)}, f32[8,768]{1,0:T(8,128)}) custom-call(s32[5]{0:T(128)S(1)} %pad_add_fusion.place, bf16[768,768]{1,0:T(8,128)(2,1)} %get-tuple-element.137.refs_0_, f32[8,768]{1,0:T(8,128)S(1)} %stack.79.refs_2_.vec.refs_1_, ...), custom_call_target="tpu_custom_call" | custom-call | flops 11000000512 | bytes 11000000 | tf_op jit(solution)/shard_map/attention_backward/pallas_call | solution.py:909
  203.7 1.4 add_convert_fusion.4.refs_15_
  209.2 11.9 %attention_backward.5 = (bf16[2,192,768]{2,1,0:T(8,128)(2,1)}, bf16[2,192,768]{2,1,0:T(8,128)(2,1)S(1)}, bf16[768,576]{1,0:T(8,128)(2,1)}, f32[8,768]{1,0:T(8,128)}) custom-call(s32[5]{0:T(128)S(1)} %pad_add_fusion.place, bf16[768,768]{1,0:T(8,128)(2,1)} %get-tuple-element.145.refs_0_, f32[8,768]{1,0:T(8,128)S(1)} %stack.79.refs_2_.vec.refs_1_, ...), custom_call_target="tpu_custom_call" | custom-call | flops 11000000512 | bytes 11000000 | tf_op jit(solution)/shard_map/attention_backward/pallas_call | solution.py:909
  223.4 6.8 %collective-permute-done.36 = bf16[4,96,1536]{2,1,0:T(8,128)(2,1)} collective-permute-done((bf16[4,96,1536]{2,1,0:T(8,128)(2,1)S(1)}, bf16[4,96,1536]{2,1,0:T(8,128)(2,1)}, u32[]{:S(2)}, u32[]{:S(2)}) %collective-permute-start.36) | collective-permute-done | bytes 1179680 | tf_op jit(solution)/shard_map/ppermute | solution.py:66
  230.1 2.6 add_convert_fusion.1
  235.4 4.9 %qkv_outer.2 = (bf16[4,96,768]{2,1,0:T(8,128)(2,1)S(1)}, bf16[4,96,768]{2,1,0:T(8,128)(2,1)S(1)}) custom-call(s32[4]{0:T(128)S(1)} %pad_add_fusion.1.scalars, f32[8,768]{1,0:T(8,128)S(1)} %stack.79.refs_2_.vec.refs_1_, bf16[768,768]{1,0:T(8,128)(2,1)} %get-tuple-element.125.refs_1_.refs_2_.refs_9_.refs_0_, bf16[768,576]{1,0:T(8,128)(2,1)} %get-tuple-element.161.refs_1_, ...), custom_call_target="tpu_custom_call" | custom-call | flops 6000000000 | bytes 6000000 | tf_op jit(solution)/shard_map/qkv_outer/pallas_call | solution.py:972
  241.6 3.4 finish_grad.2
  245.0 3.9 collective-permute-done.34.refs_0_
  249.8 3.3 finish_grad.3
  253.1 3.0 collective-permute-done.37
  256.1 2.1 add_convert_fusion.2
  260.1 17.6 %mlp_backward.3 = (bf16[768,768]{1,0:T(8,128)(2,1)}, bf16[768,768]{1,0:T(8,128)(2,1)}, bf16[768,768]{1,0:T(8,128)(2,1)}, f32[8,768]{1,0:T(8,128)}, bf16[768,768]...) custom-call(s32[5]{0:T(128)S(1)} %pad_add_fusion.place, ...), custom_call_target="tpu_custom_call" | custom-call | flops 20000000000 | bytes 20000000 | tf_op jit(solution)/shard_map/mlp_backward/pallas_call | solution.py:867
  278.7 11.8 %attention_backward.6 = (bf16[2,192,768]{2,1,0:T(8,128)(2,1)}, bf16[2,192,768]{2,1,0:T(8,128)(2,1)S(1)}, bf16[768,576]{1,0:T(8,128)(2,1)}, f32[8,768]{1,0:T(8,128)}) custom-call(s32[5]{0:T(128)S(1)} %pad_add_fusion.place, bf16[768,768]{1,0:T(8,128)(2,1)} %get-tuple-element.168.refs_0_, f32[8,768]{1,0:T(8,128)S(1)} %stack.74.refs_2_.vec.refs_1_, ...), custom_call_target="tpu_custom_call" | custom-call | flops 11000000512 | bytes 11000000 | tf_op jit(solution)/shard_map/attention_backward/pallas_call | solution.py:909
  290.6 11.9 %attention_backward.7 = (bf16[2,192,768]{2,1,0:T(8,128)(2,1)}, bf16[2,192,768]{2,1,0:T(8,128)(2,1)S(1)}, bf16[768,576]{1,0:T(8,128)(2,1)}, f32[8,768]{1,0:T(8,128)}) custom-call(s32[5]{0:T(128)S(1)} %pad_add_fusion.place, bf16[768,768]{1,0:T(8,128)(2,1)} %get-tuple-element.178.refs_0_, f32[8,768]{1,0:T(8,128)S(1)} %stack.74.refs_2_.vec.refs_1_, ...), custom_call_target="tpu_custom_call" | custom-call | flops 11000000512 | bytes 11000000 | tf_op jit(solution)/shard_map/attention_backward/pallas_call | solution.py:909
  302.5 2.0 collective-permute-done.43
  304.5 2.9 add_convert_fusion
  310.7 1.6 examples.1.refs_0_
  312.3 1.9 collective-permute-done.41.refs_6_
  314.9 5.2 %qkv_outer.3 = (bf16[4,96,768]{2,1,0:T(8,128)(2,1)S(1)}, bf16[4,96,768]{2,1,0:T(8,128)(2,1)S(1)}) custom-call(s32[4]{0:T(128)S(1)} %pad_add_fusion.1.scalars, f32[8,768]{1,0:T(8,128)S(1)} %stack.74.refs_2_.vec.refs_1_, bf16[768,768]{1,0:T(8,128)(2,1)} %get-tuple-element.119.refs_1_.refs_2_.refs_9_.refs_0_, bf16[768,576]{1,0:T(8,128)(2,1)} %get-tuple-element.177.refs_1_, ...), custom_call_target="tpu_custom_call" | custom-call | flops 6000000000 | bytes 6000000 | tf_op jit(solution)/shard_map/qkv_outer/pallas_call | solution.py:972
  328.5 5.1 %reduce-scatter.4.cloned.1.call-done.refs_1_.refs_0_ = bf16[96,1536]{1,0:T(8,128)(2,1)} async-done(((bf16[384,1536]{1,0:T(8,128)(2,1)}), bf16[96,1536]{1,0:T(8,128)(2,1)}) %reduce-scatter.4.cloned.1.call-update) | async-done | bytes 294928 | tf_op jit(solution)/shard_map/reduce_scatter | solution.py:120
  333.6 3.6 collective-permute-done.44
  339.6 3.5 collective-permute-start.52
  345.5 3.9 input_grad.1.refs_10_
  351.6 2.6 collective-permute-done.48
  356.8 1.7 collective-permute-start.54
  363.7 2.0 collective-permute-start.57
  367.8 2.3 collective-permute-done.56.refs_1_
  373.7 2.9 collective-permute-start.59
  377.3 2.3 collective-permute-done.59.refs_1_
  381.6 1.5 copy-done.34
  383.1 1.4 squares.1
  386.9 1.6 convert_add_fusion.1.totals
  389.2 1.7 collective-permute-start.62
  390.9 2.3 small_vectors.1
  393.3 1.5 slice_reduce_fusion
  394.8 2.1 collective-permute-done.63
  396.9 1.8 collective-permute-start.64
  398.7 2.7 collective-permute-done.64
  402.1 2.2 update.1
  (399 shorter events, 85.4 us)
Async XLA Ops:
  7.2 113.0 %all-gather.2.cloned.1.call-start = ((), (), s32[]{:S(2)}) async-start(), calls=%async_computation.3 | async-start | bytes 3981312 | tf_op jit(solution)/shard_map/all_gather | solution.py:1252
  9.8 17.1 %collective-permute-start.2 = (bf16[96,2304]{1,0:T(8,128)(2,1)S(1)}, bf16[96,2304]{1,0:T(8,128)(2,1)}, u32[]{:S(2)}, u32[]{:S(2)}) collective-permute-start(bf16[96,2304]{1,0:T(8,128)(2,1)S(1)} %concatenate.23.refs_10_.refs_18_.refs_12_.refs_14_), channel_id=1, source_target_pairs={{0,4},{4,0},{8,12},{12,8},{16,20},{20,16},{24,28},{28,24},{1,5},{5... | collective-permute-start | bytes 1327112 | tf_op jit(solution)/shard_map/ppermute | solution.py:66
  12.8 13.6 %collective-permute-start.3 = (bf16[96,2304]{1,0:T(8,128)(2,1)S(1)}, bf16[96,2304]{1,0:T(8,128)(2,1)}, u32[]{:S(2)}, u32[]{:S(2)}) collective-permute-start(bf16[96,2304]{1,0:T(8,128)(2,1)S(1)} %concatenate.23.refs_10_.refs_18_.refs_12_.refs_14_), channel_id=1, source_target_pairs={{0,8},{4,12},{8,16},{12,20},{16,24},{20,28},{24,0},{28,4},{1,9},{5... | collective-permute-start | bytes 1327112 | tf_op jit(solution)/shard_map/ppermute | solution.py:94
  14.4 26.2 %collective-permute-start = (bf16[2,192,768]{2,1,0:T(8,128)(2,1)S(1)}, bf16[2,192,768]{2,1,0:T(8,128)(2,1)S(1)}, u32[]{:S(2)}, u32[]{:S(2)}) collective-permute-start(bf16[2,192,768]{2,1,0:T(8,128)(2,1)S(1)} %copy-done.42), channel_id=1, source_target_pairs={{0,2},{1,3},{2,0},{3,1},{4,6},{5,7},{6,4},{7,5},{8,10},{9,11},{10,... | collective-permute-start | bytes 1769480 | tf_op jit(solution)/shard_map/ppermute | solution.py:66
  15.9 59.1 %collective-permute-start.14 = (bf16[2,192,768]{2,1,0:T(8,128)(2,1)}, bf16[2,192,768]{2,1,0:T(8,128)(2,1)}, u32[]{:S(2)}, u32[]{:S(2)}) collective-permute-start(bf16[2,192,768]{2,1,0:T(8,128)(2,1)} %param.12), channel_id=1, source_target_pairs={{0,2},{1,3},{2,0},{3,1},{4,6},{5,7},{6,4},{7,5},{8,10},{9,11},{10,... | collective-permute-start | bytes 1769480 | tf_op jit(solution)/shard_map/ppermute | solution.py:66
  26.4 17.5 %collective-permute-start.4 = (bf16[96,2304]{1,0:T(8,128)(2,1)}, bf16[96,2304]{1,0:T(8,128)(2,1)}, u32[]{:S(2)}, u32[]{:S(2)}) collective-permute-start(bf16[96,2304]{1,0:T(8,128)(2,1)} %collective-permute-done.3.refs_12_.refs_20_.refs_14_.refs_16_), channel_id=1, source_target_pairs={{0,4},{4,0},{8,12},{12,8},{16,20},{20,16},{24,28},{28,24},{1,5},{5... | collective-permute-start | bytes 1327112 | tf_op jit(solution)/shard_map/ppermute | solution.py:66
  27.0 12.8 %collective-permute-start.5 = (bf16[96,2304]{1,0:T(8,128)(2,1)}, bf16[96,2304]{1,0:T(8,128)(2,1)S(1)}, u32[]{:S(2)}, u32[]{:S(2)}) collective-permute-start(bf16[96,2304]{1,0:T(8,128)(2,1)} %collective-permute-done.3.refs_12_.refs_20_.refs_14_.refs_16_), channel_id=1, source_target_pairs={{0,8},{4,12},{8,16},{12,20},{16,24},{20,28},{24,0},{28,4},{1,9},{5... | collective-permute-start | bytes 1327112 | tf_op jit(solution)/shard_map/ppermute | solution.py:94
  40.5 280.8 %reduce-scatter.6.cloned.1.call-start = ((), (), s32[]{:S(2)}) async-start(), calls=%async_computation.5 | async-start | bytes 1474560 | tf_op jit(solution)/shard_map/reduce_scatter | solution.py:120
  41.8 35.1 %collective-permute-start.1 = (bf16[2,2,192,768]{3,2,1,0:T(8,128)(2,1)S(1)}, bf16[2,2,192,768]{3,2,1,0:T(8,128)(2,1)S(1)}, u32[]{:S(2)}, u32[]{:S(2)}) collective-permute-start(bf16[2,2,192,768]{3,2,1,0:T(8,128)(2,1)S(1)} %fusion.3.refs_0_), channel_id=1, source_target_pairs={{0,1},{1,0},{2,3},{3,2},{4,5},{5,4},{6,7},{7,6},{8,9},{9,8},{10,11... | collective-permute-start | bytes 3538952 | tf_op jit(solution)/shard_map/ppermute | solution.py:66
  42.4 22.3 %collective-permute-start.6 = (bf16[96,2304]{1,0:T(8,128)(2,1)S(1)}, bf16[96,2304]{1,0:T(8,128)(2,1)S(1)}, u32[]{:S(2)}, u32[]{:S(2)}) collective-permute-start(bf16[96,2304]{1,0:T(8,128)(2,1)S(1)} %copy-done.66), channel_id=1, source_target_pairs={{0,4},{4,0},{8,12},{12,8},{16,20},{20,16},{24,28},{28,24},{1,5},{5... | collective-permute-start | bytes 1327112 | tf_op jit(solution)/shard_map/ppermute | solution.py:66
  43.7 20.9 %collective-permute-start.7 = (bf16[96,2304]{1,0:T(8,128)(2,1)S(1)}, bf16[96,2304]{1,0:T(8,128)(2,1)S(1)}, u32[]{:S(2)}, u32[]{:S(2)}) collective-permute-start(bf16[96,2304]{1,0:T(8,128)(2,1)S(1)} %copy-done.66), channel_id=1, source_target_pairs={{0,8},{4,12},{8,16},{12,20},{16,24},{20,28},{24,0},{28,4},{1,9},{5... | collective-permute-start | bytes 1327112 | tf_op jit(solution)/shard_map/ppermute | solution.py:94
  64.6 8.3 %collective-permute-start.8 = (bf16[96,2304]{1,0:T(8,128)(2,1)S(1)}, bf16[96,2304]{1,0:T(8,128)(2,1)S(1)}, u32[]{:S(2)}, u32[]{:S(2)}) collective-permute-start(bf16[96,2304]{1,0:T(8,128)(2,1)S(1)} %collective-permute-done.7.refs_16_.refs_24_.refs_18_.refs_20_), channel_id=1, source_target_pairs={{0,4},{4,0},{8,12},{12,8},{16,20},{20,16},{24,28},{28,24},{1,5},{5... | collective-permute-start | bytes 1327112 | tf_op jit(solution)/shard_map/ppermute | solution.py:66
  73.1 3.8 collective-permute-start.9
  73.2 5.7 %collective-permute-start.10 = (bf16[192,192]{1,0:T(8,128)(2,1)S(1)}, bf16[192,192]{1,0:T(8,128)(2,1)S(1)}, u32[]{:S(2)}, u32[]{:S(2)}) collective-permute-start(bf16[192,192]{1,0:T(8,128)(2,1)S(1)} %get-tuple-element.234), channel_id=1, source_target_pairs={{0,2},{1,3},{2,0},{3,1},{4,6},{5,7},{6,4},{7,5},{8,10},{9,11},{10,... | collective-permute-start | bytes 221192 | tf_op jit(solution)/shard_map/ppermute | solution.py:66
  74.8 5.2 %collective-permute-start.11 = (bf16[192,192]{1,0:T(8,128)(2,1)S(1)}, bf16[192,192]{1,0:T(8,128)(2,1)S(1)}, u32[]{:S(2)}, u32[]{:S(2)}) collective-permute-start(bf16[192,192]{1,0:T(8,128)(2,1)S(1)} %get-tuple-element.233), channel_id=1, source_target_pairs={{0,3},{1,2},{2,1},{3,0},{4,7},{5,6},{6,5},{7,4},{8,11},{9,10},{10,... | collective-permute-start | bytes 221192 | tf_op jit(solution)/shard_map/ppermute | solution.py:66
  76.5 23.2 %collective-permute-start.15 = (bf16[2,2,192,768]{3,2,1,0:T(8,128)(2,1)S(1)}, bf16[2,2,192,768]{3,2,1,0:T(8,128)(2,1)}, u32[]{:S(2)}, u32[]{:S(2)}) collective-permute-start(bf16[2,2,192,768]{3,2,1,0:T(8,128)(2,1)S(1)} %pad_maximum_fusion.1.refs_0_.refs_6_.grad), channel_id=1, source_target_pairs={{0,1},{1,0},{2,3},{3,2},{4,5},{5,4},{6,7},{7,6},{8,9},{9,8},{10,11... | collective-permute-start | bytes 3538952 | tf_op jit(solution)/shard_map/ppermute | solution.py:66
  98.1 16.9 %collective-permute-start.13 = (bf16[2,192,768]{2,1,0:T(8,128)(2,1)S(1)}, bf16[2,192,768]{2,1,0:T(8,128)(2,1)}, u32[]{:S(2)}, u32[]{:S(2)}) collective-permute-start(bf16[2,192,768]{2,1,0:T(8,128)(2,1)S(1)} %add_convert_fusion.6.refs_26_), channel_id=1, source_target_pairs={{0,2},{1,3},{2,0},{3,1},{4,6},{5,7},{6,4},{7,5},{8,10},{9,11},{10,... | collective-permute-start | bytes 1769480 | tf_op jit(solution)/shard_map/ppermute | solution.py:66
  115.0 8.5 %collective-permute-start.20 = (bf16[2,192,768]{2,1,0:T(8,128)(2,1)}, bf16[2,192,768]{2,1,0:T(8,128)(2,1)}, u32[]{:S(2)}, u32[]{:S(2)}) collective-permute-start(bf16[2,192,768]{2,1,0:T(8,128)(2,1)} %after.25), channel_id=1, source_target_pairs={{0,1},{1,0},{2,3},{3,2},{4,5},{5,4},{6,7},{7,6},{8,9},{9,8},{10,11... | collective-permute-start | bytes 1769480 | tf_op jit(solution)/shard_map/ppermute | solution.py:66
  120.0 5.7 %collective-permute-start.16 = (bf16[2,192,768]{2,1,0:T(8,128)(2,1)S(1)}, bf16[2,192,768]{2,1,0:T(8,128)(2,1)S(1)}, u32[]{:S(2)}, u32[]{:S(2)}) collective-permute-start(bf16[2,192,768]{2,1,0:T(8,128)(2,1)S(1)} %get-tuple-element.118.refs_0_), channel_id=1, source_target_pairs={{0,1},{1,0},{2,3},{3,2},{4,5},{5,4},{6,7},{7,6},{8,9},{9,8},{10,11... | collective-permute-start | bytes 1769480 | tf_op jit(solution)/shard_map/ppermute | solution.py:66
  121.5 4.2 %collective-permute-start.17 = (bf16[192,192]{1,0:T(8,128)(2,1)S(1)}, bf16[192,192]{1,0:T(8,128)(2,1)S(1)}, u32[]{:S(2)}, u32[]{:S(2)}) collective-permute-start(bf16[192,192]{1,0:T(8,128)(2,1)S(1)} %get-tuple-element.231), channel_id=1, source_target_pairs={{0,1},{1,0},{2,3},{3,2},{4,5},{5,4},{6,7},{7,6},{8,9},{9,8},{10,11... | collective-permute-start | bytes 221192 | tf_op jit(solution)/shard_map/ppermute | solution.py:66
  122.1 5.7 %collective-permute-start.18 = (bf16[192,192]{1,0:T(8,128)(2,1)S(1)}, bf16[192,192]{1,0:T(8,128)(2,1)S(1)}, u32[]{:S(2)}, u32[]{:S(2)}) collective-permute-start(bf16[192,192]{1,0:T(8,128)(2,1)S(1)} %get-tuple-element.230), channel_id=1, source_target_pairs={{0,2},{1,3},{2,0},{3,1},{4,6},{5,7},{6,4},{7,5},{8,10},{9,11},{10,... | collective-permute-start | bytes 221192 | tf_op jit(solution)/shard_map/ppermute | solution.py:66
  122.8 5.3 %collective-permute-start.19 = (bf16[192,192]{1,0:T(8,128)(2,1)S(1)}, bf16[192,192]{1,0:T(8,128)(2,1)S(1)}, u32[]{:S(2)}, u32[]{:S(2)}) collective-permute-start(bf16[192,192]{1,0:T(8,128)(2,1)S(1)} %get-tuple-element.229), channel_id=1, source_target_pairs={{0,3},{1,2},{2,1},{3,0},{4,7},{5,6},{6,5},{7,4},{8,11},{9,10},{10,... | collective-permute-start | bytes 221192 | tf_op jit(solution)/shard_map/ppermute | solution.py:66
  124.7 18.7 %collective-permute-start.21 = (bf16[2,192,768]{2,1,0:T(8,128)(2,1)S(1)}, bf16[2,192,768]{2,1,0:T(8,128)(2,1)}, u32[]{:S(2)}, u32[]{:S(2)}) collective-permute-start(bf16[2,192,768]{2,1,0:T(8,128)(2,1)S(1)} %add_convert_fusion.5.refs_12_), channel_id=1, source_target_pairs={{0,2},{1,3},{2,0},{3,1},{4,6},{5,7},{6,4},{7,5},{8,10},{9,11},{10,... | collective-permute-start | bytes 1769480 | tf_op jit(solution)/shard_map/ppermute | solution.py:66
  146.2 3.1 collective-permute-start.24
  147.7 16.2 %collective-permute-start.22 = (bf16[2,192,768]{2,1,0:T(8,128)(2,1)S(1)}, bf16[2,192,768]{2,1,0:T(8,128)(2,1)S(1)}, u32[]{:S(2)}, u32[]{:S(2)}) collective-permute-start(bf16[2,192,768]{2,1,0:T(8,128)(2,1)S(1)} %copy-done.11), channel_id=1, source_target_pairs={{0,1},{1,0},{2,3},{3,2},{4,5},{5,4},{6,7},{7,6},{8,9},{9,8},{10,11... | collective-permute-start | bytes 1769480 | tf_op jit(solution)/shard_map/ppermute | solution.py:66
  164.0 22.0 %collective-permute-start.23 = (bf16[192,768]{1,0:T(8,128)(2,1)S(1)}, bf16[192,768]{1,0:T(8,128)(2,1)S(1)}, u32[]{:S(2)}, u32[]{:S(2)}) collective-permute-start(bf16[192,768]{1,0:T(8,128)(2,1)S(1)} %fusion.4), channel_id=1, source_target_pairs={{0,2},{1,3},{2,0},{3,1},{4,6},{5,7},{6,4},{7,5},{8,10},{9,11},{10,... | collective-permute-start | bytes 884744 | tf_op jit(solution)/shard_map/ppermute | solution.py:66
  166.8 19.3 %collective-permute-start.26 = (bf16[192,768]{1,0:T(8,128)(2,1)S(1)}, bf16[192,768]{1,0:T(8,128)(2,1)S(1)}, u32[]{:S(2)}, u32[]{:S(2)}) collective-permute-start(bf16[192,768]{1,0:T(8,128)(2,1)S(1)} %fusion.5), channel_id=1, source_target_pairs={{0,2},{1,3},{2,0},{3,1},{4,6},{5,7},{6,4},{7,5},{8,10},{9,11},{10,... | collective-permute-start | bytes 884744 | tf_op jit(solution)/shard_map/ppermute | solution.py:66
  201.7 28.4 %collective-permute-start.36 = (bf16[4,96,1536]{2,1,0:T(8,128)(2,1)S(1)}, bf16[4,96,1536]{2,1,0:T(8,128)(2,1)}, u32[]{:S(2)}, u32[]{:S(2)}) collective-permute-start(bf16[4,96,1536]{2,1,0:T(8,128)(2,1)S(1)} %copy-done.16), channel_id=1, source_target_pairs={{0,4},{4,0},{8,12},{12,8},{16,20},{20,16},{24,28},{28,24},{1,5},{5... | collective-permute-start | bytes 3538952 | tf_op jit(solution)/shard_map/ppermute | solution.py:66
  201.8 4.7 %collective-permute-start.29 = (bf16[192,192]{1,0:T(8,128)(2,1)S(1)}, bf16[192,192]{1,0:T(8,128)(2,1)S(1)}, u32[]{:S(2)}, u32[]{:S(2)}) collective-permute-start(bf16[192,192]{1,0:T(8,128)(2,1)S(1)} %get-tuple-element.151), channel_id=1, source_target_pairs={{0,1},{1,0},{2,3},{3,2},{4,5},{5,4},{6,7},{7,6},{8,9},{9,8},{10,11... | collective-permute-start | bytes 221192 | tf_op jit(solution)/shard_map/ppermute | solution.py:66
  202.1 5.5 %collective-permute-start.30 = (bf16[192,192]{1,0:T(8,128)(2,1)S(1)}, bf16[192,192]{1,0:T(8,128)(2,1)S(1)}, u32[]{:S(2)}, u32[]{:S(2)}) collective-permute-start(bf16[192,192]{1,0:T(8,128)(2,1)S(1)} %get-tuple-element.152), channel_id=1, source_target_pairs={{0,2},{1,3},{2,0},{3,1},{4,6},{5,7},{6,4},{7,5},{8,10},{9,11},{10,... | collective-permute-start | bytes 221192 | tf_op jit(solution)/shard_map/ppermute | solution.py:66
  203.4 5.2 %collective-permute-start.31 = (bf16[192,192]{1,0:T(8,128)(2,1)S(1)}, bf16[192,192]{1,0:T(8,128)(2,1)S(1)}, u32[]{:S(2)}, u32[]{:S(2)}) collective-permute-start(bf16[192,192]{1,0:T(8,128)(2,1)S(1)} %get-tuple-element.153), channel_id=1, source_target_pairs={{0,3},{1,2},{2,1},{3,0},{4,7},{5,6},{6,5},{7,4},{8,11},{9,10},{10,... | collective-permute-start | bytes 221192 | tf_op jit(solution)/shard_map/ppermute | solution.py:66
  205.1 16.9 %collective-permute-start.28 = (bf16[2,192,768]{2,1,0:T(8,128)(2,1)S(1)}, bf16[2,192,768]{2,1,0:T(8,128)(2,1)}, u32[]{:S(2)}, u32[]{:S(2)}) collective-permute-start(bf16[2,192,768]{2,1,0:T(8,128)(2,1)S(1)} %add_convert_fusion.4.refs_15_), channel_id=1, source_target_pairs={{0,2},{1,3},{2,0},{3,1},{4,6},{5,7},{6,4},{7,5},{8,10},{9,11},{10,... | collective-permute-start | bytes 1769480 | tf_op jit(solution)/shard_map/ppermute | solution.py:66
  222.0 10.9 %collective-permute-start.33 = (bf16[2,192,768]{2,1,0:T(8,128)(2,1)}, bf16[2,192,768]{2,1,0:T(8,128)(2,1)S(1)}, u32[]{:S(2)}, u32[]{:S(2)}) collective-permute-start(bf16[2,192,768]{2,1,0:T(8,128)(2,1)} %after.29), channel_id=1, source_target_pairs={{0,1},{1,0},{2,3},{3,2},{4,5},{5,4},{6,7},{7,6},{8,9},{9,8},{10,11... | collective-permute-start | bytes 1769480 | tf_op jit(solution)/shard_map/ppermute | solution.py:66
  232.8 88.6 %reduce-scatter.8.cloned.1.call-start = ((), (), s32[]{:S(2)}) async-start(), calls=%async_computation.6 | async-start | bytes 737280 | tf_op jit(solution)/shard_map/reduce_scatter | solution.py:120
  234.0 14.9 %collective-permute-start.34 = (bf16[2,192,768]{2,1,0:T(8,128)(2,1)S(1)}, bf16[2,192,768]{2,1,0:T(8,128)(2,1)S(1)}, u32[]{:S(2)}, u32[]{:S(2)}) collective-permute-start(bf16[2,192,768]{2,1,0:T(8,128)(2,1)S(1)} %add_convert_fusion.3.refs_8_), channel_id=1, source_target_pairs={{0,2},{1,3},{2,0},{3,1},{4,6},{5,7},{6,4},{7,5},{8,10},{9,11},{10,... | collective-permute-start | bytes 1769480 | tf_op jit(solution)/shard_map/ppermute | solution.py:66
  241.2 14.9 %collective-permute-start.37 = (bf16[4,96,768]{2,1,0:T(8,128)(2,1)S(1)}, bf16[4,96,768]{2,1,0:T(8,128)(2,1)}, u32[]{:S(2)}, u32[]{:S(2)}) collective-permute-start(bf16[4,96,768]{2,1,0:T(8,128)(2,1)S(1)} %get-tuple-element.174), channel_id=1, source_target_pairs={{0,4},{4,0},{8,12},{12,8},{16,20},{20,16},{24,28},{28,24},{1,5},{5... | collective-permute-start | bytes 1769480 | tf_op jit(solution)/shard_map/ppermute | solution.py:66
  245.0 13.2 %collective-permute-start.32 = (bf16[2,192,768]{2,1,0:T(8,128)(2,1)S(1)}, bf16[2,192,768]{2,1,0:T(8,128)(2,1)S(1)}, u32[]{:S(2)}, u32[]{:S(2)}) collective-permute-start(bf16[2,192,768]{2,1,0:T(8,128)(2,1)S(1)} %get-tuple-element.155.refs_0_), channel_id=1, source_target_pairs={{0,1},{1,0},{2,3},{3,2},{4,5},{5,4},{6,7},{7,6},{8,9},{9,8},{10,11... | collective-permute-start | bytes 1769480 | tf_op jit(solution)/shard_map/ppermute | solution.py:66
  253.1 5.1 %collective-permute-start.35 = (bf16[2,192,768]{2,1,0:T(8,128)(2,1)S(1)}, bf16[2,192,768]{2,1,0:T(8,128)(2,1)S(1)}, u32[]{:S(2)}, u32[]{:S(2)}) collective-permute-start(bf16[2,192,768]{2,1,0:T(8,128)(2,1)S(1)} %get-tuple-element.163.refs_6_), channel_id=1, source_target_pairs={{0,1},{1,0},{2,3},{3,2},{4,5},{5,4},{6,7},{7,6},{8,9},{9,8},{10,11... | collective-permute-start | bytes 1769480 | tf_op jit(solution)/shard_map/ppermute | solution.py:66
  258.2 75.4 %reduce-scatter.4.cloned.1.call-start = ((), (), s32[]{:S(2)}) async-start(), calls=%async_computation.4 | async-start | bytes 1474560 | tf_op jit(solution)/shard_map/reduce_scatter | solution.py:120
  277.8 26.7 %collective-permute-start.43 = (bf16[4,96,1536]{2,1,0:T(8,128)(2,1)S(1)}, bf16[4,96,1536]{2,1,0:T(8,128)(2,1)}, u32[]{:S(2)}, u32[]{:S(2)}) collective-permute-start(bf16[4,96,1536]{2,1,0:T(8,128)(2,1)S(1)} %get-tuple-element.173.refs_22_), channel_id=1, source_target_pairs={{0,4},{4,0},{8,12},{12,8},{16,20},{20,16},{24,28},{28,24},{1,5},{5... | collective-permute-start | bytes 3538952 | tf_op jit(solution)/shard_map/ppermute | solution.py:66
  308.0 16.3 %collective-permute-start.38 = (bf16[2,192,768]{2,1,0:T(8,128)(2,1)S(1)}, bf16[2,192,768]{2,1,0:T(8,128)(2,1)}, u32[]{:S(2)}, u32[]{:S(2)}) collective-permute-start(bf16[2,192,768]{2,1,0:T(8,128)(2,1)S(1)} %get-tuple-element.176), channel_id=1, source_target_pairs={{0,1},{1,0},{2,3},{3,2},{4,5},{5,4},{6,7},{7,6},{8,9},{9,8},{10,11... | collective-permute-start | bytes 1769480 | tf_op jit(solution)/shard_map/ppermute | solution.py:66
  308.3 4.0 collective-permute-start.40
  308.6 5.6 %collective-permute-start.41 = (bf16[192,192]{1,0:T(8,128)(2,1)S(1)}, bf16[192,192]{1,0:T(8,128)(2,1)S(1)}, u32[]{:S(2)}, u32[]{:S(2)}) collective-permute-start(bf16[192,192]{1,0:T(8,128)(2,1)S(1)} %copy-done.23), channel_id=1, source_target_pairs={{0,2},{1,3},{2,0},{3,1},{4,6},{5,7},{6,4},{7,5},{8,10},{9,11},{10,... | collective-permute-start | bytes 221192 | tf_op jit(solution)/shard_map/ppermute | solution.py:66
  309.6 5.3 %collective-permute-start.42 = (bf16[192,192]{1,0:T(8,128)(2,1)S(1)}, bf16[192,192]{1,0:T(8,128)(2,1)S(1)}, u32[]{:S(2)}, u32[]{:S(2)}) collective-permute-start(bf16[192,192]{1,0:T(8,128)(2,1)S(1)} %get-tuple-element.187), channel_id=1, source_target_pairs={{0,3},{1,2},{2,1},{3,0},{4,7},{5,6},{6,5},{7,4},{8,11},{9,10},{10,... | collective-permute-start | bytes 221192 | tf_op jit(solution)/shard_map/ppermute | solution.py:66
  310.2 16.6 %collective-permute-start.45 = (bf16[2,192,768]{2,1,0:T(8,128)(2,1)S(1)}, bf16[2,192,768]{2,1,0:T(8,128)(2,1)}, u32[]{:S(2)}, u32[]{:S(2)}) collective-permute-start(bf16[2,192,768]{2,1,0:T(8,128)(2,1)S(1)} %get-tuple-element.193), channel_id=1, source_target_pairs={{0,1},{1,0},{2,3},{3,2},{4,5},{5,4},{6,7},{7,6},{8,9},{9,8},{10,11... | collective-permute-start | bytes 1769480 | tf_op jit(solution)/shard_map/ppermute | solution.py:66
  321.0 16.3 %collective-permute-start.44 = (bf16[4,96,768]{2,1,0:T(8,128)(2,1)S(1)}, bf16[4,96,768]{2,1,0:T(8,128)(2,1)}, u32[]{:S(2)}, u32[]{:S(2)}) collective-permute-start(bf16[4,96,768]{2,1,0:T(8,128)(2,1)S(1)} %get-tuple-element.190), channel_id=1, source_target_pairs={{0,4},{4,0},{8,12},{12,8},{16,20},{20,16},{24,28},{28,24},{1,5},{5... | collective-permute-start | bytes 1769480 | tf_op jit(solution)/shard_map/ppermute | solution.py:66
  325.3 18.7 %collective-permute-start.39 = (bf16[192,768]{1,0:T(8,128)(2,1)S(1)}, bf16[192,768]{1,0:T(8,128)(2,1)S(1)}, u32[]{:S(2)}, u32[]{:S(2)}) collective-permute-start(bf16[192,768]{1,0:T(8,128)(2,1)S(1)} %fusion.6), channel_id=1, source_target_pairs={{0,2},{1,3},{2,0},{3,1},{4,6},{5,7},{6,4},{7,5},{8,10},{9,11},{10,... | collective-permute-start | bytes 884744 | tf_op jit(solution)/shard_map/ppermute | solution.py:66
  327.7 17.1 %collective-permute-start.46 = (bf16[192,768]{1,0:T(8,128)(2,1)S(1)}, bf16[192,768]{1,0:T(8,128)(2,1)S(1)}, u32[]{:S(2)}, u32[]{:S(2)}) collective-permute-start(bf16[192,768]{1,0:T(8,128)(2,1)S(1)} %fusion.7), channel_id=1, source_target_pairs={{0,2},{1,3},{2,0},{3,1},{4,6},{5,7},{6,4},{7,5},{8,10},{9,11},{10,... | collective-permute-start | bytes 884744 | tf_op jit(solution)/shard_map/ppermute | solution.py:66
  338.7 17.0 %collective-permute-start.50 = (bf16[96,768]{1,0:T(8,128)(2,1)S(1)}, bf16[96,768]{1,0:T(8,128)(2,1)S(1)}, u32[]{:S(2)}, u32[]{:S(2)}) collective-permute-start(bf16[96,768]{1,0:T(8,128)(2,1)S(1)} %get-tuple-element.224.refs_1_), channel_id=1, source_target_pairs={{0,8},{4,12},{8,0},{12,4},{16,24},{20,28},{24,16},{28,20},{1,9},{5... | collective-permute-start | bytes 442376 | tf_op jit(solution)/shard_map/ppermute | solution.py:66
  338.8 16.9 %collective-permute-start.51 = (bf16[96,768]{1,0:T(8,128)(2,1)S(1)}, bf16[96,768]{1,0:T(8,128)(2,1)S(1)}, u32[]{:S(2)}, u32[]{:S(2)}) collective-permute-start(bf16[96,768]{1,0:T(8,128)(2,1)S(1)} %get-tuple-element.223), channel_id=1, source_target_pairs={{0,16},{4,20},{8,24},{12,28},{16,0},{20,4},{24,8},{28,12},{1,17},{... | collective-permute-start | bytes 442376 | tf_op jit(solution)/shard_map/ppermute | solution.py:66
  339.6 16.1 %collective-permute-start.52 = (bf16[96,768]{1,0:T(8,128)(2,1)S(1)}, bf16[96,768]{1,0:T(8,128)(2,1)S(1)}, u32[]{:S(2)}, u32[]{:S(2)}) collective-permute-start(bf16[96,768]{1,0:T(8,128)(2,1)S(1)} %get-tuple-element.222), channel_id=1, source_target_pairs={{0,24},{4,28},{8,16},{12,20},{16,8},{20,12},{24,0},{28,4},{1,25},{... | collective-permute-start | bytes 442376 | tf_op jit(solution)/shard_map/ppermute | solution.py:66
  344.1 5.3 %collective-permute-start.47 = (bf16[4,16,768]{2,1,0:T(8,128)(2,1)S(1)}, bf16[4,16,768]{2,1,0:T(8,128)(2,1)S(1)}, u32[]{:S(2)}, u32[]{:S(2)}) collective-permute-start(bf16[4,16,768]{2,1,0:T(8,128)(2,1)S(1)} %convert_element_type.252), channel_id=1, source_target_pairs={{0,1},{1,0},{2,3},{3,2},{4,5},{5,4},{6,7},{7,6},{8,9},{9,8},{10,11... | collective-permute-start | bytes 294920 | tf_op jit(solution)/shard_map/ppermute | solution.py:66
  349.5 4.7 %collective-permute-start.48 = (bf16[4,16,768]{2,1,0:T(8,128)(2,1)S(1)}, bf16[4,16,768]{2,1,0:T(8,128)(2,1)S(1)}, u32[]{:S(2)}, u32[]{:S(2)}) collective-permute-start(bf16[4,16,768]{2,1,0:T(8,128)(2,1)S(1)} %add_convert_fusion.13), channel_id=1, source_target_pairs={{0,2},{1,3},{2,0},{3,1},{4,6},{5,7},{6,4},{7,5},{8,10},{9,11},{10,... | collective-permute-start | bytes 294920 | tf_op jit(solution)/shard_map/ppermute | solution.py:66
  355.3 6.0 %collective-permute-start.49 = (bf16[4,16,768]{2,1,0:T(8,128)(2,1)S(1)}, bf16[4,16,768]{2,1,0:T(8,128)(2,1)S(1)}, u32[]{:S(2)}, u32[]{:S(2)}) collective-permute-start(bf16[4,16,768]{2,1,0:T(8,128)(2,1)S(1)} %convert_element_type.258), channel_id=1, source_target_pairs={{0,4},{4,0},{8,12},{12,8},{16,20},{20,16},{24,28},{28,24},{1,5},{5... | collective-permute-start | bytes 294920 | tf_op jit(solution)/shard_map/ppermute | solution.py:66
  356.8 3.8 collective-permute-start.54
  362.9 8.4 %collective-permute-start.55 = (bf16[4,16,768]{2,1,0:T(8,128)(2,1)S(1)}, bf16[4,16,768]{2,1,0:T(8,128)(2,1)S(1)}, u32[]{:S(2)}, u32[]{:S(2)}) collective-permute-start(bf16[4,16,768]{2,1,0:T(8,128)(2,1)S(1)} %add_convert_fusion.12), channel_id=1, source_target_pairs={{0,8},{4,12},{8,0},{12,4},{16,24},{20,28},{24,16},{28,20},{1,9},{5... | collective-permute-start | bytes 294920 | tf_op jit(solution)/shard_map/ppermute | solution.py:66
  363.7 7.0 %collective-permute-start.57 = (f32[2,24,128]{2,1,0:T(8,128)S(1)}, f32[2,24,128]{2,1,0:T(8,128)S(1)}, u32[]{:S(2)}, u32[]{:S(2)}) collective-permute-start(f32[2,24,128]{2,1,0:T(8,128)S(1)} %add.265), channel_id=1, source_target_pairs={{0,8},{4,12},{8,0},{12,4},{16,24},{20,28},{24,16},{28,20},{1,9},{5... | collective-permute-start | bytes 73736 | tf_op jit(solution)/shard_map/ppermute | solution.py:66
  366.4 3.7 collective-permute-start.56
  372.9 7.3 %collective-permute-start.58 = (bf16[4,16,768]{2,1,0:T(8,128)(2,1)S(1)}, bf16[4,16,768]{2,1,0:T(8,128)(2,1)S(1)}, u32[]{:S(2)}, u32[]{:S(2)}) collective-permute-start(bf16[4,16,768]{2,1,0:T(8,128)(2,1)S(1)} %add_convert_fusion.11), channel_id=1, source_target_pairs={{0,16},{4,20},{8,24},{12,28},{16,0},{20,4},{24,8},{28,12},{1,17},{... | collective-permute-start | bytes 294920 | tf_op jit(solution)/shard_map/ppermute | solution.py:66
  373.7 5.9 %collective-permute-start.59 = (f32[2,24,128]{2,1,0:T(8,128)S(1)}, f32[2,24,128]{2,1,0:T(8,128)S(1)}, u32[]{:S(2)}, u32[]{:S(2)}) collective-permute-start(f32[2,24,128]{2,1,0:T(8,128)S(1)} %add.267), channel_id=1, source_target_pairs={{0,16},{4,20},{8,24},{12,28},{16,0},{20,4},{24,8},{28,12},{1,17},{... | collective-permute-start | bytes 73736 | tf_op jit(solution)/shard_map/ppermute | solution.py:66
  385.6 3.6 collective-permute-start.61
  389.2 4.0 collective-permute-start.62
  393.2 3.7 collective-permute-start.63
  396.9 4.5 %collective-permute-start.64 = (f32[8,128]{1,0:T(8,128)S(1)}, f32[8,128]{1,0:T(8,128)S(1)}, u32[]{:S(2)}, u32[]{:S(2)}) collective-permute-start(f32[8,128]{1,0:T(8,128)S(1)} %add.274), channel_id=1, source_target_pairs={{0,16},{4,20},{8,24},{12,28},{16,0},{20,4},{24,8},{28,12},{1,17},{... | collective-permute-start | bytes 12296 | tf_op jit(solution)/shard_map/ppermute | solution.py:66
  (90 other events, 534.4 us)
Sparse Core Ops, SparseCore 0:
  40.7 68.2 all-gather.1
  232.9 26.2 reduce-scatter.5
  261.4 20.6 reduce-scatter.7
  307.5 26.0 reduce-scatter.3

commit v2 on v1

--- a/solution.py
+++ b/solution.py
@@ -818,7 +818,7 @@
         ),
         out_shape=[
             pltpu.HBM((2, chunk, D), BF16),
-            jax.ShapeDtypeStruct((2, chunk, D), BF16),
+            pltpu.HBM((2, chunk, D), BF16),
             *shapes,
         ],
         compiler_params=pltpu.CompilerParams(vmem_limit_bytes=VMEM_BYTES),
@@ -939,7 +939,7 @@
         ),
         out_shape=[
             pltpu.HBM((2, chunk, D), BF16),
-            jax.ShapeDtypeStruct((2, chunk, D), BF16),
+            pltpu.HBM((2, chunk, D), BF16),
             pltpu.HBM((length, wide), BF16),
             pltpu.HBM((8, D), F32),
         ],
@@ -962,7 +962,7 @@
         kinds = [BF16, BF16]
     else:
         shape, kinds = (D, columns), [BF16]
-    return [jax.ShapeDtypeStruct(shape, kind) for kind in kinds], [whole_spec(shape)] * len(kinds)
+    return [pltpu.HBM(shape, kind) for kind in kinds], [whole_spec(shape)] * len(kinds)
 
 
 def run_qkv_outer(scalars, vec, groups, outward, split, riders=()):

time: 416 us -> 415 us (level)
  local copies, waits for them, and re-layouts: 35.1 us -> 26.6 us
  Pallas kernels: 179 us -> 184 us
    unnamed x175 -> x139, local copies, waits for them, and re-layouts: 24.6 us -> 16.9 us
  transfers between devices with their start and end apart: 69 -> 69, of which waited for: 30 -> 32; matrix products, arithmetic and copies ran while one was open for 10% -> 9% of each run, Pallas kernels for 38% -> 40%
where the time goes in v2:
time: 415 us; the launch traced here: 410 us
  Pallas kernels  184 us (44%)
  waiting for transfers between devices  102 us (25%)
  starting transfers between devices  50 us (12%)
  other arithmetic  30.9 us (7%)
  local copies, waits for them, and re-layouts  26.6 us (6%)
  between operations  15.6 us (4%)
    ppermute x62, waiting for transfers between devices, swap(): return lax.ppermute(values, axis, [(i, i ^ bits) for i in range(size)])  58.8 us
    pallas_call x4, Pallas kernels, run_forward(): pl.pallas_call(functools.partial(forward_kernel, counts, firsts), grid_sp...  57.8 us
    pallas_call x4, Pallas kernels, run_attention_backward(): pl.pallas_call(functools.partial(attention_backward_kernel, len(pieces),...  48.1 us
    ppermute x62, starting transfers between devices, swap(): return lax.ppermute(values, axis, [(i, i ^ bits) for i in range(size)])  48 us
    ppermute x3, waiting for transfers between devices, gather_rows(): rows = lax.ppermute(rows, 'dp', [(i, (i + 2) % 8) for i in range(8)])  38.6 us
    pallas_call x2, Pallas kernels, run_mlp_backward(): pl.pallas_call(functools.partial(mlp_backward_kernel, len(pieces), first,...  37.6 us
    unnamed x139, local copies, waits for them, and re-layouts  16.9 us
    pallas_call x2, Pallas kernels, run_qkv_outer(): pl.pallas_call(functools.partial(qkv_outer_kernel, len(groups[0]), len(ou...  12.2 us
  transfers between devices with their start and end apart: 69, of which 32 were waited for; matrix products, arithmetic and copies ran while one was open for 9% of the time, Pallas kernels for 40%

profile of v2, /device:TPU:0, one launch (start us, length us, event | category | flops | bytes accessed | tf_op | source)
XLA Modules:
  0.0 409.7 jit_solution(3267067059046031140)
XLA Ops:
  7.2 1.6 convert_element_type.209
  9.8 3.0 collective-permute-start.2
  12.8 1.6 collective-permute-start.3
  14.4 1.5 collective-permute-start
  19.1 7.3 %collective-permute-done.3.refs_12_.refs_20_.refs_14_.refs_16_ = bf16[96,2304]{1,0:T(8,128)(2,1)} collective-permute-done((bf16[96,2304]{1,0:T(8,128)(2,1)S(1)}, bf16[96,2304]{1,0:T(8,128)(2,1)}, u32[]{:S(2)}, u32[]{:S(2)}) %collective-permute-start.3) | collective-permute-done | bytes 442400 | tf_op jit(solution)/shard_map/ppermute | solution.py:94
  28.1 11.6 %collective-permute-done.5.refs_14_.refs_22_.refs_1_.refs_16_.refs_18_ = bf16[96,2304]{1,0:T(8,128)(2,1)S(1)} collective-permute-done((bf16[96,2304]{1,0:T(8,128)(2,1)}, bf16[96,2304]{1,0:T(8,128)(2,1)S(1)}, u32[]{:S(2)}, u32[]{:S(2)}) %collective-permute-start.5) | collective-permute-done | bytes 442400 | tf_op jit(solution)/shard_map/ppermute | solution.py:94
  44.9 19.7 %collective-permute-done.7.refs_16_.refs_24_.refs_18_.refs_20_ = bf16[96,2304]{1,0:T(8,128)(2,1)S(1)} collective-permute-done((bf16[96,2304]{1,0:T(8,128)(2,1)S(1)}, bf16[96,2304]{1,0:T(8,128)(2,1)S(1)}, u32[]{:S(2)}, u32[]{:S(2)}) %collective-permute-start.7) | collective-permute-done | bytes 442400 | tf_op jit(solution)/shard_map/ppermute | solution.py:94
  64.8 8.1 %collective-permute-done.8.refs_17_.refs_25_.refs_19_.refs_21_ = bf16[96,2304]{1,0:T(8,128)(2,1)S(1)} collective-permute-done((bf16[96,2304]{1,0:T(8,128)(2,1)S(1)}, bf16[96,2304]{1,0:T(8,128)(2,1)S(1)}, u32[]{:S(2)}, u32[]{:S(2)}) %collective-permute-start.8) | collective-permute-done | bytes 442400 | tf_op jit(solution)/shard_map/ppermute | solution.py:66
  73.1 1.6 collective-permute-start.10
  75.0 1.4 pad_maximum_fusion.1.refs_0_.refs_6_.grad
  76.8 1.9 collective-permute-done.10.refs_8_.refs_7_
  80.0 14.3 %layer_forward.4 = (bf16[2,192,768]{2,1,0:T(8,128)(2,1)}, bf16[2,192,768]{2,1,0:T(8,128)(2,1)}, bf16[768,768]{1,0:T(8,128)(2,1)}, bf16[768,384]{1,0:T(8,128)(2,1...) custom-call(s32[5]{0:T(128)S(1)} %pad_add_fusion.place, ...), custom_call_target="tpu_custom_call" | custom-call | flops 12999999488 | bytes 13000000 | tf_op jit(solution)/shard_map/layer_forward/pallas_call | solution.py:796
  95.2 1.8 collective-permute-done.12.near
  98.4 1.6 collective-permute-start.13
  100.0 14.6 %layer_forward.5 = (bf16[2,192,768]{2,1,0:T(8,128)(2,1)}, bf16[2,192,768]{2,1,0:T(8,128)(2,1)}, bf16[768,768]{1,0:T(8,128)(2,1)}, bf16[768,384]{1,0:T(8,128)(2,1...) custom-call(s32[5]{0:T(128)S(1)} %pad_add_fusion.place, ...), custom_call_target="tpu_custom_call" | custom-call | flops 12999999488 | bytes 13000000 | tf_op jit(solution)/shard_map/layer_forward/pallas_call | solution.py:796
  116.8 2.7 finish_stream.2
  125.2 2.0 collective-permute-done.18.refs_8_.refs_7_
  127.5 14.6 %layer_forward.6 = (bf16[2,192,768]{2,1,0:T(8,128)(2,1)}, bf16[2,192,768]{2,1,0:T(8,128)(2,1)}, bf16[768,768]{1,0:T(8,128)(2,1)}, bf16[768,384]{1,0:T(8,128)(2,1...) custom-call(s32[5]{0:T(128)S(1)} %pad_add_fusion.place, ...), custom_call_target="tpu_custom_call" | custom-call | flops 12999999488 | bytes 13000000 | tf_op jit(solution)/shard_map/layer_forward/pallas_call | solution.py:796
  142.2 2.7 finish_stream.3
  144.9 1.5 collective-permute-start.24
  146.5 1.5 collective-permute-done.24.refs_1_
  148.0 14.4 %layer_forward.7 = (bf16[2,192,768]{2,1,0:T(8,128)(2,1)}, bf16[2,192,768]{2,1,0:T(8,128)(2,1)}, bf16[768,768]{1,0:T(8,128)(2,1)}, bf16[768,384]{1,0:T(8,128)(2,1...) custom-call(s32[5]{0:T(128)S(1)} %pad_add_fusion.place, ...), custom_call_target="tpu_custom_call" | custom-call | flops 12999999488 | bytes 13000000 | tf_op jit(solution)/shard_map/layer_forward/pallas_call | solution.py:796
  166.7 19.2 %mlp_backward.2 = (bf16[768,768]{1,0:T(8,128)(2,1)}, bf16[768,768]{1,0:T(8,128)(2,1)}, bf16[768,768]{1,0:T(8,128)(2,1)}, f32[8,768]{1,0:T(8,128)}, bf16[768,768]...) custom-call(s32[5]{0:T(128)S(1)} %pad_add_fusion.place, ...), custom_call_target="tpu_custom_call" | custom-call | flops 20000000000 | bytes 20000000 | tf_op jit(solution)/shard_map/mlp_backward/pallas_call | solution.py:867
  186.8 2.9 block_out.1.refs_16_
  189.7 11.9 %attention_backward.4 = (bf16[2,192,768]{2,1,0:T(8,128)(2,1)}, bf16[2,192,768]{2,1,0:T(8,128)(2,1)}, bf16[768,576]{1,0:T(8,128)(2,1)}, f32[8,768]{1,0:T(8,128)}) custom-call(s32[5]{0:T(128)S(1)} %pad_add_fusion.place, bf16[768,768]{1,0:T(8,128)(2,1)} %get-tuple-element.137.refs_0_, f32[8,768]{1,0:T(8,128)S(1)} %stack.79.refs_2_.vec.refs_1_, ...), custom_call_target="tpu_custom_call" | custom-call | flops 11000000512 | bytes 11000000 | tf_op jit(solution)/shard_map/attention_backward/pallas_call | solution.py:909
  203.8 1.4 add_convert_fusion.4.refs_15_
  205.3 1.4 collective-permute-start.28
  209.3 12.2 %attention_backward.5 = (bf16[2,192,768]{2,1,0:T(8,128)(2,1)}, bf16[2,192,768]{2,1,0:T(8,128)(2,1)}, bf16[768,576]{1,0:T(8,128)(2,1)}, f32[8,768]{1,0:T(8,128)}) custom-call(s32[5]{0:T(128)S(1)} %pad_add_fusion.place, bf16[768,768]{1,0:T(8,128)(2,1)} %get-tuple-element.145.refs_0_, f32[8,768]{1,0:T(8,128)S(1)} %stack.79.refs_2_.vec.refs_1_, ...), custom_call_target="tpu_custom_call" | custom-call | flops 11000000512 | bytes 11000000 | tf_op jit(solution)/shard_map/attention_backward/pallas_call | solution.py:909
  223.7 6.6 %collective-permute-done.36 = bf16[4,96,1536]{2,1,0:T(8,128)(2,1)} collective-permute-done((bf16[4,96,1536]{2,1,0:T(8,128)(2,1)}, bf16[4,96,1536]{2,1,0:T(8,128)(2,1)}, u32[]{:S(2)}, u32[]{:S(2)}) %collective-permute-start.36) | collective-permute-done | bytes 1179680 | tf_op jit(solution)/shard_map/ppermute | solution.py:66
  230.3 2.9 add_convert_fusion.1
  235.9 5.9 %qkv_outer.2 = (bf16[4,96,768]{2,1,0:T(8,128)(2,1)}, bf16[4,96,768]{2,1,0:T(8,128)(2,1)}) custom-call(s32[4]{0:T(128)S(1)} %pad_add_fusion.1.scalars, f32[8,768]{1,0:T(8,128)S(1)} %stack.79.refs_2_.vec.refs_1_, bf16[768,768]{1,0:T(8,128)(2,1)} %get-tuple-element.125.refs_1_.refs_2_.refs_9_.refs_0_, bf16[768,576]{1,0:T(8,128)(2,1)} %get-tuple-element.161.refs_1_, ...), custom_call_target="tpu_custom_call" | custom-call | flops 6000000000 | bytes 6000000 | tf_op jit(solution)/shard_map/qkv_outer/pallas_call | solution.py:972
  242.4 3.4 finish_grad.2
  245.8 3.7 collective-permute-done.34.refs_0_
  250.3 3.4 finish_grad.3
  253.6 3.4 collective-permute-done.37
  257.0 2.0 add_convert_fusion.2
  259.2 18.4 %mlp_backward.3 = (bf16[768,768]{1,0:T(8,128)(2,1)}, bf16[768,768]{1,0:T(8,128)(2,1)}, bf16[768,768]{1,0:T(8,128)(2,1)}, f32[8,768]{1,0:T(8,128)}, bf16[768,768]...) custom-call(s32[5]{0:T(128)S(1)} %pad_add_fusion.place, ...), custom_call_target="tpu_custom_call" | custom-call | flops 20000000000 | bytes 20000000 | tf_op jit(solution)/shard_map/mlp_backward/pallas_call | solution.py:867
  278.0 12.0 %attention_backward.6 = (bf16[2,192,768]{2,1,0:T(8,128)(2,1)}, bf16[2,192,768]{2,1,0:T(8,128)(2,1)}, bf16[768,576]{1,0:T(8,128)(2,1)}, f32[8,768]{1,0:T(8,128)}) custom-call(s32[5]{0:T(128)S(1)} %pad_add_fusion.place, bf16[768,768]{1,0:T(8,128)(2,1)} %get-tuple-element.168.refs_0_, f32[8,768]{1,0:T(8,128)S(1)} %stack.74.refs_2_.vec.refs_1_, ...), custom_call_target="tpu_custom_call" | custom-call | flops 11000000512 | bytes 11000000 | tf_op jit(solution)/shard_map/attention_backward/pallas_call | solution.py:909
  289.9 12.1 %attention_backward.7 = (bf16[2,192,768]{2,1,0:T(8,128)(2,1)}, bf16[2,192,768]{2,1,0:T(8,128)(2,1)}, bf16[768,576]{1,0:T(8,128)(2,1)}, f32[8,768]{1,0:T(8,128)}) custom-call(s32[5]{0:T(128)S(1)} %pad_add_fusion.place, bf16[768,768]{1,0:T(8,128)(2,1)} %get-tuple-element.178.refs_0_, f32[8,768]{1,0:T(8,128)S(1)} %stack.74.refs_2_.vec.refs_1_, ...), custom_call_target="tpu_custom_call" | custom-call | flops 11000000512 | bytes 11000000 | tf_op jit(solution)/shard_map/attention_backward/pallas_call | solution.py:909
  302.0 2.4 collective-permute-done.43
  304.4 2.6 add_convert_fusion
  310.3 1.6 examples.1.refs_0_
  311.9 1.6 collective-permute-done.41.refs_6_
  314.3 6.3 %qkv_outer.3 = (bf16[4,96,768]{2,1,0:T(8,128)(2,1)}, bf16[4,96,768]{2,1,0:T(8,128)(2,1)}) custom-call(s32[4]{0:T(128)S(1)} %pad_add_fusion.1.scalars, f32[8,768]{1,0:T(8,128)S(1)} %stack.74.refs_2_.vec.refs_1_, bf16[768,768]{1,0:T(8,128)(2,1)} %get-tuple-element.119.refs_1_.refs_2_.refs_9_.refs_0_, bf16[768,576]{1,0:T(8,128)(2,1)} %get-tuple-element.177.refs_1_, ...), custom_call_target="tpu_custom_call" | custom-call | flops 6000000000 | bytes 6000000 | tf_op jit(solution)/shard_map/qkv_outer/pallas_call | solution.py:972
  328.5 4.8 %reduce-scatter.4.cloned.1.call-done.refs_1_.refs_0_ = bf16[96,1536]{1,0:T(8,128)(2,1)} async-done(((bf16[384,1536]{1,0:T(8,128)(2,1)}), bf16[96,1536]{1,0:T(8,128)(2,1)}) %reduce-scatter.4.cloned.1.call-update) | async-done | bytes 294928 | tf_op jit(solution)/shard_map/reduce_scatter | solution.py:120
  333.2 3.8 collective-permute-done.44
  339.2 3.5 collective-permute-start.52
  345.1 3.9 input_grad.1.refs_10_
  351.1 2.6 collective-permute-done.48
  356.4 1.7 collective-permute-start.54
  362.6 2.0 collective-permute-start.57
  366.2 2.8 collective-permute-done.56.refs_1_
  372.0 2.9 collective-permute-start.59
  375.6 2.3 collective-permute-done.59.refs_1_
  379.9 1.5 copy-done.17
  381.4 1.4 squares.1
  384.9 1.6 convert_add_fusion.1.totals
  387.6 1.7 collective-permute-start.62
  389.3 2.3 small_vectors.1
  391.6 1.5 slice_reduce_fusion
  393.1 2.1 collective-permute-done.63
  395.2 1.8 collective-permute-start.64
  397.1 2.7 collective-permute-done.64
  400.5 2.2 update.1
  (363 shorter events, 77.1 us)
Async XLA Ops:
  7.2 112.4 %all-gather.2.cloned.1.call-start = ((), (), s32[]{:S(2)}) async-start(), calls=%async_computation.3 | async-start | bytes 3981312 | tf_op jit(solution)/shard_map/all_gather | solution.py:1252
  9.8 17.1 %collective-permute-start.2 = (bf16[96,2304]{1,0:T(8,128)(2,1)S(1)}, bf16[96,2304]{1,0:T(8,128)(2,1)S(1)}, u32[]{:S(2)}, u32[]{:S(2)}) collective-permute-start(bf16[96,2304]{1,0:T(8,128)(2,1)S(1)} %concatenate.23.refs_10_.refs_18_.refs_12_.refs_14_), channel_id=1, source_target_pairs={{0,4},{4,0},{8,12},{12,8},{16,20},{20,16},{24,28},{28,24},{1,5},{5... | collective-permute-start | bytes 1327112 | tf_op jit(solution)/shard_map/ppermute | solution.py:66
  12.8 13.6 %collective-permute-start.3 = (bf16[96,2304]{1,0:T(8,128)(2,1)S(1)}, bf16[96,2304]{1,0:T(8,128)(2,1)}, u32[]{:S(2)}, u32[]{:S(2)}) collective-permute-start(bf16[96,2304]{1,0:T(8,128)(2,1)S(1)} %concatenate.23.refs_10_.refs_18_.refs_12_.refs_14_), channel_id=1, source_target_pairs={{0,8},{4,12},{8,16},{12,20},{16,24},{20,28},{24,0},{28,4},{1,9},{5... | collective-permute-start | bytes 1327112 | tf_op jit(solution)/shard_map/ppermute | solution.py:94
  14.4 26.2 %collective-permute-start = (bf16[2,192,768]{2,1,0:T(8,128)(2,1)S(1)}, bf16[2,192,768]{2,1,0:T(8,128)(2,1)S(1)}, u32[]{:S(2)}, u32[]{:S(2)}) collective-permute-start(bf16[2,192,768]{2,1,0:T(8,128)(2,1)S(1)} %copy-done.23), channel_id=1, source_target_pairs={{0,2},{1,3},{2,0},{3,1},{4,6},{5,7},{6,4},{7,5},{8,10},{9,11},{10,... | collective-permute-start | bytes 1769480 | tf_op jit(solution)/shard_map/ppermute | solution.py:66
  15.9 59.1 %collective-permute-start.14 = (bf16[2,192,768]{2,1,0:T(8,128)(2,1)}, bf16[2,192,768]{2,1,0:T(8,128)(2,1)}, u32[]{:S(2)}, u32[]{:S(2)}) collective-permute-start(bf16[2,192,768]{2,1,0:T(8,128)(2,1)} %param.12), channel_id=1, source_target_pairs={{0,2},{1,3},{2,0},{3,1},{4,6},{5,7},{6,4},{7,5},{8,10},{9,11},{10,... | collective-permute-start | bytes 1769480 | tf_op jit(solution)/shard_map/ppermute | solution.py:66
  26.4 17.4 %collective-permute-start.4 = (bf16[96,2304]{1,0:T(8,128)(2,1)}, bf16[96,2304]{1,0:T(8,128)(2,1)}, u32[]{:S(2)}, u32[]{:S(2)}) collective-permute-start(bf16[96,2304]{1,0:T(8,128)(2,1)} %collective-permute-done.3.refs_12_.refs_20_.refs_14_.refs_16_), channel_id=1, source_target_pairs={{0,4},{4,0},{8,12},{12,8},{16,20},{20,16},{24,28},{28,24},{1,5},{5... | collective-permute-start | bytes 1327112 | tf_op jit(solution)/shard_map/ppermute | solution.py:66
  27.0 12.8 %collective-permute-start.5 = (bf16[96,2304]{1,0:T(8,128)(2,1)}, bf16[96,2304]{1,0:T(8,128)(2,1)S(1)}, u32[]{:S(2)}, u32[]{:S(2)}) collective-permute-start(bf16[96,2304]{1,0:T(8,128)(2,1)} %collective-permute-done.3.refs_12_.refs_20_.refs_14_.refs_16_), channel_id=1, source_target_pairs={{0,8},{4,12},{8,16},{12,20},{16,24},{20,28},{24,0},{28,4},{1,9},{5... | collective-permute-start | bytes 1327112 | tf_op jit(solution)/shard_map/ppermute | solution.py:94
  40.5 280.7 %reduce-scatter.6.cloned.1.call-start = ((), (), s32[]{:S(2)}) async-start(), calls=%async_computation.5 | async-start | bytes 1474560 | tf_op jit(solution)/shard_map/reduce_scatter | solution.py:120
  41.8 35.1 %collective-permute-start.1 = (bf16[2,2,192,768]{3,2,1,0:T(8,128)(2,1)S(1)}, bf16[2,2,192,768]{3,2,1,0:T(8,128)(2,1)S(1)}, u32[]{:S(2)}, u32[]{:S(2)}) collective-permute-start(bf16[2,2,192,768]{3,2,1,0:T(8,128)(2,1)S(1)} %fusion.3.refs_0_), channel_id=1, source_target_pairs={{0,1},{1,0},{2,3},{3,2},{4,5},{5,4},{6,7},{7,6},{8,9},{9,8},{10,11... | collective-permute-start | bytes 3538952 | tf_op jit(solution)/shard_map/ppermute | solution.py:66
  42.4 22.3 %collective-permute-start.6 = (bf16[96,2304]{1,0:T(8,128)(2,1)S(1)}, bf16[96,2304]{1,0:T(8,128)(2,1)S(1)}, u32[]{:S(2)}, u32[]{:S(2)}) collective-permute-start(bf16[96,2304]{1,0:T(8,128)(2,1)S(1)} %copy-done.47), channel_id=1, source_target_pairs={{0,4},{4,0},{8,12},{12,8},{16,20},{20,16},{24,28},{28,24},{1,5},{5... | collective-permute-start | bytes 1327112 | tf_op jit(solution)/shard_map/ppermute | solution.py:66
  43.6 21.0 %collective-permute-start.7 = (bf16[96,2304]{1,0:T(8,128)(2,1)S(1)}, bf16[96,2304]{1,0:T(8,128)(2,1)S(1)}, u32[]{:S(2)}, u32[]{:S(2)}) collective-permute-start(bf16[96,2304]{1,0:T(8,128)(2,1)S(1)} %copy-done.47), channel_id=1, source_target_pairs={{0,8},{4,12},{8,16},{12,20},{16,24},{20,28},{24,0},{28,4},{1,9},{5... | collective-permute-start | bytes 1327112 | tf_op jit(solution)/shard_map/ppermute | solution.py:94
  64.6 8.3 %collective-permute-start.8 = (bf16[96,2304]{1,0:T(8,128)(2,1)S(1)}, bf16[96,2304]{1,0:T(8,128)(2,1)S(1)}, u32[]{:S(2)}, u32[]{:S(2)}) collective-permute-start(bf16[96,2304]{1,0:T(8,128)(2,1)S(1)} %collective-permute-done.7.refs_16_.refs_24_.refs_18_.refs_20_), channel_id=1, source_target_pairs={{0,4},{4,0},{8,12},{12,8},{16,20},{20,16},{24,28},{28,24},{1,5},{5... | collective-permute-start | bytes 1327112 | tf_op jit(solution)/shard_map/ppermute | solution.py:66
  73.0 3.8 collective-permute-start.9
  73.1 5.7 %collective-permute-start.10 = (bf16[192,192]{1,0:T(8,128)(2,1)S(1)}, bf16[192,192]{1,0:T(8,128)(2,1)S(1)}, u32[]{:S(2)}, u32[]{:S(2)}) collective-permute-start(bf16[192,192]{1,0:T(8,128)(2,1)S(1)} %get-tuple-element.234), channel_id=1, source_target_pairs={{0,2},{1,3},{2,0},{3,1},{4,6},{5,7},{6,4},{7,5},{8,10},{9,11},{10,... | collective-permute-start | bytes 221192 | tf_op jit(solution)/shard_map/ppermute | solution.py:66
  74.7 5.3 %collective-permute-start.11 = (bf16[192,192]{1,0:T(8,128)(2,1)S(1)}, bf16[192,192]{1,0:T(8,128)(2,1)S(1)}, u32[]{:S(2)}, u32[]{:S(2)}) collective-permute-start(bf16[192,192]{1,0:T(8,128)(2,1)S(1)} %get-tuple-element.233), channel_id=1, source_target_pairs={{0,3},{1,2},{2,1},{3,0},{4,7},{5,6},{6,5},{7,4},{8,11},{9,10},{10,... | collective-permute-start | bytes 221192 | tf_op jit(solution)/shard_map/ppermute | solution.py:66
  76.4 23.6 %collective-permute-start.15 = (bf16[2,2,192,768]{3,2,1,0:T(8,128)(2,1)S(1)}, bf16[2,2,192,768]{3,2,1,0:T(8,128)(2,1)}, u32[]{:S(2)}, u32[]{:S(2)}) collective-permute-start(bf16[2,2,192,768]{3,2,1,0:T(8,128)(2,1)S(1)} %pad_maximum_fusion.1.refs_0_.refs_6_.grad), channel_id=1, source_target_pairs={{0,1},{1,0},{2,3},{3,2},{4,5},{5,4},{6,7},{7,6},{8,9},{9,8},{10,11... | collective-permute-start | bytes 3538952 | tf_op jit(solution)/shard_map/ppermute | solution.py:66
  98.4 16.2 %collective-permute-start.13 = (bf16[2,192,768]{2,1,0:T(8,128)(2,1)S(1)}, bf16[2,192,768]{2,1,0:T(8,128)(2,1)}, u32[]{:S(2)}, u32[]{:S(2)}) collective-permute-start(bf16[2,192,768]{2,1,0:T(8,128)(2,1)S(1)} %add_convert_fusion.6.refs_26_), channel_id=1, source_target_pairs={{0,2},{1,3},{2,0},{3,1},{4,6},{5,7},{6,4},{7,5},{8,10},{9,11},{10,... | collective-permute-start | bytes 1769480 | tf_op jit(solution)/shard_map/ppermute | solution.py:66
  114.6 8.3 %collective-permute-start.20 = (bf16[2,192,768]{2,1,0:T(8,128)(2,1)}, bf16[2,192,768]{2,1,0:T(8,128)(2,1)}, u32[]{:S(2)}, u32[]{:S(2)}) collective-permute-start(bf16[2,192,768]{2,1,0:T(8,128)(2,1)} %after.25), channel_id=1, source_target_pairs={{0,1},{1,0},{2,3},{3,2},{4,5},{5,4},{6,7},{7,6},{8,9},{9,8},{10,11... | collective-permute-start | bytes 1769480 | tf_op jit(solution)/shard_map/ppermute | solution.py:66
  119.4 5.7 %collective-permute-start.16 = (bf16[2,192,768]{2,1,0:T(8,128)(2,1)S(1)}, bf16[2,192,768]{2,1,0:T(8,128)(2,1)S(1)}, u32[]{:S(2)}, u32[]{:S(2)}) collective-permute-start(bf16[2,192,768]{2,1,0:T(8,128)(2,1)S(1)} %get-tuple-element.118.refs_0_), channel_id=1, source_target_pairs={{0,1},{1,0},{2,3},{3,2},{4,5},{5,4},{6,7},{7,6},{8,9},{9,8},{10,11... | collective-permute-start | bytes 1769480 | tf_op jit(solution)/shard_map/ppermute | solution.py:66
  121.0 4.2 %collective-permute-start.17 = (bf16[192,192]{1,0:T(8,128)(2,1)S(1)}, bf16[192,192]{1,0:T(8,128)(2,1)S(1)}, u32[]{:S(2)}, u32[]{:S(2)}) collective-permute-start(bf16[192,192]{1,0:T(8,128)(2,1)S(1)} %get-tuple-element.231), channel_id=1, source_target_pairs={{0,1},{1,0},{2,3},{3,2},{4,5},{5,4},{6,7},{7,6},{8,9},{9,8},{10,11... | collective-permute-start | bytes 221192 | tf_op jit(solution)/shard_map/ppermute | solution.py:66
  121.5 5.7 %collective-permute-start.18 = (bf16[192,192]{1,0:T(8,128)(2,1)S(1)}, bf16[192,192]{1,0:T(8,128)(2,1)S(1)}, u32[]{:S(2)}, u32[]{:S(2)}) collective-permute-start(bf16[192,192]{1,0:T(8,128)(2,1)S(1)} %get-tuple-element.230), channel_id=1, source_target_pairs={{0,2},{1,3},{2,0},{3,1},{4,6},{5,7},{6,4},{7,5},{8,10},{9,11},{10,... | collective-permute-start | bytes 221192 | tf_op jit(solution)/shard_map/ppermute | solution.py:66
  122.2 5.3 %collective-permute-start.19 = (bf16[192,192]{1,0:T(8,128)(2,1)S(1)}, bf16[192,192]{1,0:T(8,128)(2,1)S(1)}, u32[]{:S(2)}, u32[]{:S(2)}) collective-permute-start(bf16[192,192]{1,0:T(8,128)(2,1)S(1)} %get-tuple-element.229), channel_id=1, source_target_pairs={{0,3},{1,2},{2,1},{3,0},{4,7},{5,6},{6,5},{7,4},{8,11},{9,10},{10,... | collective-permute-start | bytes 221192 | tf_op jit(solution)/shard_map/ppermute | solution.py:66
  124.2 18.0 %collective-permute-start.21 = (bf16[2,192,768]{2,1,0:T(8,128)(2,1)S(1)}, bf16[2,192,768]{2,1,0:T(8,128)(2,1)}, u32[]{:S(2)}, u32[]{:S(2)}) collective-permute-start(bf16[2,192,768]{2,1,0:T(8,128)(2,1)S(1)} %add_convert_fusion.5.refs_12_), channel_id=1, source_target_pairs={{0,2},{1,3},{2,0},{3,1},{4,6},{5,7},{6,4},{7,5},{8,10},{9,11},{10,... | collective-permute-start | bytes 1769480 | tf_op jit(solution)/shard_map/ppermute | solution.py:66
  144.9 3.1 collective-permute-start.24
  146.4 16.5 %collective-permute-start.22 = (bf16[2,192,768]{2,1,0:T(8,128)(2,1)S(1)}, bf16[2,192,768]{2,1,0:T(8,128)(2,1)S(1)}, u32[]{:S(2)}, u32[]{:S(2)}) collective-permute-start(bf16[2,192,768]{2,1,0:T(8,128)(2,1)S(1)} %copy-done.45), channel_id=1, source_target_pairs={{0,1},{1,0},{2,3},{3,2},{4,5},{5,4},{6,7},{7,6},{8,9},{9,8},{10,11... | collective-permute-start | bytes 1769480 | tf_op jit(solution)/shard_map/ppermute | solution.py:66
  162.9 23.0 %collective-permute-start.23 = (bf16[192,768]{1,0:T(8,128)(2,1)S(1)}, bf16[192,768]{1,0:T(8,128)(2,1)S(1)}, u32[]{:S(2)}, u32[]{:S(2)}) collective-permute-start(bf16[192,768]{1,0:T(8,128)(2,1)S(1)} %fusion.4), channel_id=1, source_target_pairs={{0,2},{1,3},{2,0},{3,1},{4,6},{5,7},{6,4},{7,5},{8,10},{9,11},{10,... | collective-permute-start | bytes 884744 | tf_op jit(solution)/shard_map/ppermute | solution.py:66
  165.9 20.0 %collective-permute-start.26 = (bf16[192,768]{1,0:T(8,128)(2,1)S(1)}, bf16[192,768]{1,0:T(8,128)(2,1)S(1)}, u32[]{:S(2)}, u32[]{:S(2)}) collective-permute-start(bf16[192,768]{1,0:T(8,128)(2,1)S(1)} %fusion.5), channel_id=1, source_target_pairs={{0,2},{1,3},{2,0},{3,1},{4,6},{5,7},{6,4},{7,5},{8,10},{9,11},{10,... | collective-permute-start | bytes 884744 | tf_op jit(solution)/shard_map/ppermute | solution.py:66
  201.7 28.7 %collective-permute-start.36 = (bf16[4,96,1536]{2,1,0:T(8,128)(2,1)}, bf16[4,96,1536]{2,1,0:T(8,128)(2,1)}, u32[]{:S(2)}, u32[]{:S(2)}) collective-permute-start(bf16[4,96,1536]{2,1,0:T(8,128)(2,1)} %get-tuple-element.142.refs_15_), channel_id=1, source_target_pairs={{0,4},{4,0},{8,12},{12,8},{16,20},{20,16},{24,28},{28,24},{1,5},{5... | collective-permute-start | bytes 3538952 | tf_op jit(solution)/shard_map/ppermute | solution.py:66
  201.8 4.8 %collective-permute-start.29 = (bf16[192,192]{1,0:T(8,128)(2,1)S(1)}, bf16[192,192]{1,0:T(8,128)(2,1)S(1)}, u32[]{:S(2)}, u32[]{:S(2)}) collective-permute-start(bf16[192,192]{1,0:T(8,128)(2,1)S(1)} %get-tuple-element.151), channel_id=1, source_target_pairs={{0,1},{1,0},{2,3},{3,2},{4,5},{5,4},{6,7},{7,6},{8,9},{9,8},{10,11... | collective-permute-start | bytes 221192 | tf_op jit(solution)/shard_map/ppermute | solution.py:66
  202.1 5.5 %collective-permute-start.30 = (bf16[192,192]{1,0:T(8,128)(2,1)S(1)}, bf16[192,192]{1,0:T(8,128)(2,1)S(1)}, u32[]{:S(2)}, u32[]{:S(2)}) collective-permute-start(bf16[192,192]{1,0:T(8,128)(2,1)S(1)} %get-tuple-element.152), channel_id=1, source_target_pairs={{0,2},{1,3},{2,0},{3,1},{4,6},{5,7},{6,4},{7,5},{8,10},{9,11},{10,... | collective-permute-start | bytes 221192 | tf_op jit(solution)/shard_map/ppermute | solution.py:66
  203.5 5.2 %collective-permute-start.31 = (bf16[192,192]{1,0:T(8,128)(2,1)S(1)}, bf16[192,192]{1,0:T(8,128)(2,1)S(1)}, u32[]{:S(2)}, u32[]{:S(2)}) collective-permute-start(bf16[192,192]{1,0:T(8,128)(2,1)S(1)} %get-tuple-element.153), channel_id=1, source_target_pairs={{0,3},{1,2},{2,1},{3,0},{4,7},{5,6},{6,5},{7,4},{8,11},{9,10},{10,... | collective-permute-start | bytes 221192 | tf_op jit(solution)/shard_map/ppermute | solution.py:66
  205.3 16.5 %collective-permute-start.28 = (bf16[2,192,768]{2,1,0:T(8,128)(2,1)S(1)}, bf16[2,192,768]{2,1,0:T(8,128)(2,1)S(1)}, u32[]{:S(2)}, u32[]{:S(2)}) collective-permute-start(bf16[2,192,768]{2,1,0:T(8,128)(2,1)S(1)} %add_convert_fusion.4.refs_15_), channel_id=1, source_target_pairs={{0,2},{1,3},{2,0},{3,1},{4,6},{5,7},{6,4},{7,5},{8,10},{9,11},{10,... | collective-permute-start | bytes 1769480 | tf_op jit(solution)/shard_map/ppermute | solution.py:66
  222.7 10.8 %collective-permute-start.33 = (bf16[2,192,768]{2,1,0:T(8,128)(2,1)}, bf16[2,192,768]{2,1,0:T(8,128)(2,1)S(1)}, u32[]{:S(2)}, u32[]{:S(2)}) collective-permute-start(bf16[2,192,768]{2,1,0:T(8,128)(2,1)} %after.29), channel_id=1, source_target_pairs={{0,1},{1,0},{2,3},{3,2},{4,5},{5,4},{6,7},{7,6},{8,9},{9,8},{10,11... | collective-permute-start | bytes 1769480 | tf_op jit(solution)/shard_map/ppermute | solution.py:66
  233.3 87.9 %reduce-scatter.8.cloned.1.call-start = ((), (), s32[]{:S(2)}) async-start(), calls=%async_computation.6 | async-start | bytes 737280 | tf_op jit(solution)/shard_map/reduce_scatter | solution.py:120
  234.5 15.0 %collective-permute-start.34 = (bf16[2,192,768]{2,1,0:T(8,128)(2,1)S(1)}, bf16[2,192,768]{2,1,0:T(8,128)(2,1)S(1)}, u32[]{:S(2)}, u32[]{:S(2)}) collective-permute-start(bf16[2,192,768]{2,1,0:T(8,128)(2,1)S(1)} %add_convert_fusion.3.refs_8_), channel_id=1, source_target_pairs={{0,2},{1,3},{2,0},{3,1},{4,6},{5,7},{6,4},{7,5},{8,10},{9,11},{10,... | collective-permute-start | bytes 1769480 | tf_op jit(solution)/shard_map/ppermute | solution.py:66
  241.9 15.2 %collective-permute-start.37 = (bf16[4,96,768]{2,1,0:T(8,128)(2,1)}, bf16[4,96,768]{2,1,0:T(8,128)(2,1)}, u32[]{:S(2)}, u32[]{:S(2)}) collective-permute-start(bf16[4,96,768]{2,1,0:T(8,128)(2,1)} %get-tuple-element.174), channel_id=1, source_target_pairs={{0,4},{4,0},{8,12},{12,8},{16,20},{20,16},{24,28},{28,24},{1,5},{5... | collective-permute-start | bytes 1769480 | tf_op jit(solution)/shard_map/ppermute | solution.py:66
  245.8 13.3 %collective-permute-start.32 = (bf16[2,192,768]{2,1,0:T(8,128)(2,1)S(1)}, bf16[2,192,768]{2,1,0:T(8,128)(2,1)S(1)}, u32[]{:S(2)}, u32[]{:S(2)}) collective-permute-start(bf16[2,192,768]{2,1,0:T(8,128)(2,1)S(1)} %get-tuple-element.155.refs_0_), channel_id=1, source_target_pairs={{0,1},{1,0},{2,3},{3,2},{4,5},{5,4},{6,7},{7,6},{8,9},{9,8},{10,11... | collective-permute-start | bytes 1769480 | tf_op jit(solution)/shard_map/ppermute | solution.py:66
  253.6 5.5 %collective-permute-start.35 = (bf16[2,192,768]{2,1,0:T(8,128)(2,1)S(1)}, bf16[2,192,768]{2,1,0:T(8,128)(2,1)S(1)}, u32[]{:S(2)}, u32[]{:S(2)}) collective-permute-start(bf16[2,192,768]{2,1,0:T(8,128)(2,1)S(1)} %get-tuple-element.163.refs_6_), channel_id=1, source_target_pairs={{0,1},{1,0},{2,3},{3,2},{4,5},{5,4},{6,7},{7,6},{8,9},{9,8},{10,11... | collective-permute-start | bytes 1769480 | tf_op jit(solution)/shard_map/ppermute | solution.py:66
  259.1 74.1 %reduce-scatter.4.cloned.1.call-start = ((), (), s32[]{:S(2)}) async-start(), calls=%async_computation.4 | async-start | bytes 1474560 | tf_op jit(solution)/shard_map/reduce_scatter | solution.py:120
  277.6 26.8 %collective-permute-start.43 = (bf16[4,96,1536]{2,1,0:T(8,128)(2,1)}, bf16[4,96,1536]{2,1,0:T(8,128)(2,1)S(1)}, u32[]{:S(2)}, u32[]{:S(2)}) collective-permute-start(bf16[4,96,1536]{2,1,0:T(8,128)(2,1)} %get-tuple-element.173.refs_22_), channel_id=1, source_target_pairs={{0,4},{4,0},{8,12},{12,8},{16,20},{20,16},{24,28},{28,24},{1,5},{5... | collective-permute-start | bytes 3538952 | tf_op jit(solution)/shard_map/ppermute | solution.py:66
  307.6 16.6 %collective-permute-start.38 = (bf16[2,192,768]{2,1,0:T(8,128)(2,1)}, bf16[2,192,768]{2,1,0:T(8,128)(2,1)}, u32[]{:S(2)}, u32[]{:S(2)}) collective-permute-start(bf16[2,192,768]{2,1,0:T(8,128)(2,1)} %get-tuple-element.176), channel_id=1, source_target_pairs={{0,1},{1,0},{2,3},{3,2},{4,5},{5,4},{6,7},{7,6},{8,9},{9,8},{10,11... | collective-permute-start | bytes 1769480 | tf_op jit(solution)/shard_map/ppermute | solution.py:66
  307.6 4.2 %collective-permute-start.40 = (bf16[192,192]{1,0:T(8,128)(2,1)S(1)}, bf16[192,192]{1,0:T(8,128)(2,1)S(1)}, u32[]{:S(2)}, u32[]{:S(2)}) collective-permute-start(bf16[192,192]{1,0:T(8,128)(2,1)S(1)} %get-tuple-element.185), channel_id=1, source_target_pairs={{0,1},{1,0},{2,3},{3,2},{4,5},{5,4},{6,7},{7,6},{8,9},{9,8},{10,11... | collective-permute-start | bytes 221192 | tf_op jit(solution)/shard_map/ppermute | solution.py:66
  308.1 5.3 %collective-permute-start.41 = (bf16[192,192]{1,0:T(8,128)(2,1)S(1)}, bf16[192,192]{1,0:T(8,128)(2,1)S(1)}, u32[]{:S(2)}, u32[]{:S(2)}) collective-permute-start(bf16[192,192]{1,0:T(8,128)(2,1)S(1)} %get-tuple-element.186), channel_id=1, source_target_pairs={{0,2},{1,3},{2,0},{3,1},{4,6},{5,7},{6,4},{7,5},{8,10},{9,11},{10,... | collective-permute-start | bytes 221192 | tf_op jit(solution)/shard_map/ppermute | solution.py:66
  309.3 5.0 %collective-permute-start.42 = (bf16[192,192]{1,0:T(8,128)(2,1)S(1)}, bf16[192,192]{1,0:T(8,128)(2,1)S(1)}, u32[]{:S(2)}, u32[]{:S(2)}) collective-permute-start(bf16[192,192]{1,0:T(8,128)(2,1)S(1)} %get-tuple-element.187), channel_id=1, source_target_pairs={{0,3},{1,2},{2,1},{3,0},{4,7},{5,6},{6,5},{7,4},{8,11},{9,10},{10,... | collective-permute-start | bytes 221192 | tf_op jit(solution)/shard_map/ppermute | solution.py:66
  309.5 16.6 %collective-permute-start.45 = (bf16[2,192,768]{2,1,0:T(8,128)(2,1)}, bf16[2,192,768]{2,1,0:T(8,128)(2,1)}, u32[]{:S(2)}, u32[]{:S(2)}) collective-permute-start(bf16[2,192,768]{2,1,0:T(8,128)(2,1)} %get-tuple-element.193), channel_id=1, source_target_pairs={{0,1},{1,0},{2,3},{3,2},{4,5},{5,4},{6,7},{7,6},{8,9},{9,8},{10,11... | collective-permute-start | bytes 1769480 | tf_op jit(solution)/shard_map/ppermute | solution.py:66
  320.6 16.4 %collective-permute-start.44 = (bf16[4,96,768]{2,1,0:T(8,128)(2,1)}, bf16[4,96,768]{2,1,0:T(8,128)(2,1)S(1)}, u32[]{:S(2)}, u32[]{:S(2)}) collective-permute-start(bf16[4,96,768]{2,1,0:T(8,128)(2,1)} %get-tuple-element.190), channel_id=1, source_target_pairs={{0,4},{4,0},{8,12},{12,8},{16,20},{20,16},{24,28},{28,24},{1,5},{5... | collective-permute-start | bytes 1769480 | tf_op jit(solution)/shard_map/ppermute | solution.py:66
  325.2 18.4 %collective-permute-start.39 = (bf16[192,768]{1,0:T(8,128)(2,1)S(1)}, bf16[192,768]{1,0:T(8,128)(2,1)S(1)}, u32[]{:S(2)}, u32[]{:S(2)}) collective-permute-start(bf16[192,768]{1,0:T(8,128)(2,1)S(1)} %fusion.6), channel_id=1, source_target_pairs={{0,2},{1,3},{2,0},{3,1},{4,6},{5,7},{6,4},{7,5},{8,10},{9,11},{10,... | collective-permute-start | bytes 884744 | tf_op jit(solution)/shard_map/ppermute | solution.py:66
  327.1 17.3 %collective-permute-start.46 = (bf16[192,768]{1,0:T(8,128)(2,1)S(1)}, bf16[192,768]{1,0:T(8,128)(2,1)S(1)}, u32[]{:S(2)}, u32[]{:S(2)}) collective-permute-start(bf16[192,768]{1,0:T(8,128)(2,1)S(1)} %fusion.7), channel_id=1, source_target_pairs={{0,2},{1,3},{2,0},{3,1},{4,6},{5,7},{6,4},{7,5},{8,10},{9,11},{10,... | collective-permute-start | bytes 884744 | tf_op jit(solution)/shard_map/ppermute | solution.py:66
  338.2 17.0 %collective-permute-start.50 = (bf16[96,768]{1,0:T(8,128)(2,1)S(1)}, bf16[96,768]{1,0:T(8,128)(2,1)S(1)}, u32[]{:S(2)}, u32[]{:S(2)}) collective-permute-start(bf16[96,768]{1,0:T(8,128)(2,1)S(1)} %get-tuple-element.224.refs_1_), channel_id=1, source_target_pairs={{0,8},{4,12},{8,0},{12,4},{16,24},{20,28},{24,16},{28,20},{1,9},{5... | collective-permute-start | bytes 442376 | tf_op jit(solution)/shard_map/ppermute | solution.py:66
  338.3 16.9 %collective-permute-start.51 = (bf16[96,768]{1,0:T(8,128)(2,1)S(1)}, bf16[96,768]{1,0:T(8,128)(2,1)S(1)}, u32[]{:S(2)}, u32[]{:S(2)}) collective-permute-start(bf16[96,768]{1,0:T(8,128)(2,1)S(1)} %get-tuple-element.223), channel_id=1, source_target_pairs={{0,16},{4,20},{8,24},{12,28},{16,0},{20,4},{24,8},{28,12},{1,17},{... | collective-permute-start | bytes 442376 | tf_op jit(solution)/shard_map/ppermute | solution.py:66
  339.2 16.1 %collective-permute-start.52 = (bf16[96,768]{1,0:T(8,128)(2,1)S(1)}, bf16[96,768]{1,0:T(8,128)(2,1)S(1)}, u32[]{:S(2)}, u32[]{:S(2)}) collective-permute-start(bf16[96,768]{1,0:T(8,128)(2,1)S(1)} %get-tuple-element.222), channel_id=1, source_target_pairs={{0,24},{4,28},{8,16},{12,20},{16,8},{20,12},{24,0},{28,4},{1,25},{... | collective-permute-start | bytes 442376 | tf_op jit(solution)/shard_map/ppermute | solution.py:66
  343.7 5.3 %collective-permute-start.47 = (bf16[4,16,768]{2,1,0:T(8,128)(2,1)S(1)}, bf16[4,16,768]{2,1,0:T(8,128)(2,1)S(1)}, u32[]{:S(2)}, u32[]{:S(2)}) collective-permute-start(bf16[4,16,768]{2,1,0:T(8,128)(2,1)S(1)} %convert_element_type.252), channel_id=1, source_target_pairs={{0,1},{1,0},{2,3},{3,2},{4,5},{5,4},{6,7},{7,6},{8,9},{9,8},{10,11... | collective-permute-start | bytes 294920 | tf_op jit(solution)/shard_map/ppermute | solution.py:66
  349.0 4.7 %collective-permute-start.48 = (bf16[4,16,768]{2,1,0:T(8,128)(2,1)S(1)}, bf16[4,16,768]{2,1,0:T(8,128)(2,1)S(1)}, u32[]{:S(2)}, u32[]{:S(2)}) collective-permute-start(bf16[4,16,768]{2,1,0:T(8,128)(2,1)S(1)} %add_convert_fusion.13), channel_id=1, source_target_pairs={{0,2},{1,3},{2,0},{3,1},{4,6},{5,7},{6,4},{7,5},{8,10},{9,11},{10,... | collective-permute-start | bytes 294920 | tf_op jit(solution)/shard_map/ppermute | solution.py:66
  354.9 6.0 %collective-permute-start.49 = (bf16[4,16,768]{2,1,0:T(8,128)(2,1)S(1)}, bf16[4,16,768]{2,1,0:T(8,128)(2,1)}, u32[]{:S(2)}, u32[]{:S(2)}) collective-permute-start(bf16[4,16,768]{2,1,0:T(8,128)(2,1)S(1)} %convert_element_type.258), channel_id=1, source_target_pairs={{0,4},{4,0},{8,12},{12,8},{16,20},{20,16},{24,28},{28,24},{1,5},{5... | collective-permute-start | bytes 294920 | tf_op jit(solution)/shard_map/ppermute | solution.py:66
  356.4 3.8 collective-permute-start.54
  361.8 8.4 %collective-permute-start.55 = (bf16[4,16,768]{2,1,0:T(8,128)(2,1)S(1)}, bf16[4,16,768]{2,1,0:T(8,128)(2,1)}, u32[]{:S(2)}, u32[]{:S(2)}) collective-permute-start(bf16[4,16,768]{2,1,0:T(8,128)(2,1)S(1)} %add_convert_fusion.12), channel_id=1, source_target_pairs={{0,8},{4,12},{8,0},{12,4},{16,24},{20,28},{24,16},{28,20},{1,9},{5... | collective-permute-start | bytes 294920 | tf_op jit(solution)/shard_map/ppermute | solution.py:66
  362.6 7.0 %collective-permute-start.57 = (f32[2,24,128]{2,1,0:T(8,128)S(1)}, f32[2,24,128]{2,1,0:T(8,128)S(1)}, u32[]{:S(2)}, u32[]{:S(2)}) collective-permute-start(f32[2,24,128]{2,1,0:T(8,128)S(1)} %add.265), channel_id=1, source_target_pairs={{0,8},{4,12},{8,0},{12,4},{16,24},{20,28},{24,16},{28,20},{1,9},{5... | collective-permute-start | bytes 73736 | tf_op jit(solution)/shard_map/ppermute | solution.py:66
  365.4 3.7 collective-permute-start.56
  371.2 7.3 %collective-permute-start.58 = (bf16[4,16,768]{2,1,0:T(8,128)(2,1)S(1)}, bf16[4,16,768]{2,1,0:T(8,128)(2,1)S(1)}, u32[]{:S(2)}, u32[]{:S(2)}) collective-permute-start(bf16[4,16,768]{2,1,0:T(8,128)(2,1)S(1)} %add_convert_fusion.11), channel_id=1, source_target_pairs={{0,16},{4,20},{8,24},{12,28},{16,0},{20,4},{24,8},{28,12},{1,17},{... | collective-permute-start | bytes 294920 | tf_op jit(solution)/shard_map/ppermute | solution.py:66
  372.0 5.9 %collective-permute-start.59 = (f32[2,24,128]{2,1,0:T(8,128)S(1)}, f32[2,24,128]{2,1,0:T(8,128)S(1)}, u32[]{:S(2)}, u32[]{:S(2)}) collective-permute-start(f32[2,24,128]{2,1,0:T(8,128)S(1)} %add.267), channel_id=1, source_target_pairs={{0,16},{4,20},{8,24},{12,28},{16,0},{20,4},{24,8},{28,12},{1,17},{... | collective-permute-start | bytes 73736 | tf_op jit(solution)/shard_map/ppermute | solution.py:66
  383.9 3.6 collective-permute-start.61
  387.6 4.0 collective-permute-start.62
  391.5 3.7 collective-permute-start.63
  395.2 4.5 %collective-permute-start.64 = (f32[8,128]{1,0:T(8,128)S(1)}, f32[8,128]{1,0:T(8,128)S(1)}, u32[]{:S(2)}, u32[]{:S(2)}) collective-permute-start(f32[8,128]{1,0:T(8,128)S(1)} %add.274), channel_id=1, source_target_pairs={{0,16},{4,20},{8,24},{12,28},{16,0},{20,4},{24,8},{28,12},{1,17},{... | collective-permute-start | bytes 12296 | tf_op jit(solution)/shard_map/ppermute | solution.py:66
  (72 other events, 474.5 us)
Sparse Core Ops, SparseCore 0:
  40.6 68.2 all-gather.1
  233.4 26.2 reduce-scatter.5
  262.6 20.7 reduce-scatter.7
  307.1 26.0 reduce-scatter.3
